TPU v7x, 32 devices: a whole 2x2x4 slice. The times are simulated.
32 devices in a mesh: expert: 8 (over y, x, core), ffn: 4 (over z).
Axes of the slice: x: 2, y: 2, z: 4, core: 2. Of those that a mesh axis runs over, the one named last changes fastest.
Arguments:
- tokens: bfloat16 [512, 4096], P('expert', 'ffn'), may hold values from -6 to 6
- cotangent: bfloat16 [512, 4096], P('expert', 'ffn'), may hold values from -6 to 6
- route_ids: int32 [512, 4], P('expert'), may hold values from 0 to 7, all different within a row; in each aligned block of 64 rows (0 to 63, 64 to 127, ...) at most 48 rows name the same one
- route_weights: bfloat16 [512, 4], P('expert'), may hold values from 0.019897461 to 0.5
- gate_weight: bfloat16 [8, 4096, 1024], P('expert', None, 'ffn'), may hold values from -0.09375 to 0.09375
- up_weight: bfloat16 [8, 4096, 1024], P('expert', None, 'ffn'), may hold values from -0.09375 to 0.09375
- down_weight: bfloat16 [8, 1024, 4096], P('expert', 'ffn'), may hold values from -0.1875 to 0.1875
- fisher: float32 [8, 1024, 4096], P('expert', 'ffn'), may hold values from 20 to 400
- anchor: float32 [8, 1024, 4096], P('expert', 'ffn'), may hold values from -0.18 to 0.18
Outputs:
- grad_tokens: bfloat16 [512, 4096], P('expert', 'ffn')
- grad_route_weights: float32 [512, 4], P('expert')
- grad_gate: bfloat16 [8, 4096, 1024], P('expert', None, 'ffn')
- grad_up: bfloat16 [8, 4096, 1024], P('expert', None, 'ffn')
- grad_down: bfloat16 [8, 1024, 4096], P('expert', 'ffn')
Inputs may be any that keep to these rules, and one draw needn't show every extreme that they name: `route_ids`: each row names 4 different experts. Among the 64 rows of one index of expert, no expert is named more than 48 times, a bound that some block reaches.
All inputs are finite; a program needn't handle non-finite values.
Results may differ from a plain program's by a relative error of at most 0.005.
Values may be sent and summed in bfloat16 or wider, within the bound.
No kernel may reach another device: no remote copies, remote signals or barrier semaphores. Data moves between devices by JAX's collectives and lax.ppermute only.
A program may use at most 128 MiB of HBM per device.

v0:
```python
import jax
import jax.numpy as jnp
from jax import lax
from jax.sharding import PartitionSpec as P


def slot_layout(route_ids, capacity, expert_count):
    flat_ids = route_ids.reshape(-1)
    onehot = (flat_ids[:, None] == jnp.arange(expert_count, dtype=jnp.int32)[None, :]).astype(
        jnp.int32
    )
    earlier = jnp.cumsum(onehot, axis=0) - onehot
    position = jnp.sum(earlier * onehot, axis=1)
    return flat_ids * capacity + position


def expert_pass(rows_x, rows_dy, rows_w, gate_part, up_part, down_part, fisher_part, anchor_part):
    gate_pre = jnp.dot(rows_x, gate_part, preferred_element_type=jnp.float32)
    up_pre = jnp.dot(rows_x, up_part, preferred_element_type=jnp.float32)
    logistic = jax.nn.sigmoid(gate_pre)
    active = gate_pre * logistic
    hidden = active * up_pre
    back = lax.dot_general(
        rows_dy, down_part, (((1,), (1,)), ((), ())), preferred_element_type=jnp.float32
    )
    route_part = jnp.sum(back * hidden, axis=1)
    weight_col = rows_w.astype(jnp.float32)[:, None]
    scaled = weight_col * back
    grad_pre_gate = (scaled * up_pre * logistic * (1.0 + gate_pre * (1.0 - logistic))).astype(
        jnp.bfloat16
    )
    grad_pre_up = (scaled * active).astype(jnp.bfloat16)
    weighted = (weight_col * hidden).astype(jnp.bfloat16)
    over_rows = (((0,), (0,)), ((), ()))
    grad_gate = lax.dot_general(
        rows_x, grad_pre_gate, over_rows, preferred_element_type=jnp.float32
    ).astype(jnp.bfloat16)
    grad_up = lax.dot_general(
        rows_x, grad_pre_up, over_rows, preferred_element_type=jnp.float32
    ).astype(jnp.bfloat16)
    down_data = lax.dot_general(weighted, rows_dy, over_rows, preferred_element_type=jnp.float32)
    grad_down = (down_data + fisher_part * (down_part.astype(jnp.float32) - anchor_part)).astype(
        jnp.bfloat16
    )
    return (route_part, grad_pre_gate, grad_pre_up, grad_gate, grad_up, grad_down)


def unit_product(grad_pre_gate, grad_pre_up, gate_part, up_part):
    over_units = (((1,), (1,)), ((), ()))
    feature_part = lax.dot_general(
        grad_pre_gate, gate_part, over_units, preferred_element_type=jnp.float32
    )
    return feature_part + lax.dot_general(
        grad_pre_up, up_part, over_units, preferred_element_type=jnp.float32
    )


def per_device(
    tokens, cotangent, route_ids, route_weights, gate_weight, up_weight, down_weight, fisher, anchor
):
    expert_count = lax.axis_size("expert")
    token_count = route_ids.shape[0]
    route_count = route_ids.shape[1]
    capacity = 3 * token_count * route_count // (2 * expert_count)
    total_slots = expert_count * capacity
    slots = slot_layout(route_ids, capacity, expert_count)
    owner = jnp.arange(token_count * route_count, dtype=jnp.int32) // route_count
    slot_token = jnp.zeros((total_slots,), jnp.int32).at[slots].set(owner)
    slot_weight = jnp.zeros((total_slots,), jnp.bfloat16).at[slots].set(route_weights.reshape(-1))
    slot_weight = slot_weight.reshape(expert_count, capacity)
    whole_x, whole_dy = (
        lax.all_gather(tokens, "ffn", axis=1, tiled=True),
        lax.all_gather(cotangent, "ffn", axis=1, tiled=True),
    )
    sent_x = whole_x[slot_token].reshape(expert_count, capacity, -1)
    sent_dy = whole_dy[slot_token].reshape(expert_count, capacity, -1)
    rows_x, rows_dy, rows_w = (
        lax.all_to_all(sent_x, "expert", split_axis=0, concat_axis=0, tiled=True),
        lax.all_to_all(sent_dy, "expert", split_axis=0, concat_axis=0, tiled=True),
        lax.all_to_all(slot_weight, "expert", split_axis=0, concat_axis=0, tiled=True),
    )
    width = rows_x.shape[2]
    route_part, grad_pre_gate, grad_pre_up, grad_gate, grad_up, grad_down = expert_pass(
        rows_x.reshape(total_slots, width),
        rows_dy.reshape(total_slots, width),
        rows_w.reshape(-1),
        gate_weight[0],
        up_weight[0],
        down_weight[0],
        fisher[0],
        anchor[0],
    )
    route_total = lax.psum(route_part, "ffn").reshape(expert_count, capacity)
    feature_part = unit_product(grad_pre_gate, grad_pre_up, gate_weight[0], up_weight[0])
    feature_part = feature_part.reshape(expert_count, capacity, width)
    feature_share = lax.psum_scatter(feature_part, "ffn", scatter_dimension=2, tiled=True)
    home_rows, home_route = (
        lax.all_to_all(feature_share, "expert", split_axis=0, concat_axis=0, tiled=True),
        lax.all_to_all(route_total, "expert", split_axis=0, concat_axis=0, tiled=True),
    )
    picked_rows = home_rows.reshape(total_slots, -1)[slots]
    grad_tokens = jnp.sum(picked_rows.reshape(token_count, route_count, -1), axis=1)
    grad_route_weights = home_route.reshape(-1)[slots].reshape(token_count, route_count)
    return (
        grad_tokens.astype(jnp.bfloat16),
        grad_route_weights,
        grad_gate[None],
        grad_up[None],
        grad_down[None],
    )


def solution(mesh):
    return jax.shard_map(
        per_device,
        mesh=mesh,
        in_specs=(
            P("expert", "ffn"),
            P("expert", "ffn"),
            P("expert", None),
            P("expert", None),
            P("expert", None, "ffn"),
            P("expert", None, "ffn"),
            P("expert", "ffn", None),
            P("expert", "ffn", None),
            P("expert", "ffn", None),
        ),
        out_specs=(
            P("expert", "ffn"),
            P("expert", None),
            P("expert", None, "ffn"),
            P("expert", None, "ffn"),
            P("expert", "ffn", None),
        ),
        check_vma=False,
    )
```

profile of v0, /device:TPU:0, one launch (start us, length us, event | category | flops | bytes accessed | tf_op | source)
XLA Modules:
  0.0 284.6 jit_solution(13350797669737464404)
XLA Ops:
  7.2 0.8 broadcast_multiply_fusion
  8.0 0.8 copy.20
  8.8 0.1 eq.29
  8.9 0.1 eq.25
  9.0 0.8 copy.22
  9.8 0.1 reshape.152
  9.9 0.1 copy.19
  10.0 0.1 mul.62
  10.1 0.6 reduce-window.6
  10.7 0.2 slice_reduce_fusion
  11.0 0.1 fusion.18
  11.1 2.2 scatter_custom_fusion
  13.2 0.7 all_to_all.28
  13.9 5.2 %all-to-all-start = ((bf16[8,1,48]{2,1,0:T(2,128)(2,1)}), bf16[8,1,48]{2,1,0:T(2,128)(2,1)S(1)}, u32[]{:S(2)}, u32[]{:S(2)}) async-start(bf16[8,1,48]{2,1,0:T(2,128)(2,1)} %all_to_all.28), calls=%async_computation | async-start | bytes 8192 | tf_op jit(solution)/shard_map/all_to_all | solution.py:80
  19.1 1.4 scatter_custom_fusion.1
  20.5 16.8 %all_gather.7 = bf16[64,4096]{1,0:T(8,128)(2,1)S(1)} all-gather(bf16[64,1024]{1,0:T(8,128)(2,1)} %param.9), channel_id=1, replica_groups=mesh['expert'=8,'ffn'=4] {'ffn'}, dimensions={1}, use_global_device_ids=true | all-gather | bytes 655360 | tf_op jit(solution)/shard_map/all_gather | solution.py:72
  37.3 4.0 %gather_fusion.1 = bf16[384,4096]{1,0:T(8,128)(2,1)} fusion(bf16[64,4096]{1,0:T(8,128)(2,1)S(1)} %all_gather.7, s32[1024]{0:T(1024)S(1)} %pad_clamp_fusion.1), kind=kCustom, calls=%fused_computation.1 | custom fusion | bytes 6292992 | tf_op jit(solution)/shard_map/gather | solution.py:75
  41.3 4.6 %all-to-all-start.2 = ((bf16[8,48,4096]{2,1,0:T(8,128)(2,1)}), bf16[8,48,4096]{2,1,0:T(8,128)(2,1)}, u32[]{:S(2)}, u32[]{:S(2)}) async-start(bf16[8,48,4096]{2,1,0:T(8,128)(2,1)} %bitcast.60), calls=%async_computation.2 | async-start | bytes 6291456 | tf_op jit(solution)/shard_map/all_to_all | solution.py:78
  46.0 16.2 %all_gather.6 = bf16[64,4096]{1,0:T(8,128)(2,1)S(1)} all-gather(bf16[64,1024]{1,0:T(8,128)(2,1)S(1)} %copy-done.6), channel_id=1, replica_groups=mesh['expert'=8,'ffn'=4] {'ffn'}, dimensions={1}, use_global_device_ids=true | all-gather | bytes 655360 | tf_op jit(solution)/shard_map/all_gather | solution.py:73
  62.1 4.1 %gather_fusion = bf16[384,4096]{1,0:T(8,128)(2,1)} fusion(bf16[64,4096]{1,0:T(8,128)(2,1)S(1)} %all_gather.6, s32[1024]{0:T(1024)S(1)} %pad_clamp_fusion.1), kind=kCustom, calls=%fused_computation | custom fusion | bytes 6292992 | tf_op jit(solution)/shard_map/gather | solution.py:76
  66.2 17.6 %all-to-all-done.2 = bf16[8,48,4096]{2,1,0:T(8,128)(2,1)} async-done(((bf16[8,48,4096]{2,1,0:T(8,128)(2,1)}), bf16[8,48,4096]{2,1,0:T(8,128)(2,1)}, u32[]{:S(2)}, u32[]{:S(2)}) %all-to-all-start.2) | async-done | bytes 3145760 | tf_op jit(solution)/shard_map/all_to_all | solution.py:78
  83.8 4.4 %all-to-all-start.1 = ((bf16[8,48,4096]{2,1,0:T(8,128)(2,1)}), bf16[8,48,4096]{2,1,0:T(8,128)(2,1)}, u32[]{:S(2)}, u32[]{:S(2)}) async-start(bf16[8,48,4096]{2,1,0:T(8,128)(2,1)} %bitcast.59), calls=%async_computation.1 | async-start | bytes 6291456 | tf_op jit(solution)/shard_map/all_to_all | solution.py:79
  88.3 0.2 reduce-scatter.2.cloned.1.call-start
  88.5 0.1 reshape.115
  88.6 3.3 %fusion.7 = f32[384,256]{0,1:T(8,128)S(1)} fusion(bf16[384,4096]{1,0:T(8,128)(2,1)} %bitcast.8, bf16[1,4096,256]{2,1,0:T(8,128)(2,1)S(1)} %copy-done), kind=kOutput, calls=%fused_computation.18 | convolution fusion | flops 805306368 | bytes 5636096 | tf_op jit(solution)/shard_map/dot_general | solution.py:18
  92.0 3.2 %fusion.10 = f32[384,256]{0,1:T(8,128)S(1)} fusion(bf16[384,4096]{1,0:T(8,128)(2,1)} %bitcast.8, bf16[1,4096,256]{2,1,0:T(8,128)(2,1)S(1)} %copy-done.3), kind=kOutput, calls=%fused_computation.21 | convolution fusion | flops 805306368 | bytes 5636096 | tf_op jit(solution)/shard_map/dot_general | solution.py:19
  95.2 31.0 %all-to-all-done.1 = bf16[8,48,4096]{2,1,0:T(8,128)(2,1)} async-done(((bf16[8,48,4096]{2,1,0:T(8,128)(2,1)}), bf16[8,48,4096]{2,1,0:T(8,128)(2,1)}, u32[]{:S(2)}, u32[]{:S(2)}) %all-to-all-start.1) | async-done | bytes 3145760 | tf_op jit(solution)/shard_map/all_to_all | solution.py:79
  126.2 3.9 %multiply_reduce_fusion = (f32[384]{0:T(512)S(1)}, bf16[384,256]{0,1:T(8,128)(2,1)S(1)}, bf16[384,256]{0,1:T(8,128)(2,1)S(1)}) fusion(f32[384,256]{0,1:T(8,128)S(1)} %fusion.10, f32[384,256]{0,1:T(8,128)S(1)} %fusion.7, f32[384]{0:T(512)S(1)} %reshape.115, bf16[384,4096]{1,0:T(8,128)(2,1)} %bitcast.5, bf16[1,256,4096]{2,1,0:T(8,128)(2,1)} %param.15), kind=kOutput, calls=%fused_computation.26 | convolution fusion | flops 806977152 | bytes 6425600 | tf_op jit(solution)/shard_map/dot_general | solution.py:23
  130.1 1.0 fusion.5
  131.1 0.5 copy-done.4
  131.7 3.7 %convolution_add_fusion = f32[384,4096]{1,0:T(8,128)} fusion(f32[384,4096]{1,0:T(8,128)S(1)} %fusion.5, bf16[384,256]{0,1:T(8,128)(2,1)S(1)} %get-tuple-element.17, bf16[1,4096,256]{2,1,0:T(8,128)(2,1)S(1)} %copy-done.4), kind=kOutput, calls=%fused_computation.6 | convolution fusion | flops 806879232 | bytes 14876672 | tf_op jit(solution)/shard_map/dot_general | solution.py:53
  135.4 0.1 all_to_all.26
  135.5 12.0 %psum.7 = f32[8,1,48]{2,1,0:T(1,128)S(1)} all-reduce(f32[8,1,48]{2,1,0:T(1,128)S(1)} %all_to_all.26), channel_id=1, replica_groups=mesh['expert'=8,'ffn'=4] {'ffn'}, use_global_device_ids=true, to_apply=%region_8.9 | all-reduce | flops 384 | bytes 3072 | tf_op jit(solution)/shard_map/psum | solution.py:93
  147.6 7.0 %all_to_all.34 = f32[8,1,48]{2,1,0:T(1,128)S(1)} all-to-all(f32[8,1,48]{2,1,0:T(1,128)S(1)} %psum.7), channel_id=1, replica_groups=mesh['expert'=8,'ffn'=4] {'expert'}, dimensions={0} | all-to-all | bytes 3072 | tf_op jit(solution)/shard_map/all_to_all | solution.py:99
  154.6 91.0 %reduce-scatter.2.cloned.1.call-done = f32[8,48,1024]{2,1,0:T(8,128)} async-done(((f32[8,48,4096]{2,1,0:T(8,128)}), f32[8,48,1024]{2,1,0:T(8,128)}) %reduce-scatter.2.cloned.1.call-update) | async-done | bytes 1572880 | tf_op jit(solution)/shard_map/reduce_scatter | solution.py:96
  245.6 4.5 %all-to-all-start.3 = ((f32[8,48,1024]{2,1,0:T(8,128)}), f32[8,48,1024]{2,1,0:T(8,128)}, u32[]{:S(2)}, u32[]{:S(2)}) async-start(f32[8,48,1024]{2,1,0:T(8,128)} %reduce-scatter.2.cloned.1.call-done), calls=%async_computation.4 | async-start | bytes 3145728 | tf_op jit(solution)/shard_map/all_to_all | solution.py:98
  250.1 4.7 %fusion.1 = bf16[1,4096,256]{2,1,0:T(8,128)(2,1)} fusion(bf16[384,4096]{1,0:T(8,128)(2,1)} %bitcast.8, bf16[384,256]{0,1:T(8,128)(2,1)S(1)} %get-tuple-element.16), kind=kOutput, calls=%fused_computation.11 | convolution fusion | flops 806354944 | bytes 5439488 | tf_op jit(solution)/shard_map/dot_general | solution.py:35
  254.8 4.7 %fusion.2 = bf16[1,4096,256]{2,1,0:T(8,128)(2,1)} fusion(bf16[384,4096]{1,0:T(8,128)(2,1)} %bitcast.8, bf16[384,256]{0,1:T(8,128)(2,1)S(1)} %get-tuple-element.17), kind=kOutput, calls=%fused_computation.12 | convolution fusion | flops 806354944 | bytes 5439488 | tf_op jit(solution)/shard_map/dot_general | solution.py:38
  259.5 4.8 %fusion.3 = bf16[1,256,4096]{2,1,0:T(8,128)(2,1)} fusion(bf16[384,4096]{1,0:T(8,128)(2,1)} %bitcast.5, f32[1,256,4096]{2,1,0:T(8,128)S(1)} %copy-done.1, f32[1,256,4096]{2,1,0:T(8,128)S(1)} %copy-done.2, bf16[1,256,4096]{2,1,0:T(8,128)(2,1)S(1)} %copy-done.5, f32[384]{0:T(512)S(1)} %reshape.115, f32[384,256]{0,1:T(8,128)S(1)} %fusion.10, ...), kind=kOutput, calls=%fused_computation.13 | convolution fusion | flops 811237376 | bytes 16516608 | tf_op jit(solution)/shard_map/dot_general | solution.py:41
  264.3 0.5 broadcast.106
  264.8 0.7 reduce.9
  265.5 1.9 gather_fusion.3
  267.5 0.1 reshape.114
  267.6 0.7 copy.24
  268.2 2.7 all-to-all-done.3
  270.9 3.0 %gather_fusion.2 = f32[256,1024]{1,0:T(8,128)S(1)} fusion(f32[384,1024]{1,0:T(8,128)} %bitcast.12, s32[1024]{0:T(1024)S(1)} %pad_clamp_fusion), kind=kCustom, calls=%fused_computation.2 | custom fusion | bytes 2098176 | tf_op jit(solution)/shard_map/gather | solution.py:101
  273.9 1.3 reshape.112
  275.2 2.5 reduce_sum.31
  (25 shorter events, 0.2 us)
Async XLA Ops:
  7.2 81.5 %copy-start = (bf16[1,4096,256]{2,1,0:T(8,128)(2,1)S(1)}, bf16[1,4096,256]{2,1,0:T(8,128)(2,1)}, u32[]{:S(2)}) copy-start(bf16[1,4096,256]{2,1,0:T(8,128)(2,1)} %param.13) | copy-start | bytes 6291460
  13.9 27.4 %all-to-all-start = ((bf16[8,1,48]{2,1,0:T(2,128)(2,1)}), bf16[8,1,48]{2,1,0:T(2,128)(2,1)S(1)}, u32[]{:S(2)}, u32[]{:S(2)}) async-start(bf16[8,1,48]{2,1,0:T(2,128)(2,1)} %all_to_all.28), calls=%async_computation | async-start | bytes 8192 | tf_op jit(solution)/shard_map/all_to_all | solution.py:80
  41.3 4.6 %copy-start.6 = (bf16[64,1024]{1,0:T(8,128)(2,1)S(1)}, bf16[64,1024]{1,0:T(8,128)(2,1)}, u32[]{:S(2)}) copy-start(bf16[64,1024]{1,0:T(8,128)(2,1)} %param.10) | copy-start | bytes 393220
  41.3 42.5 %all-to-all-start.2 = ((bf16[8,48,4096]{2,1,0:T(8,128)(2,1)}), bf16[8,48,4096]{2,1,0:T(8,128)(2,1)}, u32[]{:S(2)}, u32[]{:S(2)}) async-start(bf16[8,48,4096]{2,1,0:T(8,128)(2,1)} %bitcast.60), calls=%async_computation.2 | async-start | bytes 6291456 | tf_op jit(solution)/shard_map/all_to_all | solution.py:78
  83.8 42.3 %all-to-all-start.1 = ((bf16[8,48,4096]{2,1,0:T(8,128)(2,1)}), bf16[8,48,4096]{2,1,0:T(8,128)(2,1)}, u32[]{:S(2)}, u32[]{:S(2)}) async-start(bf16[8,48,4096]{2,1,0:T(8,128)(2,1)} %bitcast.59), calls=%async_computation.1 | async-start | bytes 6291456 | tf_op jit(solution)/shard_map/all_to_all | solution.py:79
  88.3 157.3 %reduce-scatter.2.cloned.1.call-start = ((), (), s32[]{:S(2)}) async-start(), calls=%async_computation.6 | async-start | bytes 7864320 | tf_op jit(solution)/shard_map/reduce_scatter | solution.py:96
  88.6 3.3 %copy-start.3 = (bf16[1,4096,256]{2,1,0:T(8,128)(2,1)S(1)}, bf16[1,4096,256]{2,1,0:T(8,128)(2,1)}, u32[]{:S(2)}) copy-start(bf16[1,4096,256]{2,1,0:T(8,128)(2,1)} %param.14) | copy-start | bytes 6291460
  130.1 1.6 copy-start.4
  245.6 25.3 %all-to-all-start.3 = ((f32[8,48,1024]{2,1,0:T(8,128)}), f32[8,48,1024]{2,1,0:T(8,128)}, u32[]{:S(2)}, u32[]{:S(2)}) async-start(f32[8,48,1024]{2,1,0:T(8,128)} %reduce-scatter.2.cloned.1.call-done), calls=%async_computation.4 | async-start | bytes 3145728 | tf_op jit(solution)/shard_map/all_to_all | solution.py:98
  250.1 9.3 %copy-start.2 = (f32[1,256,4096]{2,1,0:T(8,128)S(1)}, f32[1,256,4096]{2,1,0:T(8,128)}, u32[]{:S(2)}) copy-start(f32[1,256,4096]{2,1,0:T(8,128)} %param.16) | copy-start | bytes 12582916
  254.8 4.7 %copy-start.1 = (f32[1,256,4096]{2,1,0:T(8,128)S(1)}, f32[1,256,4096]{2,1,0:T(8,128)}, u32[]{:S(2)}) copy-start(f32[1,256,4096]{2,1,0:T(8,128)} %param.17) | copy-start | bytes 12582916
  254.8 4.7 %copy-start.5 = (bf16[1,256,4096]{2,1,0:T(8,128)(2,1)S(1)}, bf16[1,256,4096]{2,1,0:T(8,128)(2,1)}, u32[]{:S(2)}) copy-start(bf16[1,256,4096]{2,1,0:T(8,128)(2,1)} %param.15) | copy-start | bytes 6291460
Sparse Core Ops, SparseCore 0:
  135.6 109.9 reduce-scatter.1
where the time goes:
time: 285 us
  waiting for transfers between devices  142 us (50%)
  blocking collectives  52 us (18%)
  matrix products  29.3 us (10%)
  local copies, waits for them, and re-layouts  23 us (8%)
  starting transfers between devices  18.9 us (7%)
  between operations  14.2 us (5%)
  other arithmetic  4.79 us (2%)
    reduce_scatter x1, waiting for transfers between devices, per_device(): lax.psum_scatter(feature_part, 'ffn', scatter_dimension=2, tiled=True)  91 us
    all_to_all x1, waiting for transfers between devices, per_device(): lax.all_to_all(sent_dy, 'expert', split_axis=0, concat_axis=0, tiled=True)  31 us
    all_to_all x1, waiting for transfers between devices, per_device(): lax.all_to_all(sent_x, 'expert', split_axis=0, concat_axis=0, tiled=True)  17.6 us
    all_gather x1, blocking collectives, per_device(): lax.all_gather(tokens, 'ffn', axis=1, tiled=True)  16.8 us
    all_gather x1, blocking collectives, per_device(): lax.all_gather(cotangent, 'ffn', axis=1, tiled=True)  16.2 us
    psum x1, blocking collectives, per_device(): route_total = lax.psum(route_part, 'ffn').reshape(expert_count, capacity)  12 us
    all_to_all x1, blocking collectives, per_device(): lax.all_to_all(route_total, 'expert', split_axis=0, concat_axis=0, tiled=...  7.01 us
  transfers between devices with their start and end apart: 5, of which 4 were waited for; matrix products, arithmetic and copies ran while one was open for 12% of the time, Pallas kernels for 0%

commit v1 on v0

v1 whole, which is shorter than its diff:
```python
import functools

import jax
import jax.numpy as jnp
from jax import lax
from jax.experimental import pallas as pl
from jax.experimental.pallas import tpu as pltpu
from jax.sharding import PartitionSpec as P

BF = jnp.bfloat16
F32 = jnp.float32
LANES = 128
VMEM_LIMIT = 56 * 1024 * 1024


def whole_block(shape):
    zeros = (0,) * len(shape)
    return pl.BlockSpec(shape, lambda *_: zeros, pipeline_mode=pl.Buffered(1))


def dot(a, b, a_dim, b_dim):
    return lax.dot_general(a, b, (((a_dim,), (b_dim,)), ((), ())), preferred_element_type=F32)


def split_pair(value):
    high = lax.reduce_precision(value, 8, 7)
    return jnp.concatenate([high, value - high], axis=-1).astype(BF)


def join_pair(pair, count):
    pair = pair.astype(F32)
    return pair[..., :count] + pair[..., count : 2 * count]


def forward_kernel(n_slice, n_expert, place, *refs):
    xs, dys = refs[:n_slice], refs[n_slice : 2 * n_slice]
    route_w, gate_a, up_a, down_a, gate_b, up_b, down_b = refs[2 * n_slice : 2 * n_slice + 7]
    grad_pre, weighted, route, acc = refs[2 * n_slice + 7 :]
    step = pl.program_id(0)
    units = gate_a.shape[1]

    for at in range(n_slice):

        @pl.when(step == at)
        def _(at=at):
            x, dy = xs[at][...], dys[at][...]
            for number, (source, weight, dim) in enumerate(
                (
                    (x, gate_a, 0),
                    (x, up_a, 0),
                    (dy, down_a, 1),
                    (x, gate_b, 0),
                    (x, up_b, 0),
                    (dy, down_b, 1),
                )
            ):
                part = dot(source, weight[...], 1, dim)
                if at == 0:
                    acc[number] = part
                else:
                    acc[number] += part

    @pl.when(step == n_slice - 1)
    def _():
        lane = lax.broadcasted_iota(jnp.int32, (route_w.shape[0], LANES), 1)
        own = place[1]
        total = jnp.zeros((route_w.shape[0], LANES), F32)
        for j in range(2):
            expert = jnp.bitwise_xor(own, j)
            gate_pre, up_pre, back = acc[3 * j], acc[3 * j + 1], acc[3 * j + 2]
            weight = jnp.sum(
                jnp.where(lane == expert, route_w[...].astype(F32), 0.0), axis=1, keepdims=True
            )
            logistic = jax.nn.sigmoid(gate_pre)
            active = gate_pre * logistic
            hidden = active * up_pre
            route_part = jnp.sum(back * hidden, axis=1, keepdims=True)
            high = route_part.astype(BF).astype(F32)
            total = total + jnp.where(lane == expert, high, 0.0)
            total = total + jnp.where(lane == expert + n_expert, route_part - high, 0.0)
            scaled = weight * back
            grad_pre[:, 2 * j * units : (2 * j + 1) * units] = (
                scaled * up_pre * logistic * (1.0 + gate_pre * (1.0 - logistic))
            ).astype(BF)
            grad_pre[:, (2 * j + 1) * units : (2 * j + 2) * units] = (scaled * active).astype(BF)
            weighted[:, j * units : (j + 1) * units] = (weight * hidden).astype(BF)
        route[...] = total.astype(BF)


def forward_values(place, xs, dys, route_w, mine, other, n_expert):
    n_slice = len(xs)
    rows, width = xs[0].shape
    units = mine[0].shape[1]
    wide = pl.BlockSpec((width, units), lambda s, p: (p[0] ^ s, 0))
    tall = pl.BlockSpec((units, width), lambda s, p: (0, p[0] ^ s))
    return pl.pallas_call(
        functools.partial(forward_kernel, n_slice, n_expert),
        grid_spec=pltpu.PrefetchScalarGridSpec(
            num_scalar_prefetch=1,
            grid=(n_slice,),
            in_specs=[whole_block((rows, width))] * (2 * n_slice)
            + [whole_block((rows, LANES))]
            + [wide, wide, tall] * 2,
            out_specs=[
                whole_block((rows, 4 * units)),
                whole_block((rows, 2 * units)),
                whole_block((rows, LANES)),
            ],
            scratch_shapes=[pltpu.VMEM((6, rows, units), F32)],
        ),
        out_shape=[
            jax.ShapeDtypeStruct((rows, 4 * units), BF),
            jax.ShapeDtypeStruct((rows, 2 * units), BF),
            jax.ShapeDtypeStruct((rows, LANES), BF),
        ],
        compiler_params=pltpu.CompilerParams(vmem_limit_bytes=VMEM_LIMIT),
        cost_estimate=pl.CostEstimate(
            flops=12 * rows * width * n_slice * units,
            bytes_accessed=2 * n_slice * width * (2 * rows + 6 * units),
            transcendentals=2 * rows * units,
        ),
        name="forward_values",
    )(place, *xs, *dys, route_w, *mine, *other)


def unit_kernel(lo, hi, tokens, with_route, place, grad_pre, *refs):
    if with_route:
        route, refs = refs[0], refs[1:]
    weights, outs = refs[:4], refs[4:]
    units = weights[0].shape[1]
    half = weights[0].shape[0] // 2
    grads = grad_pre[...]
    total = None
    for number, weight in enumerate(weights):
        part = dot(grads[:, number * units : (number + 1) * units], weight[...], 1, 1)
        total = part if total is None else total + part
    for m in range(lo):
        for h in range(hi):
            at = (h * lo + m) * tokens
            outs[m][h, :, :half] = total[at : at + tokens, :half].astype(outs[m].dtype)
            if with_route:
                outs[m][h, :, half:] = route[at : at + tokens, :].astype(outs[m].dtype)
    for h in range(hi):
        for m in range(lo):
            at = (h * lo + m) * tokens
            outs[lo + h][m] = total[at : at + tokens, half:].astype(outs[lo + h].dtype)


def unit_product(place, grad_pre, weights, slot, lo, hi, tokens, width, route=None):
    rows = grad_pre.shape[0]
    units = weights[0].shape[1]
    half = width // 2
    first = half + (LANES if route is not None else 0)
    wide = pl.BlockSpec((width, units), lambda i, p: (p[0] ^ slot, 0))
    shapes = [
        jax.ShapeDtypeStruct((hi, tokens, first), F32 if m == 0 else BF) for m in range(lo)
    ] + [jax.ShapeDtypeStruct((lo, tokens, half), F32 if h == 0 else BF) for h in range(hi)]
    extra = [] if route is None else [route]
    outs = pl.pallas_call(
        functools.partial(unit_kernel, lo, hi, tokens, route is not None),
        grid_spec=pltpu.PrefetchScalarGridSpec(
            num_scalar_prefetch=1,
            grid=(1,),
            in_specs=[whole_block(grad_pre.shape)]
            + [whole_block(r.shape) for r in extra]
            + [wide] * 4,
            out_specs=[whole_block(s.shape) for s in shapes],
        ),
        out_shape=shapes,
        compiler_params=pltpu.CompilerParams(vmem_limit_bytes=VMEM_LIMIT),
        cost_estimate=pl.CostEstimate(
            flops=8 * rows * width * units,
            bytes_accessed=8 * width * units + 2 * rows * (4 * units + 3 * width // 2),
            transcendentals=0,
        ),
        name="unit_product",
    )(place, grad_pre, *extra, *weights)
    return outs[:lo], outs[lo:]


def outer_kernel(n_slice, which, final, place, *refs):
    xs, dys = refs[:n_slice], refs[n_slice : 2 * n_slice]
    grad_pre, weighted = refs[2 * n_slice : 2 * n_slice + 2]
    rest = refs[2 * n_slice + 2 :]
    gate_out, up_out, down_out = rest[-3:]
    units = gate_out.shape[1]
    step = pl.program_id(0)
    for at in range(n_slice):

        @pl.when(step == at)
        def _(at=at):
            x, dy = xs[at][...], dys[at][...]
            both = dot(x, grad_pre[:, 2 * which * units : 2 * (which + 1) * units], 0, 0)
            gate, up = both[:, :units], both[:, units:]
            down = dot(weighted[:, which * units : (which + 1) * units], dy, 0, 0)
            if final:
                gate_in, up_in, down_in, down_w, fisher, anchor = rest[:6]
                gate = gate + gate_in[...].astype(F32)
                up = up + up_in[...].astype(F32)
                down = down + down_in[...].astype(F32)
                down = down + fisher[...] * (down_w[...].astype(F32) - anchor[...])
            gate_out[...] = gate.astype(BF)
            up_out[...] = up.astype(BF)
            down_out[...] = down.astype(BF)


def outer_products(place, xs, dys, grad_pre, weighted, which, final=()):
    n_slice = len(xs)
    rows, width = xs[0].shape
    units = grad_pre.shape[1] // 4
    wide = pl.BlockSpec((width, units), lambda s, p: (p[0] ^ s, 0))
    tall = pl.BlockSpec((units, width), lambda s, p: (0, p[0] ^ s))
    full = n_slice * width
    return pl.pallas_call(
        functools.partial(outer_kernel, n_slice, which, bool(final)),
        grid_spec=pltpu.PrefetchScalarGridSpec(
            num_scalar_prefetch=1,
            grid=(n_slice,),
            in_specs=[whole_block((rows, width))] * (2 * n_slice)
            + [whole_block(grad_pre.shape), whole_block(weighted.shape)]
            + ([wide, wide, tall, tall, tall, tall] if final else []),
            out_specs=[wide, wide, tall],
        ),
        out_shape=[
            jax.ShapeDtypeStruct((full, units), BF),
            jax.ShapeDtypeStruct((full, units), BF),
            jax.ShapeDtypeStruct((units, full), BF),
        ],
        compiler_params=pltpu.CompilerParams(vmem_limit_bytes=VMEM_LIMIT),
        cost_estimate=pl.CostEstimate(
            flops=6 * rows * full * units,
            bytes_accessed=full * (4 * rows + 6 * units + (16 * units if final else 0)),
            transcendentals=0,
        ),
        name="outer_final" if final else "outer_other",
    )(place, *xs, *dys, grad_pre, weighted, *final)


def per_device(
    n_expert,
    n_slice,
    tokens,
    cotangent,
    route_ids,
    route_weights,
    gate_weight,
    up_weight,
    down_weight,
    fisher,
    anchor,
):
    count, width = tokens.shape
    chips = n_expert // 2
    lo = 1 << ((chips.bit_length() - 1) // 2)
    hi = chips // lo
    own_e, own_f = lax.axis_index("expert"), lax.axis_index("ffn")
    place = jnp.stack([own_f, own_e]).astype(jnp.int32)

    def over_expert(value, mask):
        pairs = [(i, i ^ mask) for i in range(n_expert)]
        return lax.ppermute(value, "expert", pairs)

    def over_lo(value, mask):
        return over_expert(value, 2 * mask)

    def over_hi(value, mask):
        return over_expert(value, 2 * lo * mask)

    def over_slice(value, mask):
        return lax.ppermute(value, "ffn", [(i, i ^ mask) for i in range(n_slice)])

    def collect(value, send, number, axis):
        return jnp.stack([value] + [send(value, m) for m in range(1, number)], axis=axis)

    named = route_ids[:, :, None] == jnp.arange(LANES, dtype=jnp.int32)[None, None, :]
    route_row = jnp.sum(
        jnp.where(named, route_weights.astype(F32)[:, :, None], 0.0), axis=1
    ).astype(BF)

    x_parts = [tokens] + [over_slice(tokens, s) for s in range(1, n_slice)]
    dy_parts = [cotangent] + [over_slice(cotangent, s) for s in range(1, n_slice)]
    dy_parts[0] = jnp.concatenate([cotangent, route_row], axis=1)
    xs, dys = [], []
    for s in range(n_slice):
        x = collect(collect(x_parts[s], over_lo, lo, 0), over_hi, hi, 0)
        dy = collect(collect(dy_parts[s], over_hi, hi, 0), over_lo, lo, 1)
        xs.append(x.reshape(chips * count, -1))
        dys.append(dy.reshape(chips * count, -1))
    route_w = dys[0][:, width:]
    dys[0] = dys[0][:, :width]

    mine = (gate_weight[0], up_weight[0], down_weight[0])
    other = tuple(over_expert(w, 1) for w in mine)
    grad_pre, weighted, route = forward_values(place, xs, dys, route_w, mine, other, n_expert)

    projections = (mine[0], mine[1], other[0], other[1])
    half = width // 2
    shares, route_sum = {}, None
    for s in reversed(range(n_slice)):
        first = s == n_slice - 1
        a, b = unit_product(
            place, grad_pre, projections, s, lo, hi, count, width, route if first else None
        )
        a_sum = a[0] + sum(over_lo(a[m], m).astype(F32) for m in range(1, lo))
        b_sum = b[0] + sum(over_hi(b[h], h).astype(F32) for h in range(1, hi))
        if first:
            pair = split_pair(join_pair(a_sum[..., half:], n_expert))
            pad = jnp.zeros(pair.shape[:-1] + (LANES - 2 * n_expert,), BF)
            a_out = jnp.concatenate([a_sum[..., :half].astype(BF), pair, pad], axis=-1)
        else:
            a_out = a_sum.astype(BF)
        a_own = a_sum[0] + sum(over_hi(a_out[h], h).astype(F32) for h in range(1, hi))
        b_out = b_sum.astype(BF)
        b_own = b_sum[0] + sum(over_lo(b_out[m], m).astype(F32) for m in range(1, lo))
        if first:
            route_sum = join_pair(a_own[:, half:], n_expert)
            a_own = a_own[:, :half]
        shares[s] = jnp.concatenate([a_own, b_own], axis=1)
    pair = split_pair(route_sum)
    pad = jnp.zeros((count, LANES - 2 * n_expert), BF)
    total, route_total = shares[0], route_sum
    for s in range(1, n_slice):
        got = over_slice(jnp.concatenate([shares[s].astype(BF), pair, pad], axis=1), s)
        total = total + got[:, :width].astype(F32)
        route_total = route_total + join_pair(got[:, width:], n_expert)
    grad_tokens = total.astype(BF)
    chosen = route_ids[:, :, None] == jnp.arange(n_expert, dtype=jnp.int32)[None, None, :]
    grad_route = jnp.sum(jnp.where(chosen, route_total[:, None, :], 0.0), axis=2)

    sent = outer_products(place, xs, dys, grad_pre, weighted, 1)
    got = [over_expert(g, 1) for g in sent]
    grads = outer_products(
        place, xs, dys, grad_pre, weighted, 0, (*got, mine[2], fisher[0], anchor[0])
    )
    return (grad_tokens, grad_route, grads[0][None], grads[1][None], grads[2][None])


def solution(mesh):
    return jax.shard_map(
        functools.partial(per_device, mesh.shape["expert"], mesh.shape["ffn"]),
        mesh=mesh,
        in_specs=(
            P("expert", "ffn"),
            P("expert", "ffn"),
            P("expert", None),
            P("expert", None),
            P("expert", None, "ffn"),
            P("expert", None, "ffn"),
            P("expert", "ffn", None),
            P("expert", "ffn", None),
            P("expert", "ffn", None),
        ),
        out_specs=(
            P("expert", "ffn"),
            P("expert", None),
            P("expert", None, "ffn"),
            P("expert", None, "ffn"),
            P("expert", "ffn", None),
        ),
        check_vma=False,
    )
```

time: 285 us -> 186 us (0.65)
  waiting for transfers between devices: 142 us -> 57.3 us
  blocking collectives: 52 us -> 0 us
  Pallas kernels: 0 us -> 45.6 us
  starting transfers between devices: 18.9 us -> 60.4 us
  matrix products: 29.3 us -> 0 us
  local copies, waits for them, and re-layouts: 23 us -> 8.63 us
  between operations: 14.2 us -> 1.33 us
  other arithmetic: 4.79 us -> 12.4 us
    reduce_scatter x1 -> x0, waiting for transfers between devices: 91 us -> none  [per_device(): lax.psum_scatter(feature_part, 'ffn', scatter_dimension=2, tiled=True)]
    ppermute x0 -> x47, starting transfers between devices: none -> 60.4 us  [the longest x38 38.4 us: over_expert(): return lax.ppermute(value, 'expert', pairs)]
    ppermute x0 -> x47, waiting for transfers between devices: none -> 57.3 us  [the longest x38 46.1 us: over_expert(): return lax.ppermute(value, 'expert', pairs)]
    all_to_all x4 -> x0, waiting for transfers between devices: 51.4 us -> none  [the longest x1 31 us: per_device(): lax.all_to_all(sent_dy, 'expert', split_axis=0, concat_axis=0, tiled=True)]
    pallas_call x0 -> x7, Pallas kernels: none -> 45.6 us  [the longest x2 19.5 us: outer_products(): pl.pallas_call(functools.partial(outer_kernel, n_slice, which, bool(final...]
    all_gather x2 -> x0, blocking collectives: 32.9 us -> none  [the longest x1 16.8 us: per_device(): lax.all_gather(tokens, 'ffn', axis=1, tiled=True)]
    dot_general x8 -> x0, matrix products: 29.3 us -> none  [the longest x1 4.79 us: expert_pass(): lax.dot_general(weighted, rows_dy, over_rows, preferred_element_type=jnp....]
    all_to_all x4 -> x0, starting transfers between devices: 18.7 us -> none  [the longest x1 5.17 us: per_device(): lax.all_to_all(slot_weight, 'expert', split_axis=0, concat_axis=0, tiled=...]
  transfers between devices with their start and end apart: 5 -> 47, of which waited for: 4 -> 23; matrix products, arithmetic and copies ran while one was open for 12% -> 9% of each run, Pallas kernels for 0% -> 10%
where the time goes in v1:
time: 186 us
  starting transfers between devices  60.4 us (32%)
  waiting for transfers between devices  57.3 us (31%)
  Pallas kernels  45.6 us (25%)
  other arithmetic  12.4 us (7%)
  local copies, waits for them, and re-layouts  8.63 us (5%)
    ppermute x38, waiting for transfers between devices, over_expert(): return lax.ppermute(value, 'expert', pairs)  46.1 us
    ppermute x38, starting transfers between devices, over_expert(): return lax.ppermute(value, 'expert', pairs)  38.4 us
    ppermute x9, starting transfers between devices, over_slice(): return lax.ppermute(value, 'ffn', [(i, i ^ mask) for i in range(n_slice)])  22.1 us
    pallas_call x2, Pallas kernels, outer_products(): pl.pallas_call(functools.partial(outer_kernel, n_slice, which, bool(final...  19.5 us
    pallas_call x4, Pallas kernels, unit_product(): pl.pallas_call(functools.partial(unit_kernel, lo, hi, tokens, route is no...  15.6 us
    ppermute x9, waiting for transfers between devices, over_slice(): return lax.ppermute(value, 'ffn', [(i, i ^ mask) for i in range(n_slice)])  11.2 us
    pallas_call x1, Pallas kernels, forward_values(): pl.pallas_call(functools.partial(forward_kernel, n_slice, n_expert), grid...  10.5 us
    another operation x17, other arithmetic, collect(): jnp.stack([value] + [send(value, m) for m in range(1, number)], axis=axis)  5.83 us
  transfers between devices with their start and end apart: 47, of which 23 were waited for; matrix products, arithmetic and copies ran while one was open for 9% of the time, Pallas kernels for 10%

profile of v1, /device:TPU:0, one launch (start us, length us, event | category | flops | bytes accessed | tf_op | source)
XLA Modules:
  0.0 185.7 jit_solution(16728799479125336155)
XLA Ops:
  0.6 3.1 %collective-permute-start.13 = (bf16[64,1024]{1,0:T(8,128)(2,1)}, bf16[64,1024]{1,0:T(8,128)(2,1)S(1)}, u32[]{:S(2)}, u32[]{:S(2)}) collective-permute-start(bf16[64,1024]{1,0:T(8,128)(2,1)} %param.10), channel_id=1, source_target_pairs={{0,1},{1,0},{2,3},{3,2},{4,5},{5,4},{6,7},{7,6},{8,9},{9,8},{10,11... | collective-permute-start | bytes 393224 | tf_op jit(solution)/shard_map/ppermute | solution.py:270
  3.7 2.5 %collective-permute-start.19 = (bf16[64,1024]{1,0:T(8,128)(2,1)}, bf16[64,1024]{1,0:T(8,128)(2,1)S(1)}, u32[]{:S(2)}, u32[]{:S(2)}) collective-permute-start(bf16[64,1024]{1,0:T(8,128)(2,1)} %param.10), channel_id=1, source_target_pairs={{0,3},{1,2},{2,1},{3,0},{4,7},{5,6},{6,5},{7,4},{8,11},{9,10},{10,... | collective-permute-start | bytes 393224 | tf_op jit(solution)/shard_map/ppermute | solution.py:270
  6.3 1.8 collective-permute-start.2
  8.1 1.5 collective-permute-start
  11.1 3.0 %collective-permute-start.8 = (bf16[64,1024]{1,0:T(8,128)(2,1)}, bf16[64,1024]{1,0:T(8,128)(2,1)S(1)}, u32[]{:S(2)}, u32[]{:S(2)}) collective-permute-start(bf16[64,1024]{1,0:T(8,128)(2,1)} %param.9), channel_id=1, source_target_pairs={{0,3},{1,2},{2,1},{3,0},{4,7},{5,6},{6,5},{7,4},{8,11},{9,10},{10,... | collective-permute-start | bytes 393224 | tf_op jit(solution)/shard_map/ppermute | solution.py:270
  14.1 4.7 %collective-permute-start.5 = (bf16[64,1024]{1,0:T(8,128)(2,1)}, bf16[64,1024]{1,0:T(8,128)(2,1)S(1)}, u32[]{:S(2)}, u32[]{:S(2)}) collective-permute-start(bf16[64,1024]{1,0:T(8,128)(2,1)} %param.9), channel_id=1, source_target_pairs={{0,2},{1,3},{2,0},{3,1},{4,6},{5,7},{6,4},{7,5},{8,10},{9,11},{10,... | collective-permute-start | bytes 393224 | tf_op jit(solution)/shard_map/ppermute | solution.py:270
  19.7 5.0 %collective-permute-done.16 = bf16[64,1024]{1,0:T(8,128)(2,1)S(1)} collective-permute-done((bf16[64,1024]{1,0:T(8,128)(2,1)}, bf16[64,1024]{1,0:T(8,128)(2,1)S(1)}, u32[]{:S(2)}, u32[]{:S(2)}) %collective-permute-start.16) | collective-permute-done | bytes 131104 | tf_op jit(solution)/shard_map/ppermute | solution.py:270
  24.7 1.5 collective-permute-start.11
  26.8 1.5 collective-permute-start.20
  29.4 1.5 collective-permute-start.6
  34.1 1.5 collective-permute-start.3
  36.2 4.2 %collective-permute-done.3 = bf16[64,1024]{1,0:T(8,128)(2,1)S(1)} collective-permute-done((bf16[64,1024]{1,0:T(8,128)(2,1)S(1)}, bf16[64,1024]{1,0:T(8,128)(2,1)S(1)}, u32[]{:S(2)}, u32[]{:S(2)}) %collective-permute-start.3) | collective-permute-done | bytes 131104 | tf_op jit(solution)/shard_map/ppermute | solution.py:261
  40.5 1.5 collective-permute-start.1
  42.4 1.5 collective-permute-start.12
  44.1 3.1 %collective-permute-done.1 = bf16[2,64,1024]{2,1,0:T(8,128)(2,1)S(1)} collective-permute-done((bf16[2,64,1024]{2,1,0:T(8,128)(2,1)S(1)}, bf16[2,64,1024]{2,1,0:T(8,128)(2,1)S(1)}, u32[]{:S(2)}, u32[]{:S(2)}) %collective-permute-start.1) | collective-permute-done | bytes 262176 | tf_op jit(solution)/shard_map/ppermute | solution.py:261
  48.6 3.8 %collective-permute-done.12 = bf16[2,64,1152]{2,1,0:T(8,128)(2,1)S(1)} collective-permute-done((bf16[2,64,1152]{2,1,0:T(8,128)(2,1)S(1)}, bf16[2,64,1152]{2,1,0:T(8,128)(2,1)S(1)}, u32[]{:S(2)}, u32[]{:S(2)}) %collective-permute-start.12) | collective-permute-done | bytes 294944 | tf_op jit(solution)/shard_map/ppermute | solution.py:261
  52.4 1.5 collective-permute-start.21
  54.8 3.2 %collective-permute-done.15 = bf16[2,64,1024]{2,1,0:T(8,128)(2,1)S(1)} collective-permute-done((bf16[2,64,1024]{2,1,0:T(8,128)(2,1)S(1)}, bf16[2,64,1024]{2,1,0:T(8,128)(2,1)S(1)}, u32[]{:S(2)}, u32[]{:S(2)}) %collective-permute-start.15) | collective-permute-done | bytes 262176 | tf_op jit(solution)/shard_map/ppermute | solution.py:261
  58.0 1.5 collective-permute-start.18
  59.5 4.1 %collective-permute-done.21 = bf16[2,64,1024]{2,1,0:T(8,128)(2,1)S(1)} collective-permute-done((bf16[2,64,1024]{2,1,0:T(8,128)(2,1)S(1)}, bf16[2,64,1024]{2,1,0:T(8,128)(2,1)S(1)}, u32[]{:S(2)}, u32[]{:S(2)}) %collective-permute-start.21) | collective-permute-done | bytes 262176 | tf_op jit(solution)/shard_map/ppermute | solution.py:261
  63.6 1.5 collective-permute-start.4
  67.5 1.5 collective-permute-start.10
  69.1 2.4 %collective-permute-done.4 = bf16[2,64,1024]{2,1,0:T(8,128)(2,1)S(1)} collective-permute-done((bf16[2,64,1024]{2,1,0:T(8,128)(2,1)S(1)}, bf16[2,64,1024]{2,1,0:T(8,128)(2,1)S(1)}, u32[]{:S(2)}, u32[]{:S(2)}) %collective-permute-start.4) | collective-permute-done | bytes 262176 | tf_op jit(solution)/shard_map/ppermute | solution.py:261
  71.5 1.5 collective-permute-start.7
  78.0 3.2 %collective-permute-done.7 = bf16[2,64,1024]{2,1,0:T(8,128)(2,1)S(1)} collective-permute-done((bf16[2,64,1024]{2,1,0:T(8,128)(2,1)S(1)}, bf16[2,64,1024]{2,1,0:T(8,128)(2,1)S(1)}, u32[]{:S(2)}, u32[]{:S(2)}) %collective-permute-start.7) | collective-permute-done | bytes 262176 | tf_op jit(solution)/shard_map/ppermute | solution.py:261
  84.8 10.5 %forward_values.1 = (bf16[256,1024]{1,0:T(8,128)(2,1)}, bf16[256,512]{1,0:T(8,128)(2,1)}, bf16[256,128]{1,0:T(8,128)(2,1)}) custom-call(s32[2]{0:T(128)} %pad_add_fusion.place, bf16[256,1024]{1,0:T(8,128)(2,1)} %bitcast.132, bf16[256,1024]{1,0:T(8,128)(2,1)} %bitcast.144, bf16[256,1024]{1,0:T(8,128)(2,1)} %bitcast.150, bf16[256,1024]{1,0:T(8,128)(2,1)} %bitcast.147, ...), custom_call_target="tpu_custom_call" | custom-call | flops 3221225472 | bytes 16777216 | tf_op jit(solution)/shard_map/forward_values/pallas_call | solution.py:96
  95.3 3.9 %unit_product.7 = (f32[2,64,512]{2,1,0:T(8,128)}, bf16[2,64,512]{2,1,0:T(8,128)(2,1)}, f32[2,64,512]{2,1,0:T(8,128)}, bf16[2,64,512]{2,1,0:T(8,128)(2,1)}) custom-call(s32[2]{0:T(128)} %pad_add_fusion.place, bf16[256,1024]{1,0:T(8,128)(2,1)} %get-tuple-element.30.grad_pre.refs_8_, bf16[4096,256]{1,0:T(8,128)(2,1)} %bitcast.119, bf16[4096,256]{1,0:T(8,128)(2,1)} %bitcast.125, ...), custom_call_target="tpu_custom_call" | custom-call | flops 536870912 | bytes 3407872 | tf_op jit(solution)/shard_map/unit_product/pallas_call | solution.py:159
  99.2 1.5 collective-permute-start.36
  100.7 1.5 collective-permute-start.38
  102.2 3.9 %unit_product.5 = (f32[2,64,512]{2,1,0:T(8,128)}, bf16[2,64,512]{2,1,0:T(8,128)(2,1)}, f32[2,64,512]{2,1,0:T(8,128)}, bf16[2,64,512]{2,1,0:T(8,128)(2,1)}) custom-call(s32[2]{0:T(128)} %pad_add_fusion.place, bf16[256,1024]{1,0:T(8,128)(2,1)} %get-tuple-element.30.grad_pre.refs_8_, bf16[4096,256]{1,0:T(8,128)(2,1)} %bitcast.120, bf16[4096,256]{1,0:T(8,128)(2,1)} %bitcast.126, ...), custom_call_target="tpu_custom_call" | custom-call | flops 536870912 | bytes 3407872 | tf_op jit(solution)/shard_map/unit_product/pallas_call | solution.py:159
  107.2 3.9 %unit_product.4 = (f32[2,64,512]{2,1,0:T(8,128)}, bf16[2,64,512]{2,1,0:T(8,128)(2,1)}, f32[2,64,512]{2,1,0:T(8,128)}, bf16[2,64,512]{2,1,0:T(8,128)(2,1)}) custom-call(s32[2]{0:T(128)} %pad_add_fusion.place, bf16[256,1024]{1,0:T(8,128)(2,1)} %get-tuple-element.30.grad_pre.refs_8_, bf16[4096,256]{1,0:T(8,128)(2,1)} %bitcast.121, bf16[4096,256]{1,0:T(8,128)(2,1)} %bitcast.127, ...), custom_call_target="tpu_custom_call" | custom-call | flops 536870912 | bytes 3407872 | tf_op jit(solution)/shard_map/unit_product/pallas_call | solution.py:159
  111.0 1.5 collective-permute-start.25
  112.5 4.0 %unit_product.6 = (f32[2,64,640]{2,1,0:T(8,128)}, bf16[2,64,640]{2,1,0:T(8,128)(2,1)}, f32[2,64,512]{2,1,0:T(8,128)}, bf16[2,64,512]{2,1,0:T(8,128)(2,1)}) custom-call(s32[2]{0:T(128)} %pad_add_fusion.place, bf16[256,1024]{1,0:T(8,128)(2,1)} %get-tuple-element.30.grad_pre.refs_8_, bf16[256,128]{1,0:T(8,128)(2,1)} %get-tuple-element.39.refs_0_, ...), custom_call_target="tpu_custom_call" | custom-call | flops 536870912 | bytes 3407872 | tf_op jit(solution)/shard_map/unit_product/pallas_call | solution.py:159
  116.5 7.4 %outer_other.1 = (bf16[4096,256]{1,0:T(8,128)(2,1)}, bf16[4096,256]{1,0:T(8,128)(2,1)}, bf16[256,4096]{1,0:T(8,128)(2,1)}) custom-call(s32[2]{0:T(128)} %pad_add_fusion.place, bf16[256,1024]{1,0:T(8,128)(2,1)} %bitcast.133, bf16[256,1024]{1,0:T(8,128)(2,1)} %bitcast.145, bf16[256,1024]{1,0:T(8,128)(2,1)} %bitcast.151, bf16[256,1024]{1,0:T(8,128)(2,1)} %bitcast.148, ...), custom_call_target="tpu_custom_call" | custom-call | flops 1610612736 | bytes 10485760 | tf_op jit(solution)/shard_map/outer_other/pallas_call | solution.py:214
  124.0 1.6 collective-permute-start.27
  129.1 1.6 collective-permute-done.41
  133.5 2.9 %collective-permute-done.26 = bf16[64,512]{1,0:T(8,128)(2,1)S(1)} collective-permute-done((bf16[64,512]{1,0:T(8,128)(2,1)S(1)}, bf16[64,512]{1,0:T(8,128)(2,1)S(1)}, u32[]{:S(2)}, u32[]{:S(2)}) %collective-permute-start.26) | collective-permute-done | bytes 65568 | tf_op jit(solution)/shard_map/ppermute | solution.py:261
  136.9 4.1 %collective-permute-done.28 = bf16[64,512]{1,0:T(8,128)(2,1)S(1)} collective-permute-done((bf16[64,512]{1,0:T(8,128)(2,1)S(1)}, bf16[64,512]{1,0:T(8,128)(2,1)S(1)}, u32[]{:S(2)}, u32[]{:S(2)}) %collective-permute-start.28) | collective-permute-done | bytes 65568 | tf_op jit(solution)/shard_map/ppermute | solution.py:261
  142.7 3.1 %collective-permute-done.39 = bf16[64,512]{1,0:T(8,128)(2,1)S(1)} collective-permute-done((bf16[64,512]{1,0:T(8,128)(2,1)S(1)}, bf16[64,512]{1,0:T(8,128)(2,1)S(1)}, u32[]{:S(2)}, u32[]{:S(2)}) %collective-permute-start.39) | collective-permute-done | bytes 65568 | tf_op jit(solution)/shard_map/ppermute | solution.py:261
  146.2 1.8 collective-permute-start.42
  148.0 2.8 %collective-permute-done.42 = bf16[64,512]{1,0:T(8,128)(2,1)S(1)} collective-permute-done((bf16[64,512]{1,0:T(8,128)(2,1)S(1)}, bf16[64,512]{1,0:T(8,128)(2,1)S(1)}, u32[]{:S(2)}, u32[]{:S(2)}) %collective-permute-start.42) | collective-permute-done | bytes 65568 | tf_op jit(solution)/shard_map/ppermute | solution.py:261
  151.9 3.4 %collective-permute-done.34 = bf16[64,640]{1,0:T(8,128)(2,1)S(1)} collective-permute-done((bf16[64,640]{1,0:T(8,128)(2,1)S(1)}, bf16[64,640]{1,0:T(8,128)(2,1)S(1)}, u32[]{:S(2)}, u32[]{:S(2)}) %collective-permute-start.34) | collective-permute-done | bytes 81952 | tf_op jit(solution)/shard_map/ppermute | solution.py:261
  155.5 4.1 %collective-permute-start.43 = (bf16[64,1152]{1,0:T(8,128)(2,1)S(1)}, bf16[64,1152]{1,0:T(8,128)(2,1)}, u32[]{:S(2)}, u32[]{:S(2)}) collective-permute-start(bf16[64,1152]{1,0:T(8,128)(2,1)S(1)} %concatenate.37), channel_id=1, source_target_pairs={{0,3},{1,2},{2,1},{3,0},{4,7},{5,6},{6,5},{7,4},{8,11},{9,10},{10,... | collective-permute-start | bytes 442376 | tf_op jit(solution)/shard_map/ppermute | solution.py:270
  159.9 3.7 %collective-permute-done.43 = bf16[64,1152]{1,0:T(8,128)(2,1)} collective-permute-done((bf16[64,1152]{1,0:T(8,128)(2,1)S(1)}, bf16[64,1152]{1,0:T(8,128)(2,1)}, u32[]{:S(2)}, u32[]{:S(2)}) %collective-permute-start.43) | collective-permute-done | bytes 147488 | tf_op jit(solution)/shard_map/ppermute | solution.py:270
  163.6 2.7 %collective-permute-start.40 = (bf16[64,1152]{1,0:T(8,128)(2,1)S(1)}, bf16[64,1152]{1,0:T(8,128)(2,1)S(1)}, u32[]{:S(2)}, u32[]{:S(2)}) collective-permute-start(bf16[64,1152]{1,0:T(8,128)(2,1)S(1)} %concatenate.36), channel_id=1, source_target_pairs={{0,2},{1,3},{2,0},{3,1},{4,6},{5,7},{6,4},{7,5},{8,10},{9,11},{10,... | collective-permute-start | bytes 442376 | tf_op jit(solution)/shard_map/ppermute | solution.py:270
  167.7 1.9 %collective-permute-done.40 = bf16[64,1152]{1,0:T(8,128)(2,1)S(1)} collective-permute-done((bf16[64,1152]{1,0:T(8,128)(2,1)S(1)}, bf16[64,1152]{1,0:T(8,128)(2,1)S(1)}, u32[]{:S(2)}, u32[]{:S(2)}) %collective-permute-start.40) | collective-permute-done | bytes 147488 | tf_op jit(solution)/shard_map/ppermute | solution.py:270
  170.4 1.7 fusion.2
  173.4 12.0 %outer_final.1 = (bf16[4096,256]{1,0:T(8,128)(2,1)}, bf16[4096,256]{1,0:T(8,128)(2,1)}, bf16[256,4096]{1,0:T(8,128)(2,1)}) custom-call(s32[2]{0:T(128)} %pad_add_fusion.place, bf16[256,1024]{1,0:T(8,128)(2,1)} %bitcast.134, bf16[256,1024]{1,0:T(8,128)(2,1)} %bitcast.146, bf16[256,1024]{1,0:T(8,128)(2,1)} %bitcast.152, bf16[256,1024]{1,0:T(8,128)(2,1)} %bitcast.149, ...), custom_call_target="tpu_custom_call" | custom-call | flops 1610612736 | bytes 27262976 | tf_op jit(solution)/shard_map/outer_final/pallas_call | solution.py:214
  (152 shorter events, 36.7 us)
Async XLA Ops:
  0.6 10.5 %collective-permute-start.13 = (bf16[64,1024]{1,0:T(8,128)(2,1)}, bf16[64,1024]{1,0:T(8,128)(2,1)S(1)}, u32[]{:S(2)}, u32[]{:S(2)}) collective-permute-start(bf16[64,1024]{1,0:T(8,128)(2,1)} %param.10), channel_id=1, source_target_pairs={{0,1},{1,0},{2,3},{3,2},{4,5},{5,4},{6,7},{7,6},{8,9},{9,8},{10,11... | collective-permute-start | bytes 393224 | tf_op jit(solution)/shard_map/ppermute | solution.py:270
  3.7 10.4 %collective-permute-start.19 = (bf16[64,1024]{1,0:T(8,128)(2,1)}, bf16[64,1024]{1,0:T(8,128)(2,1)S(1)}, u32[]{:S(2)}, u32[]{:S(2)}) collective-permute-start(bf16[64,1024]{1,0:T(8,128)(2,1)} %param.10), channel_id=1, source_target_pairs={{0,3},{1,2},{2,1},{3,0},{4,7},{5,6},{6,5},{7,4},{8,11},{9,10},{10,... | collective-permute-start | bytes 393224 | tf_op jit(solution)/shard_map/ppermute | solution.py:270
  6.2 18.5 %collective-permute-start.16 = (bf16[64,1024]{1,0:T(8,128)(2,1)}, bf16[64,1024]{1,0:T(8,128)(2,1)S(1)}, u32[]{:S(2)}, u32[]{:S(2)}) collective-permute-start(bf16[64,1024]{1,0:T(8,128)(2,1)} %param.10), channel_id=1, source_target_pairs={{0,2},{1,3},{2,0},{3,1},{4,6},{5,7},{6,4},{7,5},{8,10},{9,11},{10,... | collective-permute-start | bytes 393224 | tf_op jit(solution)/shard_map/ppermute | solution.py:270
  6.3 20.0 %collective-permute-start.2 = (bf16[64,1024]{1,0:T(8,128)(2,1)}, bf16[64,1024]{1,0:T(8,128)(2,1)S(1)}, u32[]{:S(2)}, u32[]{:S(2)}) collective-permute-start(bf16[64,1024]{1,0:T(8,128)(2,1)} %param.9), channel_id=1, source_target_pairs={{0,1},{1,0},{2,3},{3,2},{4,5},{5,4},{6,7},{7,6},{8,9},{9,8},{10,11... | collective-permute-start | bytes 393224 | tf_op jit(solution)/shard_map/ppermute | solution.py:270
  8.1 18.7 %collective-permute-start = (bf16[64,1024]{1,0:T(8,128)(2,1)}, bf16[64,1024]{1,0:T(8,128)(2,1)S(1)}, u32[]{:S(2)}, u32[]{:S(2)}) collective-permute-start(bf16[64,1024]{1,0:T(8,128)(2,1)} %param.9), channel_id=1, source_target_pairs={{0,8},{4,12},{8,0},{12,4},{16,24},{20,28},{24,16},{28,20},{1,9},{5... | collective-permute-start | bytes 393224 | tf_op jit(solution)/shard_map/ppermute | solution.py:261
  11.1 17.2 %collective-permute-start.8 = (bf16[64,1024]{1,0:T(8,128)(2,1)}, bf16[64,1024]{1,0:T(8,128)(2,1)S(1)}, u32[]{:S(2)}, u32[]{:S(2)}) collective-permute-start(bf16[64,1024]{1,0:T(8,128)(2,1)} %param.9), channel_id=1, source_target_pairs={{0,3},{1,2},{2,1},{3,0},{4,7},{5,6},{6,5},{7,4},{8,11},{9,10},{10,... | collective-permute-start | bytes 393224 | tf_op jit(solution)/shard_map/ppermute | solution.py:270
  14.1 15.3 %collective-permute-start.5 = (bf16[64,1024]{1,0:T(8,128)(2,1)}, bf16[64,1024]{1,0:T(8,128)(2,1)S(1)}, u32[]{:S(2)}, u32[]{:S(2)}) collective-permute-start(bf16[64,1024]{1,0:T(8,128)(2,1)} %param.9), channel_id=1, source_target_pairs={{0,2},{1,3},{2,0},{3,1},{4,6},{5,7},{6,4},{7,5},{8,10},{9,11},{10,... | collective-permute-start | bytes 393224 | tf_op jit(solution)/shard_map/ppermute | solution.py:270
  24.7 6.8 %collective-permute-start.11 = (bf16[64,1152]{1,0:T(8,128)(2,1)S(1)}, bf16[64,1152]{1,0:T(8,128)(2,1)S(1)}, u32[]{:S(2)}, u32[]{:S(2)}) collective-permute-start(bf16[64,1152]{1,0:T(8,128)(2,1)S(1)} %get-tuple-element.76), channel_id=1, source_target_pairs={{0,16},{4,20},{8,24},{12,28},{16,0},{20,4},{24,8},{28,12},{1,17},{... | collective-permute-start | bytes 442376 | tf_op jit(solution)/shard_map/ppermute | solution.py:261
  26.3 5.3 %collective-permute-start.14 = (bf16[64,1024]{1,0:T(8,128)(2,1)S(1)}, bf16[64,1024]{1,0:T(8,128)(2,1)S(1)}, u32[]{:S(2)}, u32[]{:S(2)}) collective-permute-start(bf16[64,1024]{1,0:T(8,128)(2,1)S(1)} %collective-permute-done.13), channel_id=1, source_target_pairs={{0,16},{4,20},{8,24},{12,28},{16,0},{20,4},{24,8},{28,12},{1,17},{... | collective-permute-start | bytes 393224 | tf_op jit(solution)/shard_map/ppermute | solution.py:261
  26.8 5.9 %collective-permute-start.20 = (bf16[64,1024]{1,0:T(8,128)(2,1)S(1)}, bf16[64,1024]{1,0:T(8,128)(2,1)S(1)}, u32[]{:S(2)}, u32[]{:S(2)}) collective-permute-start(bf16[64,1024]{1,0:T(8,128)(2,1)S(1)} %collective-permute-done.19), channel_id=1, source_target_pairs={{0,16},{4,20},{8,24},{12,28},{16,0},{20,4},{24,8},{28,12},{1,17},{... | collective-permute-start | bytes 393224 | tf_op jit(solution)/shard_map/ppermute | solution.py:261
  28.3 5.8 %collective-permute-start.17 = (bf16[64,1024]{1,0:T(8,128)(2,1)S(1)}, bf16[64,1024]{1,0:T(8,128)(2,1)S(1)}, u32[]{:S(2)}, u32[]{:S(2)}) collective-permute-start(bf16[64,1024]{1,0:T(8,128)(2,1)S(1)} %collective-permute-done.16), channel_id=1, source_target_pairs={{0,16},{4,20},{8,24},{12,28},{16,0},{20,4},{24,8},{28,12},{1,17},{... | collective-permute-start | bytes 393224 | tf_op jit(solution)/shard_map/ppermute | solution.py:261
  29.4 6.2 %collective-permute-start.6 = (bf16[64,1024]{1,0:T(8,128)(2,1)S(1)}, bf16[64,1024]{1,0:T(8,128)(2,1)S(1)}, u32[]{:S(2)}, u32[]{:S(2)}) collective-permute-start(bf16[64,1024]{1,0:T(8,128)(2,1)S(1)} %collective-permute-done.5), channel_id=1, source_target_pairs={{0,8},{4,12},{8,0},{12,4},{16,24},{20,28},{24,16},{28,20},{1,9},{5... | collective-permute-start | bytes 393224 | tf_op jit(solution)/shard_map/ppermute | solution.py:261
  31.6 50.5 %collective-permute-start.22 = (bf16[4096,256]{1,0:T(8,128)(2,1)}, bf16[4096,256]{1,0:T(8,128)(2,1)S(1)}, u32[]{:S(2)}, u32[]{:S(2)}) collective-permute-start(bf16[4096,256]{1,0:T(8,128)(2,1)} %bitcast.117), channel_id=1, source_target_pairs={{0,4},{4,0},{8,12},{12,8},{16,20},{20,16},{24,28},{28,24},{1,5},{5... | collective-permute-start | bytes 6291464 | tf_op jit(solution)/shard_map/ppermute | solution.py:261
  31.6 50.5 %collective-permute-start.23 = (bf16[4096,256]{1,0:T(8,128)(2,1)}, bf16[4096,256]{1,0:T(8,128)(2,1)S(1)}, u32[]{:S(2)}, u32[]{:S(2)}) collective-permute-start(bf16[4096,256]{1,0:T(8,128)(2,1)} %bitcast.123), channel_id=1, source_target_pairs={{0,4},{4,0},{8,12},{12,8},{16,20},{20,16},{24,28},{28,24},{1,5},{5... | collective-permute-start | bytes 6291464 | tf_op jit(solution)/shard_map/ppermute | solution.py:261
  32.7 49.4 %collective-permute-start.24 = (bf16[256,4096]{1,0:T(8,128)(2,1)}, bf16[256,4096]{1,0:T(8,128)(2,1)S(1)}, u32[]{:S(2)}, u32[]{:S(2)}) collective-permute-start(bf16[256,4096]{1,0:T(8,128)(2,1)} %bitcast.129), channel_id=1, source_target_pairs={{0,4},{4,0},{8,12},{12,8},{16,20},{20,16},{24,28},{28,24},{1,5},{5... | collective-permute-start | bytes 6291464 | tf_op jit(solution)/shard_map/ppermute | solution.py:261
  34.1 6.3 %collective-permute-start.3 = (bf16[64,1024]{1,0:T(8,128)(2,1)S(1)}, bf16[64,1024]{1,0:T(8,128)(2,1)S(1)}, u32[]{:S(2)}, u32[]{:S(2)}) collective-permute-start(bf16[64,1024]{1,0:T(8,128)(2,1)S(1)} %collective-permute-done.2), channel_id=1, source_target_pairs={{0,8},{4,12},{8,0},{12,4},{16,24},{20,28},{24,16},{28,20},{1,9},{5... | collective-permute-start | bytes 393224 | tf_op jit(solution)/shard_map/ppermute | solution.py:261
  35.6 6.8 %collective-permute-start.9 = (bf16[64,1024]{1,0:T(8,128)(2,1)S(1)}, bf16[64,1024]{1,0:T(8,128)(2,1)S(1)}, u32[]{:S(2)}, u32[]{:S(2)}) collective-permute-start(bf16[64,1024]{1,0:T(8,128)(2,1)S(1)} %collective-permute-done.8), channel_id=1, source_target_pairs={{0,8},{4,12},{8,0},{12,4},{16,24},{20,28},{24,16},{28,20},{1,9},{5... | collective-permute-start | bytes 393224 | tf_op jit(solution)/shard_map/ppermute | solution.py:261
  40.5 6.7 %collective-permute-start.1 = (bf16[2,64,1024]{2,1,0:T(8,128)(2,1)S(1)}, bf16[2,64,1024]{2,1,0:T(8,128)(2,1)S(1)}, u32[]{:S(2)}, u32[]{:S(2)}) collective-permute-start(bf16[2,64,1024]{2,1,0:T(8,128)(2,1)S(1)} %get-tuple-element.72), channel_id=1, source_target_pairs={{0,16},{4,20},{8,24},{12,28},{16,0},{20,4},{24,8},{28,12},{1,17},{... | collective-permute-start | bytes 786440 | tf_op jit(solution)/shard_map/ppermute | solution.py:261
  42.4 9.9 %collective-permute-start.12 = (bf16[2,64,1152]{2,1,0:T(8,128)(2,1)S(1)}, bf16[2,64,1152]{2,1,0:T(8,128)(2,1)S(1)}, u32[]{:S(2)}, u32[]{:S(2)}) collective-permute-start(bf16[2,64,1152]{2,1,0:T(8,128)(2,1)S(1)} %get-tuple-element.58), channel_id=1, source_target_pairs={{0,8},{4,12},{8,0},{12,4},{16,24},{20,28},{24,16},{28,20},{1,9},{5... | collective-permute-start | bytes 884744 | tf_op jit(solution)/shard_map/ppermute | solution.py:261
  47.1 10.9 %collective-permute-start.15 = (bf16[2,64,1024]{2,1,0:T(8,128)(2,1)S(1)}, bf16[2,64,1024]{2,1,0:T(8,128)(2,1)S(1)}, u32[]{:S(2)}, u32[]{:S(2)}) collective-permute-start(bf16[2,64,1024]{2,1,0:T(8,128)(2,1)S(1)} %get-tuple-element.64), channel_id=1, source_target_pairs={{0,8},{4,12},{8,0},{12,4},{16,24},{20,28},{24,16},{28,20},{1,9},{5... | collective-permute-start | bytes 786440 | tf_op jit(solution)/shard_map/ppermute | solution.py:261
  52.4 11.2 %collective-permute-start.21 = (bf16[2,64,1024]{2,1,0:T(8,128)(2,1)S(1)}, bf16[2,64,1024]{2,1,0:T(8,128)(2,1)S(1)}, u32[]{:S(2)}, u32[]{:S(2)}) collective-permute-start(bf16[2,64,1024]{2,1,0:T(8,128)(2,1)S(1)} %get-tuple-element.60), channel_id=1, source_target_pairs={{0,8},{4,12},{8,0},{12,4},{16,24},{20,28},{24,16},{28,20},{1,9},{5... | collective-permute-start | bytes 786440 | tf_op jit(solution)/shard_map/ppermute | solution.py:261
  58.0 9.5 %collective-permute-start.18 = (bf16[2,64,1024]{2,1,0:T(8,128)(2,1)S(1)}, bf16[2,64,1024]{2,1,0:T(8,128)(2,1)S(1)}, u32[]{:S(2)}, u32[]{:S(2)}) collective-permute-start(bf16[2,64,1024]{2,1,0:T(8,128)(2,1)S(1)} %get-tuple-element.62), channel_id=1, source_target_pairs={{0,8},{4,12},{8,0},{12,4},{16,24},{20,28},{24,16},{28,20},{1,9},{5... | collective-permute-start | bytes 786440 | tf_op jit(solution)/shard_map/ppermute | solution.py:261
  63.6 7.9 %collective-permute-start.4 = (bf16[2,64,1024]{2,1,0:T(8,128)(2,1)S(1)}, bf16[2,64,1024]{2,1,0:T(8,128)(2,1)S(1)}, u32[]{:S(2)}, u32[]{:S(2)}) collective-permute-start(bf16[2,64,1024]{2,1,0:T(8,128)(2,1)S(1)} %get-tuple-element.70), channel_id=1, source_target_pairs={{0,16},{4,20},{8,24},{12,28},{16,0},{20,4},{24,8},{28,12},{1,17},{... | collective-permute-start | bytes 786440 | tf_op jit(solution)/shard_map/ppermute | solution.py:261
  67.5 9.6 %collective-permute-start.10 = (bf16[2,64,1024]{2,1,0:T(8,128)(2,1)S(1)}, bf16[2,64,1024]{2,1,0:T(8,128)(2,1)S(1)}, u32[]{:S(2)}, u32[]{:S(2)}) collective-permute-start(bf16[2,64,1024]{2,1,0:T(8,128)(2,1)S(1)} %get-tuple-element.66), channel_id=1, source_target_pairs={{0,16},{4,20},{8,24},{12,28},{16,0},{20,4},{24,8},{28,12},{1,17},{... | collective-permute-start | bytes 786440 | tf_op jit(solution)/shard_map/ppermute | solution.py:261
  71.5 9.7 %collective-permute-start.7 = (bf16[2,64,1024]{2,1,0:T(8,128)(2,1)S(1)}, bf16[2,64,1024]{2,1,0:T(8,128)(2,1)S(1)}, u32[]{:S(2)}, u32[]{:S(2)}) collective-permute-start(bf16[2,64,1024]{2,1,0:T(8,128)(2,1)S(1)} %get-tuple-element.68), channel_id=1, source_target_pairs={{0,16},{4,20},{8,24},{12,28},{16,0},{20,4},{24,8},{28,12},{1,17},{... | collective-permute-start | bytes 786440 | tf_op jit(solution)/shard_map/ppermute | solution.py:261
  99.2 24.7 %collective-permute-start.36 = (bf16[2,64,512]{2,1,0:T(8,128)(2,1)}, bf16[2,64,512]{2,1,0:T(8,128)(2,1)S(1)}, u32[]{:S(2)}, u32[]{:S(2)}) collective-permute-start(bf16[2,64,512]{2,1,0:T(8,128)(2,1)} %get-tuple-element.43), channel_id=1, source_target_pairs={{0,8},{4,12},{8,0},{12,4},{16,24},{20,28},{24,16},{28,20},{1,9},{5... | collective-permute-start | bytes 393224 | tf_op jit(solution)/shard_map/ppermute | solution.py:261
  100.7 24.9 %collective-permute-start.38 = (bf16[2,64,512]{2,1,0:T(8,128)(2,1)}, bf16[2,64,512]{2,1,0:T(8,128)(2,1)S(1)}, u32[]{:S(2)}, u32[]{:S(2)}) collective-permute-start(bf16[2,64,512]{2,1,0:T(8,128)(2,1)} %get-tuple-element.45), channel_id=1, source_target_pairs={{0,16},{4,20},{8,24},{12,28},{16,0},{20,4},{24,8},{28,12},{1,17},{... | collective-permute-start | bytes 393224 | tf_op jit(solution)/shard_map/ppermute | solution.py:261
  106.1 20.2 %collective-permute-start.29 = (bf16[2,64,512]{2,1,0:T(8,128)(2,1)}, bf16[2,64,512]{2,1,0:T(8,128)(2,1)S(1)}, u32[]{:S(2)}, u32[]{:S(2)}) collective-permute-start(bf16[2,64,512]{2,1,0:T(8,128)(2,1)} %get-tuple-element.36), channel_id=1, source_target_pairs={{0,8},{4,12},{8,0},{12,4},{16,24},{20,28},{24,16},{28,20},{1,9},{5... | collective-permute-start | bytes 393224 | tf_op jit(solution)/shard_map/ppermute | solution.py:261
  106.6 20.3 %collective-permute-start.31 = (bf16[2,64,512]{2,1,0:T(8,128)(2,1)}, bf16[2,64,512]{2,1,0:T(8,128)(2,1)S(1)}, u32[]{:S(2)}, u32[]{:S(2)}) collective-permute-start(bf16[2,64,512]{2,1,0:T(8,128)(2,1)} %get-tuple-element.38), channel_id=1, source_target_pairs={{0,16},{4,20},{8,24},{12,28},{16,0},{20,4},{24,8},{28,12},{1,17},{... | collective-permute-start | bytes 393224 | tf_op jit(solution)/shard_map/ppermute | solution.py:261
  111.0 16.1 %collective-permute-start.25 = (bf16[2,64,512]{2,1,0:T(8,128)(2,1)}, bf16[2,64,512]{2,1,0:T(8,128)(2,1)S(1)}, u32[]{:S(2)}, u32[]{:S(2)}) collective-permute-start(bf16[2,64,512]{2,1,0:T(8,128)(2,1)} %get-tuple-element.32), channel_id=1, source_target_pairs={{0,8},{4,12},{8,0},{12,4},{16,24},{20,28},{24,16},{28,20},{1,9},{5... | collective-permute-start | bytes 393224 | tf_op jit(solution)/shard_map/ppermute | solution.py:261
  124.0 5.0 %collective-permute-start.27 = (bf16[2,64,512]{2,1,0:T(8,128)(2,1)S(1)}, bf16[2,64,512]{2,1,0:T(8,128)(2,1)S(1)}, u32[]{:S(2)}, u32[]{:S(2)}) collective-permute-start(bf16[2,64,512]{2,1,0:T(8,128)(2,1)S(1)} %copy-done.15), channel_id=1, source_target_pairs={{0,16},{4,20},{8,24},{12,28},{16,0},{20,4},{24,8},{28,12},{1,17},{... | collective-permute-start | bytes 393224 | tf_op jit(solution)/shard_map/ppermute | solution.py:261
  125.6 5.0 %collective-permute-start.41 = (bf16[2,64,512]{2,1,0:T(8,128)(2,1)S(1)}, bf16[2,64,512]{2,1,0:T(8,128)(2,1)S(1)}, u32[]{:S(2)}, u32[]{:S(2)}) collective-permute-start(bf16[2,64,512]{2,1,0:T(8,128)(2,1)S(1)} %copy-done.14), channel_id=1, source_target_pairs={{0,16},{4,20},{8,24},{12,28},{16,0},{20,4},{24,8},{28,12},{1,17},{... | collective-permute-start | bytes 393224 | tf_op jit(solution)/shard_map/ppermute | solution.py:261
  126.3 5.7 %collective-permute-start.33 = (bf16[2,64,640]{2,1,0:T(8,128)(2,1)S(1)}, bf16[2,64,640]{2,1,0:T(8,128)(2,1)S(1)}, u32[]{:S(2)}, u32[]{:S(2)}) collective-permute-start(bf16[2,64,640]{2,1,0:T(8,128)(2,1)S(1)} %copy-done.13), channel_id=1, source_target_pairs={{0,8},{4,12},{8,0},{12,4},{16,24},{20,28},{24,16},{28,20},{1,9},{5... | collective-permute-start | bytes 491528 | tf_op jit(solution)/shard_map/ppermute | solution.py:261
  127.0 45.1 %collective-permute-start.44 = (bf16[4096,256]{1,0:T(8,128)(2,1)}, bf16[4096,256]{1,0:T(8,128)(2,1)S(1)}, u32[]{:S(2)}, u32[]{:S(2)}) collective-permute-start(bf16[4096,256]{1,0:T(8,128)(2,1)} %get-tuple-element.49), channel_id=1, source_target_pairs={{0,4},{4,0},{8,12},{12,8},{16,20},{20,16},{24,28},{28,24},{1,5},{5... | collective-permute-start | bytes 6291464 | tf_op jit(solution)/shard_map/ppermute | solution.py:261
  127.1 45.0 %collective-permute-start.45 = (bf16[4096,256]{1,0:T(8,128)(2,1)}, bf16[4096,256]{1,0:T(8,128)(2,1)}, u32[]{:S(2)}, u32[]{:S(2)}) collective-permute-start(bf16[4096,256]{1,0:T(8,128)(2,1)} %get-tuple-element.50), channel_id=1, source_target_pairs={{0,4},{4,0},{8,12},{12,8},{16,20},{20,16},{24,28},{28,24},{1,5},{5... | collective-permute-start | bytes 6291464 | tf_op jit(solution)/shard_map/ppermute | solution.py:261
  129.0 43.1 %collective-permute-start.46 = (bf16[256,4096]{1,0:T(8,128)(2,1)}, bf16[256,4096]{1,0:T(8,128)(2,1)}, u32[]{:S(2)}, u32[]{:S(2)}) collective-permute-start(bf16[256,4096]{1,0:T(8,128)(2,1)} %get-tuple-element.51), channel_id=1, source_target_pairs={{0,4},{4,0},{8,12},{12,8},{16,20},{20,16},{24,28},{28,24},{1,5},{5... | collective-permute-start | bytes 6291464 | tf_op jit(solution)/shard_map/ppermute | solution.py:261
  130.7 10.9 %collective-permute-start.37 = (bf16[64,512]{1,0:T(8,128)(2,1)S(1)}, bf16[64,512]{1,0:T(8,128)(2,1)S(1)}, u32[]{:S(2)}, u32[]{:S(2)}) collective-permute-start(bf16[64,512]{1,0:T(8,128)(2,1)S(1)} %fusion.23), channel_id=1, source_target_pairs={{0,16},{4,20},{8,24},{12,28},{16,0},{20,4},{24,8},{28,12},{1,17},{... | collective-permute-start | bytes 196616 | tf_op jit(solution)/shard_map/ppermute | solution.py:261
  132.0 4.3 %collective-permute-start.26 = (bf16[64,512]{1,0:T(8,128)(2,1)S(1)}, bf16[64,512]{1,0:T(8,128)(2,1)S(1)}, u32[]{:S(2)}, u32[]{:S(2)}) collective-permute-start(bf16[64,512]{1,0:T(8,128)(2,1)S(1)} %fusion.19), channel_id=1, source_target_pairs={{0,16},{4,20},{8,24},{12,28},{16,0},{20,4},{24,8},{28,12},{1,17},{... | collective-permute-start | bytes 196616 | tf_op jit(solution)/shard_map/ppermute | solution.py:261
  133.4 36.3 %copy-start.12 = (s32[64,4]{0,1:T(4,128)S(1)}, s32[64,4]{0,1:T(4,128)}, u32[]{:S(2)}) copy-start(s32[64,4]{0,1:T(4,128)} %param.11) | copy-start | bytes 3076
  136.3 4.7 %collective-permute-start.28 = (bf16[64,512]{1,0:T(8,128)(2,1)S(1)}, bf16[64,512]{1,0:T(8,128)(2,1)S(1)}, u32[]{:S(2)}, u32[]{:S(2)}) collective-permute-start(bf16[64,512]{1,0:T(8,128)(2,1)S(1)} %fusion.20), channel_id=1, source_target_pairs={{0,8},{4,12},{8,0},{12,4},{16,24},{20,28},{24,16},{28,20},{1,9},{5... | collective-permute-start | bytes 196616 | tf_op jit(solution)/shard_map/ppermute | solution.py:261
  141.0 4.8 %collective-permute-start.39 = (bf16[64,512]{1,0:T(8,128)(2,1)S(1)}, bf16[64,512]{1,0:T(8,128)(2,1)S(1)}, u32[]{:S(2)}, u32[]{:S(2)}) collective-permute-start(bf16[64,512]{1,0:T(8,128)(2,1)S(1)} %fusion.24), channel_id=1, source_target_pairs={{0,8},{4,12},{8,0},{12,4},{16,24},{20,28},{24,16},{28,20},{1,9},{5... | collective-permute-start | bytes 196616 | tf_op jit(solution)/shard_map/ppermute | solution.py:261
  141.6 4.6 %collective-permute-start.30 = (bf16[64,512]{1,0:T(8,128)(2,1)S(1)}, bf16[64,512]{1,0:T(8,128)(2,1)S(1)}, u32[]{:S(2)}, u32[]{:S(2)}) collective-permute-start(bf16[64,512]{1,0:T(8,128)(2,1)S(1)} %fusion.21), channel_id=1, source_target_pairs={{0,16},{4,20},{8,24},{12,28},{16,0},{20,4},{24,8},{28,12},{1,17},{... | collective-permute-start | bytes 196616 | tf_op jit(solution)/shard_map/ppermute | solution.py:261
  145.8 13.8 %collective-permute-start.32 = (bf16[64,512]{1,0:T(8,128)(2,1)S(1)}, bf16[64,512]{1,0:T(8,128)(2,1)S(1)}, u32[]{:S(2)}, u32[]{:S(2)}) collective-permute-start(bf16[64,512]{1,0:T(8,128)(2,1)S(1)} %fusion.22), channel_id=1, source_target_pairs={{0,8},{4,12},{8,0},{12,4},{16,24},{20,28},{24,16},{28,20},{1,9},{5... | collective-permute-start | bytes 196616 | tf_op jit(solution)/shard_map/ppermute | solution.py:261
  146.2 4.6 %collective-permute-start.42 = (bf16[64,512]{1,0:T(8,128)(2,1)S(1)}, bf16[64,512]{1,0:T(8,128)(2,1)S(1)}, u32[]{:S(2)}, u32[]{:S(2)}) collective-permute-start(bf16[64,512]{1,0:T(8,128)(2,1)S(1)} %fusion.25), channel_id=1, source_target_pairs={{0,8},{4,12},{8,0},{12,4},{16,24},{20,28},{24,16},{28,20},{1,9},{5... | collective-permute-start | bytes 196616 | tf_op jit(solution)/shard_map/ppermute | solution.py:261
  150.8 4.4 %collective-permute-start.34 = (bf16[64,640]{1,0:T(8,128)(2,1)S(1)}, bf16[64,640]{1,0:T(8,128)(2,1)S(1)}, u32[]{:S(2)}, u32[]{:S(2)}) collective-permute-start(bf16[64,640]{1,0:T(8,128)(2,1)S(1)} %fusion.17), channel_id=1, source_target_pairs={{0,16},{4,20},{8,24},{12,28},{16,0},{20,4},{24,8},{28,12},{1,17},{... | collective-permute-start | bytes 245768 | tf_op jit(solution)/shard_map/ppermute | solution.py:261
  155.5 8.1 %collective-permute-start.43 = (bf16[64,1152]{1,0:T(8,128)(2,1)S(1)}, bf16[64,1152]{1,0:T(8,128)(2,1)}, u32[]{:S(2)}, u32[]{:S(2)}) collective-permute-start(bf16[64,1152]{1,0:T(8,128)(2,1)S(1)} %concatenate.37), channel_id=1, source_target_pairs={{0,3},{1,2},{2,1},{3,0},{4,7},{5,6},{6,5},{7,4},{8,11},{9,10},{10,... | collective-permute-start | bytes 442376 | tf_op jit(solution)/shard_map/ppermute | solution.py:270
  159.7 7.3 %collective-permute-start.35 = (bf16[64,1152]{1,0:T(8,128)(2,1)S(1)}, bf16[64,1152]{1,0:T(8,128)(2,1)}, u32[]{:S(2)}, u32[]{:S(2)}) collective-permute-start(bf16[64,1152]{1,0:T(8,128)(2,1)S(1)} %concatenate.35), channel_id=1, source_target_pairs={{0,1},{1,0},{2,3},{3,2},{4,5},{5,4},{6,7},{7,6},{8,9},{9,8},{10,11... | collective-permute-start | bytes 442376 | tf_op jit(solution)/shard_map/ppermute | solution.py:270
  163.6 6.0 %collective-permute-start.40 = (bf16[64,1152]{1,0:T(8,128)(2,1)S(1)}, bf16[64,1152]{1,0:T(8,128)(2,1)S(1)}, u32[]{:S(2)}, u32[]{:S(2)}) collective-permute-start(bf16[64,1152]{1,0:T(8,128)(2,1)S(1)} %concatenate.36), channel_id=1, source_target_pairs={{0,2},{1,3},{2,0},{3,1},{4,6},{5,7},{6,4},{7,5},{8,10},{9,11},{10,... | collective-permute-start | bytes 442376 | tf_op jit(solution)/shard_map/ppermute | solution.py:270
  (15 other events, 88.2 us)

commit v2 on v1

v2 whole, which is shorter than its diff:
```python
import functools
import math

import jax
import jax.numpy as jnp
from jax import lax
from jax.experimental import pallas as pl
from jax.experimental.pallas import tpu as pltpu
from jax.sharding import PartitionSpec as P

BF = jnp.bfloat16
F32 = jnp.float32
LANES = 128
MIB = 1024 * 1024


def whole_block(shape):
    zeros = (0,) * len(shape)
    return pl.BlockSpec(shape, lambda *_: zeros, pipeline_mode=pl.Buffered(1))


def dot(a, b, a_dim, b_dim):
    return lax.dot_general(a, b, (((a_dim,), (b_dim,)), ((), ())), preferred_element_type=F32)


def after(value, *first):
    return lax.optimization_barrier((value, *first))[0]


def params(need):
    return pltpu.CompilerParams(vmem_limit_bytes=min(need + 12 * MIB, 58 * MIB))


def add_slice(x, dy, weights, before):
    values = []
    for number, weight in enumerate(weights):
        from_dy = number % 3 == 2
        part = dot(dy if from_dy else x, weight[...], 1, 1 if from_dy else 0)
        values.append(part if before is None else part + before[number])
    return values


def forward_kernel(first, place, x_ref, dy_ref, *refs):
    weights, refs = refs[:6], refs[6:]
    values = add_slice(x_ref[...], dy_ref[...], weights, None if first else refs[0])
    for number in range(6):
        refs[-1][number] = values[number]


def rest_kernel(n_expert, slots, place, *refs):
    sources, refs = refs[: 2 * slots], refs[2 * slots :]
    weights, before, route_w = refs[:6], refs[6], refs[7]
    mine, other, route, held = refs[8:]
    units = weights[0].shape[1]
    step = pl.program_id(0)

    for at in range(slots - 1):

        @pl.when(step == at)
        def _(at=at):
            x, dy = sources[2 * at][...], sources[2 * at + 1][...]
            values = add_slice(x, dy, weights, held if at else before)
            for number in range(6):
                held[number] = values[number]

    @pl.when(step == slots - 1)
    def _():
        values = add_slice(sources[-2][...], sources[-1][...], weights, held)
        lane = lax.broadcasted_iota(jnp.int32, route.shape, 1)
        total = jnp.zeros(route.shape, F32)
        for j, acts in enumerate((mine, other)):
            expert = jnp.bitwise_xor(place[1], j)
            gate_pre, up_pre, back = values[3 * j : 3 * j + 3]
            weight = jnp.sum(
                jnp.where(lane == expert, route_w[...].astype(F32), 0.0), axis=1, keepdims=True
            )
            logistic = jax.nn.sigmoid(gate_pre)
            active = gate_pre * logistic
            hidden = active * up_pre
            route_part = jnp.sum(back * hidden, axis=1, keepdims=True)
            high = route_part.astype(BF).astype(F32)
            total = total + jnp.where(lane == expert, high, 0.0)
            total = total + jnp.where(lane == expert + n_expert, route_part - high, 0.0)
            scaled = weight * back
            acts[:, :units] = (
                scaled * up_pre * logistic * (1.0 + gate_pre * (1.0 - logistic))
            ).astype(BF)
            acts[:, units : 2 * units] = (scaled * active).astype(BF)
            acts[:, 2 * units :] = (weight * hidden).astype(BF)
        route[...] = total.astype(BF)


def column_block(rows, width, column):
    return pl.BlockSpec(
        (rows, width), lambda i, p: (0, column), pipeline_mode=pl.Buffered(1)
    )


def forward_cost(rows, width, units, slots):
    return pl.CostEstimate(
        flops=12 * rows * width * units * slots,
        bytes_accessed=2 * width * (2 * rows + 6 * units) * slots + 24 * rows * units,
        transcendentals=2 * rows * units,
    )


def forward_slice(place, slot, pair, weights, before, width):
    rows = pair.shape[0]
    units = weights[0].shape[1]
    wide = pl.BlockSpec((width, units), lambda i, p: (p[0] ^ slot, 0))
    tall = pl.BlockSpec((units, width), lambda i, p: (0, p[0] ^ slot))
    specs = [column_block(rows, width, column) for column in range(2)] + [wide, wide, tall] * 2
    extra = [] if before is None else [before]
    return pl.pallas_call(
        functools.partial(forward_kernel, before is None),
        grid_spec=pltpu.PrefetchScalarGridSpec(
            num_scalar_prefetch=1,
            grid=(1,),
            in_specs=specs + [whole_block(e.shape) for e in extra],
            out_specs=whole_block((6, rows, units)),
        ),
        out_shape=jax.ShapeDtypeStruct((6, rows, units), F32),
        compiler_params=params(58 * MIB),
        cost_estimate=forward_cost(rows, width, units, 1),
        name="forward_slice",
    )(place, pair, pair, *weights, *extra)


def forward_rest(place, pairs, weights, before, route_w, n_expert, width, done):
    rows = pairs[0].shape[0]
    units = weights[0].shape[1]
    slots = len(pairs)
    wide = pl.BlockSpec((width, units), lambda i, p: (p[0] ^ (i + done), 0))
    tall = pl.BlockSpec((units, width), lambda i, p: (0, p[0] ^ (i + done)))
    return pl.pallas_call(
        functools.partial(rest_kernel, n_expert, slots),
        grid_spec=pltpu.PrefetchScalarGridSpec(
            num_scalar_prefetch=1,
            grid=(slots,),
            in_specs=[column_block(rows, width, column) for column in range(2)] * slots
            + [wide, wide, tall] * 2
            + [whole_block(before.shape), column_block(rows, LANES, 2 * width // LANES)],
            out_specs=[
                whole_block((rows, 3 * units)),
                whole_block((rows, 3 * units)),
                whole_block((rows, LANES)),
            ],
            scratch_shapes=[pltpu.VMEM((6, rows, units), F32)],
        ),
        out_shape=[
            jax.ShapeDtypeStruct((rows, 3 * units), BF),
            jax.ShapeDtypeStruct((rows, 3 * units), BF),
            jax.ShapeDtypeStruct((rows, LANES), BF),
        ],
        compiler_params=params(
            4 * rows * width * slots + 24 * width * units + 120 * rows * units
        ),
        cost_estimate=forward_cost(rows, width, units, slots),
        name="forward_rest",
    )(place, *[p for pair in pairs for p in (pair, pair)], *weights, before, route_w)


def unit_kernel(tokens, with_route, place, mine, other, *refs):
    if with_route:
        route, refs = refs[0], refs[1:]
    weights, outs = refs[:4], refs[4:]
    width, units = weights[0].shape
    total = None
    for number, weight in enumerate(weights):
        acts = mine if number < 2 else other
        at = (number % 2) * units
        part = dot(acts[:, at : at + units], weight[...], 1, 1)
        total = part if total is None else total + part
    for block, out in enumerate(outs):
        at = block * tokens
        out[:, :width] = total[at : at + tokens].astype(out.dtype)
        if with_route:
            out[:, width:] = route[at : at + tokens, :].astype(out.dtype)


def unit_product(place, mine, other, weights, slot, tokens, width, route=None):
    rows = mine.shape[0]
    units = weights[0].shape[1]
    wide = pl.BlockSpec((width, units), lambda i, p: (p[0] ^ slot, 0))
    acts = column_block(rows, 2 * units, 0)
    columns = width + (0 if route is None else LANES)
    shapes = [
        jax.ShapeDtypeStruct((tokens, columns), F32 if block == 0 else BF)
        for block in range(rows // tokens)
    ]
    extra = [] if route is None else [route]
    return pl.pallas_call(
        functools.partial(unit_kernel, tokens, route is not None),
        grid_spec=pltpu.PrefetchScalarGridSpec(
            num_scalar_prefetch=1,
            grid=(1,),
            in_specs=[acts, acts] + [whole_block(r.shape) for r in extra] + [wide] * 4,
            out_specs=[whole_block(s.shape) for s in shapes],
        ),
        out_shape=shapes,
        compiler_params=params(16 * width * units + 16 * rows * units + 12 * rows * width),
        cost_estimate=pl.CostEstimate(
            flops=8 * rows * width * units,
            bytes_accessed=8 * width * units + 2 * rows * (4 * units + 3 * width // 2),
            transcendentals=0,
        ),
        name="unit_product",
    )(place, mine, other, *extra, *weights)


def outer_kernel(pieces, rows, down, place, acts, got, *refs):
    n_slice = len(pieces) // 2
    sources, refs = refs[: 2 * n_slice], refs[2 * n_slice :]
    if down:
        down_w, fisher, anchor, out = refs[:4]
    else:
        gate_out, up_out = refs[:2]
    held, grads, sems = refs[-3:]
    width = held.shape[2]
    units = acts.shape[1] // 3
    step = pl.program_id(0)

    def copies(slot):
        return [
            pltpu.make_async_copy(
                sources[side * n_slice + slot].at[
                    :, pl.ds(pieces[side * n_slice + slot] * width, width)
                ],
                held.at[slot, pl.ds(side * rows, rows)],
                sems.at[slot, side],
            )
            for side in range(2)
        ]

    @pl.when(step == 0)
    def _():
        for slot in range(n_slice):
            for copy in copies(slot):
                copy.start()
        grads[:rows] = acts[...]
        grads[rows:] = got[...]

    for slot in range(n_slice):

        @pl.when(step == slot)
        def _(slot=slot):
            for copy in copies(slot):
                copy.wait()

    block = held[step]
    if down:
        value = dot(grads[:, 2 * units :], block, 0, 0)
        value = value + fisher[...] * (down_w[...].astype(F32) - anchor[...])
        out[...] = value.astype(BF)
    else:
        value = dot(block, grads[:, : 2 * units], 0, 0)
        gate_out[...] = value[:, :units].astype(BF)
        up_out[...] = value[:, units:].astype(BF)


def outer_products(place, pieces, acts, got, width, penalty=()):
    n_slice = len(pieces) // 2
    rows = acts.shape[0]
    units = acts.shape[1] // 3
    full = n_slice * width
    down = bool(penalty)
    wide = pl.BlockSpec((width, units), lambda s, p: (p[0] ^ s, 0))
    tall = pl.BlockSpec((units, width), lambda s, p: (0, p[0] ^ s))
    anywhere = pl.BlockSpec(memory_space=pl.ANY)
    return pl.pallas_call(
        functools.partial(outer_kernel, tuple(p[1] for p in pieces), rows, down),
        grid_spec=pltpu.PrefetchScalarGridSpec(
            num_scalar_prefetch=1,
            grid=(n_slice,),
            in_specs=[whole_block(acts.shape), whole_block(got.shape)]
            + [anywhere] * (2 * n_slice)
            + [tall] * len(penalty),
            out_specs=[tall] if down else [wide, wide],
            scratch_shapes=[
                pltpu.VMEM((n_slice, 2 * rows, width), BF),
                pltpu.VMEM((2 * rows, 3 * units), BF),
                pltpu.SemaphoreType.DMA((n_slice, 2)),
            ],
        ),
        out_shape=[jax.ShapeDtypeStruct((units, full), BF)]
        if down
        else [jax.ShapeDtypeStruct((full, units), BF)] * 2,
        compiler_params=params(58 * MIB),
        cost_estimate=pl.CostEstimate(
            flops=4 * rows * full * units * (1 if down else 2),
            bytes_accessed=full * (4 * rows + units * (12 if down else 4)),
            transcendentals=0,
        ),
        name="outer_down" if down else "outer_gate_up",
    )(place, acts, got, *[p[0] for p in pieces], *penalty)


def repack(tail, count):
    lane = lax.broadcasted_iota(jnp.int32, tail.shape, 1)
    value = tail + pltpu.roll(tail, LANES - count, 1)
    high = value.astype(BF).astype(F32)
    low = pltpu.roll(value - high, count, 1)
    return jnp.where(lane < count, high, jnp.where(lane < 2 * count, low, 0.0))


def call_small(kernel, name, shapes, *args):
    size = sum(4 * math.prod(a.shape) for a in args) + sum(4 * math.prod(s.shape) for s in shapes)
    return pl.pallas_call(
        kernel,
        grid=(1,),
        in_specs=[whole_block(a.shape) for a in args],
        out_specs=[whole_block(s.shape) for s in shapes],
        out_shape=shapes,
        compiler_params=params(2 * size),
        cost_estimate=pl.CostEstimate(flops=size, bytes_accessed=size, transcendentals=0),
        name=name,
    )(*args)


def slice_sum_kernel(n_got, n_expert, width, own, *refs):
    gots, rest = refs[:n_got], refs[n_got:]
    value = own[...]
    for got in gots:
        value = value + got[...].astype(F32)
    if value.shape[1] > width:
        send, pair_out = rest
        pair = repack(value[:, width:], n_expert).astype(BF)
        pair_out[...] = pair
    else:
        pair_in, send = rest
        pair = pair_in[...]
    send[:, :width] = value[:, :width].astype(BF)
    send[:, width:] = pair


def slice_sum(own, gots, pair, n_expert, width):
    tokens = own.shape[0]
    shapes = [jax.ShapeDtypeStruct((tokens, width + LANES), BF)]
    if pair is None:
        shapes.append(jax.ShapeDtypeStruct((tokens, LANES), BF))
    kernel = functools.partial(slice_sum_kernel, len(gots), n_expert, width)
    extra = [] if pair is None else [pair]
    out = call_small(kernel, "slice_sum", shapes, own, *gots, *extra)
    return out[0], (out[1] if pair is None else pair)


def final_sum_kernel(n_got, n_far, n_expert, own, pair, ids, *refs):
    gots, fars, (grad, route) = refs[:n_got], refs[n_got : n_got + n_far], refs[n_got + n_far :]
    width = own.shape[1]
    value, tail = own[...], pair[...].astype(F32)
    for got in gots:
        value = value + got[...].astype(F32)
    for far in fars:
        value = value + far[:, :width].astype(F32)
        tail = tail + far[:, width:].astype(F32)
    grad[...] = value.astype(BF)
    tail = tail + pltpu.roll(tail, LANES - n_expert, 1)
    lane = lax.broadcasted_iota(jnp.int32, tail.shape, 1)
    for k in range(route.shape[1]):
        chosen = jnp.logical_and(lane == ids[:, k : k + 1], lane < n_expert)
        route[:, k : k + 1] = jnp.sum(jnp.where(chosen, tail, 0.0), axis=1, keepdims=True)


def final_sum(own, gots, fars, pair, ids, n_expert):
    shapes = [jax.ShapeDtypeStruct(own.shape, BF), jax.ShapeDtypeStruct(ids.shape, F32)]
    kernel = functools.partial(final_sum_kernel, len(gots), len(fars), n_expert)
    return call_small(kernel, "final_sum", shapes, own, pair, ids, *gots, *fars)


def per_device(
    n_expert,
    n_slice,
    tokens,
    cotangent,
    route_ids,
    route_weights,
    gate_weight,
    up_weight,
    down_weight,
    fisher,
    anchor,
):
    count, width = tokens.shape
    chips = n_expert // 2
    rows = chips * count
    lo = 1 << ((chips.bit_length() - 1) // 2)
    hi = chips // lo
    own_e, own_f = lax.axis_index("expert"), lax.axis_index("ffn")
    place = jnp.stack([own_f, own_e]).astype(jnp.int32)

    def over_expert(value, mask):
        return lax.ppermute(value, "expert", [(i, i ^ mask) for i in range(n_expert)])

    def over_lo(value, mask):
        return over_expert(value, 2 * mask)

    def over_hi(value, mask):
        return over_expert(value, 2 * lo * mask)

    def over_slice(value, mask):
        return lax.ppermute(value, "ffn", [(i, i ^ mask) for i in range(n_slice)])

    def collect(value, send, number, axis):
        return jnp.stack([value] + [send(value, m) for m in range(1, number)], axis=axis)

    named = route_ids[:, :, None] == jnp.arange(LANES, dtype=jnp.int32)[None, None, :]
    route_row = jnp.sum(
        jnp.where(named, route_weights.astype(F32)[:, :, None], 0.0), axis=1
    ).astype(BF)

    both = jnp.concatenate([tokens, cotangent], axis=1)
    parts = [both] + [over_slice(both, s) for s in range(1, n_slice)]
    parts[1] = jnp.concatenate([parts[1], route_row], axis=1)
    hops = [[both] + [over_expert(both, 2 * m) for m in range(1, chips)]]
    part = after(parts[1], *hops[0][1:])
    hops.append([part] + [over_expert(part, 2 * m) for m in range(1, chips)])
    mine = (gate_weight[0], up_weight[0], down_weight[0])
    weights = mine + tuple(over_expert(after(w, parts[2]), 1) for w in mine)
    rest = []
    for s in range(2, n_slice):
        value = after(parts[s], *hops[1][1:])
        rest.append(collect(value, over_lo, lo, 0) if s % 2 == 0 else collect(value, over_hi, hi, 0))
    near = [jnp.stack(h).reshape(rows, -1) for h in hops]
    acc = forward_slice(place, 0, near[0], weights, None, width)
    acc = forward_slice(place, 1, near[1], weights, acc, width)
    got_near = tuple(over_expert(v, 1) for v in near)
    for at, value in enumerate(rest):
        send, number, axis = (over_hi, hi, 0) if at % 2 == 0 else (over_lo, lo, 1)
        got = [send(value, m) for m in range(1, number)]
        value = after(value, acc, *got_near)
        rest[at] = jnp.stack([value] + got, axis=axis).reshape(rows, -1)
    acts, acts_other, route = forward_rest(
        place, rest, weights, acc, near[1], n_expert, width, 2
    )

    got_acts = over_expert(acts_other, 1)
    got_rest = tuple(over_expert(v, 1) for v in rest)
    pieces = [
        [(v, which) for v in (*near, *rest, *got_near, *got_rest)] for which in range(2)
    ]
    ready = after(place, *got_rest)

    projections = (weights[0], weights[1], weights[3], weights[4])
    order = list(reversed(range(n_slice)))
    parts, fars, pair, late = [], [], None, ready
    for at, s in enumerate(order):
        if at == 1:
            late = after(late, got_acts)
        outs = unit_product(
            late, acts, acts_other, projections, s, count, width, route if at == 0 else None
        )
        parts.append(
            (outs[0], [over_expert(v, 2 * (block + 1)) for block, v in enumerate(outs[1:])])
        )
        if at == n_slice - 2:
            send, pair = slice_sum(*parts[0], None, n_expert, width)
            fars.append(over_slice(send, order[0]))
            late = after(late, send)
    for at, s in enumerate(order[:-1]):
        if at > 0:
            own, got = parts[at]
            if at > 1 and at == n_slice - 2:
                own = after(own, grad_gate)
            send, pair = slice_sum(own, got, pair, n_expert, width)
            fars.append(over_slice(send, s))
        if at == n_slice - 3:
            late = after(place, send)
            grad_gate, grad_up = outer_products(late, pieces[0], acts, got_acts, width)
    late = after(place, send, grad_gate)
    (grad_down,) = outer_products(
        late, pieces[1], acts, got_acts, width, (mine[2], fisher[0], anchor[0])
    )
    own = after(parts[-1][0], grad_down)
    grad_tokens, grad_route = final_sum(own, parts[-1][1], fars, pair, route_ids, n_expert)
    return (grad_tokens, grad_route, grad_gate[None], grad_up[None], grad_down[None])


def solution(mesh):
    return jax.shard_map(
        functools.partial(per_device, mesh.shape["expert"], mesh.shape["ffn"]),
        mesh=mesh,
        in_specs=(
            P("expert", "ffn"),
            P("expert", "ffn"),
            P("expert", None),
            P("expert", None),
            P("expert", None, "ffn"),
            P("expert", None, "ffn"),
            P("expert", "ffn", None),
            P("expert", "ffn", None),
            P("expert", "ffn", None),
        ),
        out_specs=(
            P("expert", "ffn"),
            P("expert", None),
            P("expert", None, "ffn"),
            P("expert", None, "ffn"),
            P("expert", "ffn", None),
        ),
        check_vma=False,
    )
```

time: 186 us -> 124 us (0.67)
  waiting for transfers between devices: 57.3 us -> 25.5 us
  starting transfers between devices: 60.4 us -> 42.5 us
  local copies, waits for them, and re-layouts: 8.63 us -> 4.51 us
  other arithmetic: 12.4 us -> 8.33 us
  Pallas kernels: 45.6 us -> 42.1 us
    ppermute x38 -> x30, waiting for transfers between devices: 46.1 us -> 11.1 us  [over_expert(): lax.ppermute(value, 'expert', [(i, i ^ mask) for i in range(n_expert)])]
    ppermute x38 -> x30, starting transfers between devices: 38.4 us -> 27 us  [over_expert(): lax.ppermute(value, 'expert', [(i, i ^ mask) for i in range(n_expert)])]
    ppermute x9 -> x6, starting transfers between devices: 22.1 us -> 15.5 us  [over_slice(): return lax.ppermute(value, 'ffn', [(i, i ^ mask) for i in range(n_slice)])]
    another operation x7 -> x4, other arithmetic: 0.26 us -> 4.53 us  [the longest x2 3.25 us: per_device(): rest[at] = jnp.stack([value] + got, axis=axis).reshape(rows, -1)]
    another operation x17 -> x2, other arithmetic: 5.83 us -> 1.71 us  [collect(): jnp.stack([value] + [send(value, m) for m in range(1, number)], axis=axis)]
    pallas_call x7 -> x13, Pallas kernels: 45.6 us -> 42.1 us  [the longest x2 16.3 us: outer_products(): pl.pallas_call(functools.partial(outer_kernel, tuple((p[1] for p in piece...]
    convert_element_type x4 -> x0, other arithmetic: 3.13 us -> none  [the longest x1 1.68 us: per_device(): grad_tokens = total.astype(BF)]
    ppermute x9 -> x6, waiting for transfers between devices: 11.2 us -> 14.3 us  [over_slice(): return lax.ppermute(value, 'ffn', [(i, i ^ mask) for i in range(n_slice)])]
  transfers between devices with their start and end apart: 47 -> 36, of which waited for: 23 -> 9; matrix products, arithmetic and copies ran while one was open for 9% -> 5% of each run, Pallas kernels for 10% -> 33%
where the time goes in v2:
time: 124 us
  starting transfers between devices  42.5 us (34%)
  Pallas kernels  42.1 us (34%)
  waiting for transfers between devices  25.5 us (21%)
  other arithmetic  8.33 us (7%)
  local copies, waits for them, and re-layouts  4.51 us (4%)
    ppermute x30, starting transfers between devices, over_expert(): lax.ppermute(value, 'expert', [(i, i ^ mask) for i in range(n_expert)])  27 us
    pallas_call x2, Pallas kernels, outer_products(): pl.pallas_call(functools.partial(outer_kernel, tuple((p[1] for p in piece...  16.3 us
    ppermute x6, starting transfers between devices, over_slice(): return lax.ppermute(value, 'ffn', [(i, i ^ mask) for i in range(n_slice)])  15.5 us
    ppermute x6, waiting for transfers between devices, over_slice(): return lax.ppermute(value, 'ffn', [(i, i ^ mask) for i in range(n_slice)])  14.3 us
    ppermute x30, waiting for transfers between devices, over_expert(): lax.ppermute(value, 'expert', [(i, i ^ mask) for i in range(n_expert)])  11.1 us
    pallas_call x2, Pallas kernels, forward_slice(): pl.pallas_call(functools.partial(forward_kernel, before is None), grid_sp...  10.7 us
    pallas_call x4, Pallas kernels, unit_product(): pl.pallas_call(functools.partial(unit_kernel, tokens, route is not None),...  9.55 us
    pallas_call x1, Pallas kernels, forward_rest(): pl.pallas_call(functools.partial(rest_kernel, n_expert, slots), grid_spec...  4.14 us
  transfers between devices with their start and end apart: 36, of which 9 were waited for; matrix products, arithmetic and copies ran while one was open for 5% of the time, Pallas kernels for 33%

profile of v2, /device:TPU:0, one launch (start us, length us, event | category | flops | bytes accessed | tf_op | source)
XLA Modules:
  0.0 123.9 jit_solution(14485181736995022725)
XLA Ops:
  0.6 0.9 constant_dynamic-update-slice_fusion.1
  1.5 0.9 constant_dynamic-update-slice_fusion
  2.5 4.1 %collective-permute-start = (bf16[64,2048]{1,0:T(8,128)(2,1)S(1)}, bf16[64,2048]{1,0:T(8,128)(2,1)S(1)}, u32[]{:S(2)}, u32[]{:S(2)}) collective-permute-start(bf16[64,2048]{1,0:T(8,128)(2,1)S(1)} %constant_dynamic-update-slice_fusion), channel_id=1, source_target_pairs={{0,2},{1,3},{2,0},{3,1},{4,6},{5,7},{6,4},{7,5},{8,10},{9,11},{10,... | collective-permute-start | bytes 786440 | tf_op jit(solution)/shard_map/ppermute | solution.py:401
  6.6 2.4 %collective-permute-start.4 = (bf16[64,2048]{1,0:T(8,128)(2,1)S(1)}, bf16[64,2048]{1,0:T(8,128)(2,1)S(1)}, u32[]{:S(2)}, u32[]{:S(2)}) collective-permute-start(bf16[64,2048]{1,0:T(8,128)(2,1)S(1)} %constant_dynamic-update-slice_fusion), channel_id=1, source_target_pairs={{0,24},{4,28},{8,16},{12,20},{16,8},{20,12},{24,0},{28,4},{1,25},{... | collective-permute-start | bytes 786440 | tf_op jit(solution)/shard_map/ppermute | solution.py:392
  9.0 1.6 %collective-permute-start.1 = (bf16[64,2048]{1,0:T(8,128)(2,1)S(1)}, bf16[64,2048]{1,0:T(8,128)(2,1)S(1)}, u32[]{:S(2)}, u32[]{:S(2)}) collective-permute-start(bf16[64,2048]{1,0:T(8,128)(2,1)S(1)} %constant_dynamic-update-slice_fusion), channel_id=1, source_target_pairs={{0,1},{1,0},{2,3},{3,2},{4,5},{5,4},{6,7},{7,6},{8,9},{9,8},{10,11... | collective-permute-start | bytes 786440 | tf_op jit(solution)/shard_map/ppermute | solution.py:401
  11.6 0.7 convert_element_type.6
  12.3 6.3 %collective-permute-done = bf16[64,2048]{1,0:T(8,128)(2,1)S(1)} collective-permute-done((bf16[64,2048]{1,0:T(8,128)(2,1)S(1)}, bf16[64,2048]{1,0:T(8,128)(2,1)S(1)}, u32[]{:S(2)}, u32[]{:S(2)}) %collective-permute-start) | collective-permute-done | bytes 262176 | tf_op jit(solution)/shard_map/ppermute | solution.py:401
  18.6 0.8 select_reduce_fusion
  20.0 1.0 collective-permute-done.1
  21.0 2.3 %collective-permute-start.7 = (bf16[64,2176]{1,0:T(8,128)(2,1)S(1)}, bf16[64,2176]{1,0:T(8,128)(2,1)S(1)}, u32[]{:S(2)}, u32[]{:S(2)}) collective-permute-start(bf16[64,2176]{1,0:T(8,128)(2,1)S(1)} %pad_maximum_fusion.6), channel_id=1, source_target_pairs={{0,24},{4,28},{8,16},{12,20},{16,8},{20,12},{24,0},{28,4},{1,25},{... | collective-permute-start | bytes 835592 | tf_op jit(solution)/shard_map/ppermute | solution.py:392
  23.3 2.8 %collective-permute-start.16 = (bf16[64,2048]{1,0:T(8,128)(2,1)S(1)}, bf16[64,2048]{1,0:T(8,128)(2,1)S(1)}, u32[]{:S(2)}, u32[]{:S(2)}) collective-permute-start(bf16[64,2048]{1,0:T(8,128)(2,1)S(1)} %constant_dynamic-update-slice_fusion), channel_id=1, source_target_pairs={{0,3},{1,2},{2,1},{3,0},{4,7},{5,6},{6,5},{7,4},{8,11},{9,10},{10,... | collective-permute-start | bytes 786440 | tf_op jit(solution)/shard_map/ppermute | solution.py:401
  26.1 7.1 %collective-permute-done.16 = bf16[64,2048]{1,0:T(8,128)(2,1)S(1)} collective-permute-done((bf16[64,2048]{1,0:T(8,128)(2,1)S(1)}, bf16[64,2048]{1,0:T(8,128)(2,1)S(1)}, u32[]{:S(2)}, u32[]{:S(2)}) %collective-permute-start.16) | collective-permute-done | bytes 262176 | tf_op jit(solution)/shard_map/ppermute | solution.py:401
  33.7 1.2 collective-permute-start.5
  34.9 5.6 %collective-permute-done.6 = bf16[64,2176]{1,0:T(8,128)(2,1)S(1)} collective-permute-done((bf16[64,2176]{1,0:T(8,128)(2,1)S(1)}, bf16[64,2176]{1,0:T(8,128)(2,1)S(1)}, u32[]{:S(2)}, u32[]{:S(2)}) %collective-permute-start.6) | collective-permute-done | bytes 278560 | tf_op jit(solution)/shard_map/ppermute | solution.py:392
  40.8 1.7 %collective-permute-start.8 = (bf16[64,2048]{1,0:T(8,128)(2,1)S(1)}, bf16[64,2048]{1,0:T(8,128)(2,1)S(1)}, u32[]{:S(2)}, u32[]{:S(2)}) collective-permute-start(bf16[64,2048]{1,0:T(8,128)(2,1)S(1)} %collective-permute-done), channel_id=1, source_target_pairs={{0,8},{4,12},{8,0},{12,4},{16,24},{20,28},{24,16},{28,20},{1,9},{5... | collective-permute-start | bytes 786440 | tf_op jit(solution)/shard_map/ppermute | solution.py:392
  43.0 4.1 %collective-permute-done.8 = bf16[64,2048]{1,0:T(8,128)(2,1)S(1)} collective-permute-done((bf16[64,2048]{1,0:T(8,128)(2,1)S(1)}, bf16[64,2048]{1,0:T(8,128)(2,1)S(1)}, u32[]{:S(2)}, u32[]{:S(2)}) %collective-permute-start.8) | collective-permute-done | bytes 262176 | tf_op jit(solution)/shard_map/ppermute | solution.py:392
  47.2 1.1 pad_maximum_fusion.1
  48.9 0.8 pad_maximum_fusion.5
  49.8 1.6 %collective-permute-start.18 = (bf16[2,64,2048]{2,1,0:T(8,128)(2,1)}, bf16[2,64,2048]{2,1,0:T(8,128)(2,1)}, u32[]{:S(2)}, u32[]{:S(2)}) collective-permute-start(bf16[2,64,2048]{2,1,0:T(8,128)(2,1)} %pad_maximum_fusion.5), channel_id=1, source_target_pairs={{0,8},{4,12},{8,0},{12,4},{16,24},{20,28},{24,16},{28,20},{1,9},{5... | collective-permute-start | bytes 1572872 | tf_op jit(solution)/shard_map/ppermute | solution.py:392
  51.4 0.9 pad_maximum_fusion.4
  53.4 4.9 %forward_slice.2.refs_6_ = f32[6,256,256]{2,1,0:T(8,128)} custom-call(s32[2]{0:T(128)} %pad_add_fusion.place, bf16[256,2048]{1,0:T(8,128)(2,1)} %bitcast.16.x_ref.dy_ref.refs_0_, bf16[256,2048]{1,0:T(8,128)(2,1)} %bitcast.16.x_ref.dy_ref.refs_0_, bf16[4096,256]{1,0:T(8,128)(2,1)} %bitcast.31, bf16[4096,256]{1,0:T(8,128)(2,1)} %bitcast.39, ...), custom_call_target="tpu_custom_call" | custom-call | flops 805306368 | bytes 5767168 | tf_op jit(solution)/shard_map/forward_slice/pallas_call | solution.py:114
  58.3 5.8 %forward_slice.3.refs_10_ = f32[6,256,256]{2,1,0:T(8,128)} custom-call(s32[2]{0:T(128)} %pad_add_fusion.place, bf16[256,2176]{1,0:T(8,128)(2,1)} %bitcast.47, bf16[256,2176]{1,0:T(8,128)(2,1)} %bitcast.48, bf16[4096,256]{1,0:T(8,128)(2,1)} %bitcast.32, bf16[4096,256]{1,0:T(8,128)(2,1)} %bitcast.40, bf16[256,4096]{1,0:T(8,128)(2,1)} %bitcast.54, ...), custom_call_target="tpu_custom_call" | custom-call | flops 805306368 | bytes 5767168 | tf_op jit(solution)/shard_map/forward_slice/pallas_call | solution.py:114
  64.4 1.4 %pad_maximum_fusion.3 = bf16[2,2,64,2048]{3,2,0,1:T(8,128)(2,1)S(1)} fusion(bf16[2,1,64,2048]{3,2,0,1:T(8,128)(2,1)} %bitcast.23, bf16[2,1,64,2048]{3,2,0,1:T(8,128)(2,1)} %bitcast.22), kind=kLoop, calls=%fused_computation.3 | loop fusion | flops 524288 | bytes 2097152 | tf_op jit(solution)/shard_map/stack | solution.py:431
  66.1 1.8 %pad_maximum_fusion.2 = bf16[2,2,64,2048]{3,2,1,0:T(8,128)(2,1)S(1)} fusion(bf16[1,2,64,2048]{3,2,1,0:T(8,128)(2,1)} %bitcast.18, bf16[1,2,64,2048]{3,2,1,0:T(8,128)(2,1)} %bitcast.17), kind=kLoop, calls=%fused_computation.2 | loop fusion | flops 524288 | bytes 2097152 | tf_op jit(solution)/shard_map/stack | solution.py:431
  68.9 1.4 %copy-done.10 = f32[6,256,256]{2,1,0:T(8,128)S(1)} copy-done((f32[6,256,256]{2,1,0:T(8,128)S(1)}, f32[6,256,256]{2,1,0:T(8,128)}, u32[]{:S(2)}) %copy-start.10) | copy-done | bytes 1572888
  70.3 4.1 %forward_rest.1 = (bf16[256,768]{1,0:T(8,128)(2,1)S(1)}, bf16[256,768]{1,0:T(8,128)(2,1)S(1)}, bf16[256,128]{1,0:T(8,128)(2,1)S(1)}) custom-call(s32[2]{0:T(128)S(1)} %copy-done.11, bf16[256,2048]{1,0:T(8,128)(2,1)S(1)} %bitcast.63, bf16[256,2048]{1,0:T(8,128)(2,1)S(1)} %bitcast.64, bf16[256,2048]{1,0:T(8,128)(2,1)S(1)} %bitcast.58, ...), custom_call_target="tpu_custom_call" | custom-call | flops 1610612736 | bytes 9961472 | tf_op jit(solution)/shard_map/forward_rest/pallas_call | solution.py:135
  74.6 2.5 %unit_product.4 = (f32[64,1152]{1,0:T(8,128)S(1)}, bf16[64,1152]{1,0:T(8,128)(2,1)S(1)}, bf16[64,1152]{1,0:T(8,128)(2,1)S(1)}, bf16[64,1152]{1,0:T(8,128)(2,1)S(1)}) custom-call(s32[2]{0:T(128)S(1)} %copy-done.11, bf16[256,768]{1,0:T(8,128)(2,1)S(1)} %get-tuple-element.56.mine.acts, bf16[256,768]{1,0:T(8,128)(2,1)S(1)} %get-tuple-element.54.other, ...), custom_call_target="tpu_custom_call" | custom-call | flops 536870912 | bytes 3407872 | tf_op jit(solution)/shard_map/unit_product/pallas_call | solution.py:192
  77.1 1.2 collective-permute-start.21
  78.3 0.7 collective-permute-start.22
  79.0 1.7 %collective-permute-start.23 = (bf16[64,1152]{1,0:T(8,128)(2,1)S(1)}, bf16[64,1152]{1,0:T(8,128)(2,1)S(1)}, u32[]{:S(2)}, u32[]{:S(2)}) collective-permute-start(bf16[64,1152]{1,0:T(8,128)(2,1)S(1)} %get-tuple-element.61), channel_id=1, source_target_pairs={{0,24},{4,28},{8,16},{12,20},{16,8},{20,12},{24,0},{28,4},{1,25},{... | collective-permute-start | bytes 442376 | tf_op jit(solution)/shard_map/ppermute | solution.py:392
  80.7 2.3 %unit_product.7 = (f32[64,1024]{1,0:T(8,128)S(1)}, bf16[64,1024]{1,0:T(8,128)(2,1)S(1)}, bf16[64,1024]{1,0:T(8,128)(2,1)S(1)}, bf16[64,1024]{1,0:T(8,128)(2,1)S(1)}) custom-call(s32[2]{0:T(128)S(1)} %copy-done.11, bf16[256,768]{1,0:T(8,128)(2,1)S(1)} %get-tuple-element.56.mine.acts, bf16[256,768]{1,0:T(8,128)(2,1)S(1)} %get-tuple-element.54.other, ...), custom_call_target="tpu_custom_call" | custom-call | flops 536870912 | bytes 3407872 | tf_op jit(solution)/shard_map/unit_product/pallas_call | solution.py:192
  83.1 1.2 collective-permute-start.24
  84.3 0.7 collective-permute-start.25
  85.0 1.7 %collective-permute-start.26 = (bf16[64,1024]{1,0:T(8,128)(2,1)S(1)}, bf16[64,1024]{1,0:T(8,128)(2,1)S(1)}, u32[]{:S(2)}, u32[]{:S(2)}) collective-permute-start(bf16[64,1024]{1,0:T(8,128)(2,1)S(1)} %get-tuple-element.69), channel_id=1, source_target_pairs={{0,24},{4,28},{8,16},{12,20},{16,8},{20,12},{24,0},{28,4},{1,25},{... | collective-permute-start | bytes 393224 | tf_op jit(solution)/shard_map/ppermute | solution.py:392
  86.6 2.3 %unit_product.6 = (f32[64,1024]{1,0:T(8,128)S(1)}, bf16[64,1024]{1,0:T(8,128)(2,1)S(1)}, bf16[64,1024]{1,0:T(8,128)(2,1)S(1)}, bf16[64,1024]{1,0:T(8,128)(2,1)S(1)}) custom-call(s32[2]{0:T(128)S(1)} %copy-done.11, bf16[256,768]{1,0:T(8,128)(2,1)S(1)} %get-tuple-element.56.mine.acts, bf16[256,768]{1,0:T(8,128)(2,1)S(1)} %get-tuple-element.54.other, ...), custom_call_target="tpu_custom_call" | custom-call | flops 536870912 | bytes 3407872 | tf_op jit(solution)/shard_map/unit_product/pallas_call | solution.py:192
  89.0 1.2 collective-permute-start.27
  90.2 0.7 collective-permute-start.28
  91.1 1.7 %collective-permute-start.29 = (bf16[64,1024]{1,0:T(8,128)(2,1)S(1)}, bf16[64,1024]{1,0:T(8,128)(2,1)S(1)}, u32[]{:S(2)}, u32[]{:S(2)}) collective-permute-start(bf16[64,1024]{1,0:T(8,128)(2,1)S(1)} %get-tuple-element.76), channel_id=1, source_target_pairs={{0,24},{4,28},{8,16},{12,20},{16,8},{20,12},{24,0},{28,4},{1,25},{... | collective-permute-start | bytes 393224 | tf_op jit(solution)/shard_map/ppermute | solution.py:392
  92.9 3.8 %collective-permute-start.33 = (bf16[64,1152]{1,0:T(8,128)(2,1)S(1)}, bf16[64,1152]{1,0:T(8,128)(2,1)S(1)}, u32[]{:S(2)}, u32[]{:S(2)}) collective-permute-start(bf16[64,1152]{1,0:T(8,128)(2,1)S(1)} %get-tuple-element.62), channel_id=1, source_target_pairs={{0,3},{1,2},{2,1},{3,0},{4,7},{5,6},{6,5},{7,4},{8,11},{9,10},{10,... | collective-permute-start | bytes 442376 | tf_op jit(solution)/shard_map/ppermute | solution.py:401
  96.7 2.3 %unit_product.5 = (f32[64,1024]{1,0:T(8,128)S(1)}, bf16[64,1024]{1,0:T(8,128)(2,1)S(1)}, bf16[64,1024]{1,0:T(8,128)(2,1)S(1)}, bf16[64,1024]{1,0:T(8,128)(2,1)S(1)}) custom-call(s32[2]{0:T(128)S(1)} %copy-done.11, bf16[256,768]{1,0:T(8,128)(2,1)S(1)} %get-tuple-element.56.mine.acts, bf16[256,768]{1,0:T(8,128)(2,1)S(1)} %get-tuple-element.54.other, ...), custom_call_target="tpu_custom_call" | custom-call | flops 536870912 | bytes 3407872 | tf_op jit(solution)/shard_map/unit_product/pallas_call | solution.py:192
  99.1 0.9 collective-permute-start.30
  100.0 7.3 %outer_gate_up.1 = (bf16[4096,256]{1,0:T(8,128)(2,1)}, bf16[4096,256]{1,0:T(8,128)(2,1)}) custom-call(s32[2]{0:T(128)} %pad_add_fusion.place, bf16[256,768]{1,0:T(8,128)(2,1)} %copy-done.9, bf16[256,768]{1,0:T(8,128)(2,1)} %copy-done.14, bf16[256,2048]{1,0:T(8,128)(2,1)} %bitcast.16.x_ref.dy_ref.refs_0_, bf16[256,2176]{1,0:T(8,128)(2,1)} %bitcast.49, ...), custom_call_target="tpu_custom_call" | custom-call | flops 2147483648 | bytes 8388608 | tf_op jit(solution)/shard_map/outer_gate_up/pallas_call | solution.py:270
  107.3 3.2 %collective-permute-start.34 = (bf16[64,1152]{1,0:T(8,128)(2,1)S(1)}, bf16[64,1152]{1,0:T(8,128)(2,1)S(1)}, u32[]{:S(2)}, u32[]{:S(2)}) collective-permute-start(bf16[64,1152]{1,0:T(8,128)(2,1)S(1)} %slice_sum.4), channel_id=1, source_target_pairs={{0,2},{1,3},{2,0},{3,1},{4,6},{5,7},{6,4},{7,5},{8,10},{9,11},{10,... | collective-permute-start | bytes 442376 | tf_op jit(solution)/shard_map/ppermute | solution.py:401
  110.7 0.9 collective-permute-start.31
  111.6 1.5 %collective-permute-start.32 = (bf16[64,1024]{1,0:T(8,128)(2,1)S(1)}, bf16[64,1024]{1,0:T(8,128)(2,1)S(1)}, u32[]{:S(2)}, u32[]{:S(2)}) collective-permute-start(bf16[64,1024]{1,0:T(8,128)(2,1)S(1)} %get-tuple-element.81), channel_id=1, source_target_pairs={{0,24},{4,28},{8,16},{12,20},{16,8},{20,12},{24,0},{28,4},{1,25},{... | collective-permute-start | bytes 393224 | tf_op jit(solution)/shard_map/ppermute | solution.py:392
  113.2 9.0 %outer_down.1 = bf16[256,4096]{1,0:T(8,128)(2,1)} custom-call(s32[2]{0:T(128)} %pad_add_fusion.place, bf16[256,768]{1,0:T(8,128)(2,1)} %copy-done.9, bf16[256,768]{1,0:T(8,128)(2,1)} %copy-done.14, bf16[256,2048]{1,0:T(8,128)(2,1)} %bitcast.16.x_ref.dy_ref.refs_0_, bf16[256,2176]{1,0:T(8,128)(2,1)} %bitcast.50, bf16[256,2048]{1,0:T(8,128)(2,1)} %bitcast.66, ...), custom_call_target="tpu_custom_call" | custom-call | flops 1073741824 | bytes 16777216 | tf_op jit(solution)/shard_map/outer_down/pallas_call | solution.py:270
  122.2 1.0 final_sum.1
  123.2 0.7 copy.21
  (84 shorter events, 6.8 us)
Async XLA Ops:
  2.5 16.1 %collective-permute-start = (bf16[64,2048]{1,0:T(8,128)(2,1)S(1)}, bf16[64,2048]{1,0:T(8,128)(2,1)S(1)}, u32[]{:S(2)}, u32[]{:S(2)}) collective-permute-start(bf16[64,2048]{1,0:T(8,128)(2,1)S(1)} %constant_dynamic-update-slice_fusion), channel_id=1, source_target_pairs={{0,2},{1,3},{2,0},{3,1},{4,6},{5,7},{6,4},{7,5},{8,10},{9,11},{10,... | collective-permute-start | bytes 786440 | tf_op jit(solution)/shard_map/ppermute | solution.py:401
  6.6 12.9 %collective-permute-start.4 = (bf16[64,2048]{1,0:T(8,128)(2,1)S(1)}, bf16[64,2048]{1,0:T(8,128)(2,1)S(1)}, u32[]{:S(2)}, u32[]{:S(2)}) collective-permute-start(bf16[64,2048]{1,0:T(8,128)(2,1)S(1)} %constant_dynamic-update-slice_fusion), channel_id=1, source_target_pairs={{0,24},{4,28},{8,16},{12,20},{16,8},{20,12},{24,0},{28,4},{1,25},{... | collective-permute-start | bytes 786440 | tf_op jit(solution)/shard_map/ppermute | solution.py:392
  9.0 11.9 %collective-permute-start.1 = (bf16[64,2048]{1,0:T(8,128)(2,1)S(1)}, bf16[64,2048]{1,0:T(8,128)(2,1)S(1)}, u32[]{:S(2)}, u32[]{:S(2)}) collective-permute-start(bf16[64,2048]{1,0:T(8,128)(2,1)S(1)} %constant_dynamic-update-slice_fusion), channel_id=1, source_target_pairs={{0,1},{1,0},{2,3},{3,2},{4,5},{5,4},{6,7},{7,6},{8,9},{9,8},{10,11... | collective-permute-start | bytes 786440 | tf_op jit(solution)/shard_map/ppermute | solution.py:401
  10.6 10.4 %collective-permute-start.3 = (bf16[64,2048]{1,0:T(8,128)(2,1)S(1)}, bf16[64,2048]{1,0:T(8,128)(2,1)S(1)}, u32[]{:S(2)}, u32[]{:S(2)}) collective-permute-start(bf16[64,2048]{1,0:T(8,128)(2,1)S(1)} %constant_dynamic-update-slice_fusion), channel_id=1, source_target_pairs={{0,16},{4,20},{8,24},{12,28},{16,0},{20,4},{24,8},{28,12},{1,17},{... | collective-permute-start | bytes 786440 | tf_op jit(solution)/shard_map/ppermute | solution.py:392
  11.1 9.9 %collective-permute-start.2 = (bf16[64,2048]{1,0:T(8,128)(2,1)S(1)}, bf16[64,2048]{1,0:T(8,128)(2,1)S(1)}, u32[]{:S(2)}, u32[]{:S(2)}) collective-permute-start(bf16[64,2048]{1,0:T(8,128)(2,1)S(1)} %constant_dynamic-update-slice_fusion), channel_id=1, source_target_pairs={{0,8},{4,12},{8,0},{12,4},{16,24},{20,28},{24,16},{28,20},{1,9},{5... | collective-permute-start | bytes 786440 | tf_op jit(solution)/shard_map/ppermute | solution.py:392
  18.6 31.2 %collective-permute-start.9 = (bf16[4096,256]{1,0:T(8,128)(2,1)}, bf16[4096,256]{1,0:T(8,128)(2,1)S(1)}, u32[]{:S(2)}, u32[]{:S(2)}) collective-permute-start(bf16[4096,256]{1,0:T(8,128)(2,1)} %bitcast.30), channel_id=1, source_target_pairs={{0,4},{4,0},{8,12},{12,8},{16,20},{20,16},{24,28},{28,24},{1,5},{5... | collective-permute-start | bytes 6291464 | tf_op jit(solution)/shard_map/ppermute | solution.py:392
  19.4 32.8 %collective-permute-start.10 = (bf16[4096,256]{1,0:T(8,128)(2,1)}, bf16[4096,256]{1,0:T(8,128)(2,1)}, u32[]{:S(2)}, u32[]{:S(2)}) collective-permute-start(bf16[4096,256]{1,0:T(8,128)(2,1)} %bitcast.38), channel_id=1, source_target_pairs={{0,4},{4,0},{8,12},{12,8},{16,20},{20,16},{24,28},{28,24},{1,5},{5... | collective-permute-start | bytes 6291464 | tf_op jit(solution)/shard_map/ppermute | solution.py:392
  21.0 32.4 %collective-permute-start.11 = (bf16[256,4096]{1,0:T(8,128)(2,1)}, bf16[256,4096]{1,0:T(8,128)(2,1)}, u32[]{:S(2)}, u32[]{:S(2)}) collective-permute-start(bf16[256,4096]{1,0:T(8,128)(2,1)} %bitcast.52), channel_id=1, source_target_pairs={{0,4},{4,0},{8,12},{12,8},{16,20},{20,16},{24,28},{28,24},{1,5},{5... | collective-permute-start | bytes 6291464 | tf_op jit(solution)/shard_map/ppermute | solution.py:392
  21.0 12.7 %collective-permute-start.7 = (bf16[64,2176]{1,0:T(8,128)(2,1)S(1)}, bf16[64,2176]{1,0:T(8,128)(2,1)S(1)}, u32[]{:S(2)}, u32[]{:S(2)}) collective-permute-start(bf16[64,2176]{1,0:T(8,128)(2,1)S(1)} %pad_maximum_fusion.6), channel_id=1, source_target_pairs={{0,24},{4,28},{8,16},{12,20},{16,8},{20,12},{24,0},{28,4},{1,25},{... | collective-permute-start | bytes 835592 | tf_op jit(solution)/shard_map/ppermute | solution.py:392
  23.3 9.9 %collective-permute-start.16 = (bf16[64,2048]{1,0:T(8,128)(2,1)S(1)}, bf16[64,2048]{1,0:T(8,128)(2,1)S(1)}, u32[]{:S(2)}, u32[]{:S(2)}) collective-permute-start(bf16[64,2048]{1,0:T(8,128)(2,1)S(1)} %constant_dynamic-update-slice_fusion), channel_id=1, source_target_pairs={{0,3},{1,2},{2,1},{3,0},{4,7},{5,6},{6,5},{7,4},{8,11},{9,10},{10,... | collective-permute-start | bytes 786440 | tf_op jit(solution)/shard_map/ppermute | solution.py:401
  33.2 7.4 %collective-permute-start.6 = (bf16[64,2176]{1,0:T(8,128)(2,1)S(1)}, bf16[64,2176]{1,0:T(8,128)(2,1)S(1)}, u32[]{:S(2)}, u32[]{:S(2)}) collective-permute-start(bf16[64,2176]{1,0:T(8,128)(2,1)S(1)} %pad_maximum_fusion.6), channel_id=1, source_target_pairs={{0,16},{4,20},{8,24},{12,28},{16,0},{20,4},{24,8},{28,12},{1,17},{... | collective-permute-start | bytes 835592 | tf_op jit(solution)/shard_map/ppermute | solution.py:392
  33.7 7.1 %collective-permute-start.5 = (bf16[64,2176]{1,0:T(8,128)(2,1)S(1)}, bf16[64,2176]{1,0:T(8,128)(2,1)S(1)}, u32[]{:S(2)}, u32[]{:S(2)}) collective-permute-start(bf16[64,2176]{1,0:T(8,128)(2,1)S(1)} %pad_maximum_fusion.6), channel_id=1, source_target_pairs={{0,8},{4,12},{8,0},{12,4},{16,24},{20,28},{24,16},{28,20},{1,9},{5... | collective-permute-start | bytes 835592 | tf_op jit(solution)/shard_map/ppermute | solution.py:392
  40.8 6.4 %collective-permute-start.8 = (bf16[64,2048]{1,0:T(8,128)(2,1)S(1)}, bf16[64,2048]{1,0:T(8,128)(2,1)S(1)}, u32[]{:S(2)}, u32[]{:S(2)}) collective-permute-start(bf16[64,2048]{1,0:T(8,128)(2,1)S(1)} %collective-permute-done), channel_id=1, source_target_pairs={{0,8},{4,12},{8,0},{12,4},{16,24},{20,28},{24,16},{28,20},{1,9},{5... | collective-permute-start | bytes 786440 | tf_op jit(solution)/shard_map/ppermute | solution.py:392
  42.5 6.4 %collective-permute-start.17 = (bf16[64,2048]{1,0:T(8,128)(2,1)S(1)}, bf16[64,2048]{1,0:T(8,128)(2,1)S(1)}, u32[]{:S(2)}, u32[]{:S(2)}) collective-permute-start(bf16[64,2048]{1,0:T(8,128)(2,1)S(1)} %collective-permute-done.16), channel_id=1, source_target_pairs={{0,16},{4,20},{8,24},{12,28},{16,0},{20,4},{24,8},{28,12},{1,17},{... | collective-permute-start | bytes 786440 | tf_op jit(solution)/shard_map/ppermute | solution.py:392
  43.0 9.2 %copy-start.4 = (bf16[4,64,2176]{2,1,0:T(8,128)(2,1)}, bf16[4,64,2176]{2,1,0:T(8,128)(2,1)S(1)}, u32[]{:S(2)}) copy-start(bf16[4,64,2176]{2,1,0:T(8,128)(2,1)S(1)} %pad_maximum_fusion) | copy-start | bytes 3342340
  47.2 16.9 %collective-permute-start.13 = (bf16[256,2176]{1,0:T(8,128)(2,1)S(1)}, bf16[256,2176]{1,0:T(8,128)(2,1)}, u32[]{:S(2)}, u32[]{:S(2)}) collective-permute-start(bf16[256,2176]{1,0:T(8,128)(2,1)S(1)} %bitcast.46), channel_id=1, source_target_pairs={{0,4},{4,0},{8,12},{12,8},{16,20},{20,16},{24,28},{28,24},{1,5},{5... | collective-permute-start | bytes 3342344 | tf_op jit(solution)/shard_map/ppermute | solution.py:392
  48.9 15.2 %collective-permute-start.12 = (bf16[256,2048]{1,0:T(8,128)(2,1)}, bf16[256,2048]{1,0:T(8,128)(2,1)}, u32[]{:S(2)}, u32[]{:S(2)}) collective-permute-start(bf16[256,2048]{1,0:T(8,128)(2,1)} %bitcast.16.x_ref.dy_ref.refs_0_), channel_id=1, source_target_pairs={{0,4},{4,0},{8,12},{12,8},{16,20},{20,16},{24,28},{28,24},{1,5},{5... | collective-permute-start | bytes 3145736 | tf_op jit(solution)/shard_map/ppermute | solution.py:392
  49.8 3.6 %copy-start.2 = (bf16[4096,256]{1,0:T(8,128)(2,1)}, bf16[4096,256]{1,0:T(8,128)(2,1)S(1)}, u32[]{:S(2)}) copy-start(bf16[4096,256]{1,0:T(8,128)(2,1)S(1)} %collective-permute-done.9.refs_3_.refs_7_.refs_2_) | copy-start | bytes 6291460
  49.8 14.7 %collective-permute-start.18 = (bf16[2,64,2048]{2,1,0:T(8,128)(2,1)}, bf16[2,64,2048]{2,1,0:T(8,128)(2,1)}, u32[]{:S(2)}, u32[]{:S(2)}) collective-permute-start(bf16[2,64,2048]{2,1,0:T(8,128)(2,1)} %pad_maximum_fusion.5), channel_id=1, source_target_pairs={{0,8},{4,12},{8,0},{12,4},{16,24},{20,28},{24,16},{28,20},{1,9},{5... | collective-permute-start | bytes 1572872 | tf_op jit(solution)/shard_map/ppermute | solution.py:392
  52.3 13.9 %collective-permute-start.14 = (bf16[2,64,2048]{2,1,0:T(8,128)(2,1)}, bf16[2,64,2048]{2,1,0:T(8,128)(2,1)}, u32[]{:S(2)}, u32[]{:S(2)}) collective-permute-start(bf16[2,64,2048]{2,1,0:T(8,128)(2,1)} %pad_maximum_fusion.4), channel_id=1, source_target_pairs={{0,16},{4,20},{8,24},{12,28},{16,0},{20,4},{24,8},{28,12},{1,17},{... | collective-permute-start | bytes 1572872 | tf_op jit(solution)/shard_map/ppermute | solution.py:392
  58.3 10.2 %copy-start.5 = (bf16[4,64,2176]{2,1,0:T(8,128)(2,1)S(1)}, bf16[4,64,2176]{2,1,0:T(8,128)(2,1)}, u32[]{:S(2)}) copy-start(bf16[4,64,2176]{2,1,0:T(8,128)(2,1)} %copy-done.4) | copy-start | bytes 3342340
  58.3 10.2 %copy-start.6 = (bf16[1,256,4096]{2,1,0:T(8,128)(2,1)S(1)}, bf16[1,256,4096]{2,1,0:T(8,128)(2,1)}, u32[]{:S(2)}) copy-start(bf16[1,256,4096]{2,1,0:T(8,128)(2,1)} %param.15) | copy-start | bytes 6291460
  64.4 4.1 %copy-start.3 = (bf16[4096,256]{1,0:T(8,128)(2,1)S(1)}, bf16[4096,256]{1,0:T(8,128)(2,1)}, u32[]{:S(2)}) copy-start(bf16[4096,256]{1,0:T(8,128)(2,1)} %copy-done.2) | copy-start | bytes 6291460
  65.9 3.0 %copy-start.1 = (bf16[1,4096,256]{2,1,0:T(8,128)(2,1)S(1)}, bf16[1,4096,256]{2,1,0:T(8,128)(2,1)}, u32[]{:S(2)}) copy-start(bf16[1,4096,256]{2,1,0:T(8,128)(2,1)} %param.14) | copy-start | bytes 6291460
  65.9 3.0 %copy-start.11 = (s32[2]{0:T(128)S(1)}, s32[2]{0:T(128)}, u32[]{:S(2)}) copy-start(s32[2]{0:T(128)} %pad_add_fusion.place) | copy-start | bytes 28
  66.0 8.4 %copy-start.7 = (bf16[2,2,64,2048]{3,2,1,0:T(8,128)(2,1)}, bf16[2,2,64,2048]{3,2,1,0:T(8,128)(2,1)S(1)}, u32[]{:S(2)}) copy-start(bf16[2,2,64,2048]{3,2,1,0:T(8,128)(2,1)S(1)} %copy.19) | copy-start | bytes 3145732
  67.9 6.5 %copy-start.8 = (bf16[2,2,64,2048]{3,2,1,0:T(8,128)(2,1)}, bf16[2,2,64,2048]{3,2,1,0:T(8,128)(2,1)S(1)}, u32[]{:S(2)}) copy-start(bf16[2,2,64,2048]{3,2,1,0:T(8,128)(2,1)S(1)} %pad_maximum_fusion.2) | copy-start | bytes 3145732
  67.9 6.6 %collective-permute-start.15 = (bf16[256,2048]{1,0:T(8,128)(2,1)S(1)}, bf16[256,2048]{1,0:T(8,128)(2,1)S(1)}, u32[]{:S(2)}, u32[]{:S(2)}) collective-permute-start(bf16[256,2048]{1,0:T(8,128)(2,1)S(1)} %bitcast.62), channel_id=1, source_target_pairs={{0,4},{4,0},{8,12},{12,8},{16,20},{20,16},{24,28},{28,24},{1,5},{5... | collective-permute-start | bytes 3145736 | tf_op jit(solution)/shard_map/ppermute | solution.py:392
  68.0 6.6 %collective-permute-start.19 = (bf16[256,2048]{1,0:T(8,128)(2,1)S(1)}, bf16[256,2048]{1,0:T(8,128)(2,1)S(1)}, u32[]{:S(2)}, u32[]{:S(2)}) collective-permute-start(bf16[256,2048]{1,0:T(8,128)(2,1)S(1)} %bitcast.57), channel_id=1, source_target_pairs={{0,4},{4,0},{8,12},{12,8},{16,20},{20,16},{24,28},{28,24},{1,5},{5... | collective-permute-start | bytes 3145736 | tf_op jit(solution)/shard_map/ppermute | solution.py:392
  74.5 22.2 %copy-start.9 = (bf16[256,768]{1,0:T(8,128)(2,1)}, bf16[256,768]{1,0:T(8,128)(2,1)S(1)}, u32[]{:S(2)}) copy-start(bf16[256,768]{1,0:T(8,128)(2,1)S(1)} %get-tuple-element.56.mine.acts) | copy-start | bytes 1179652
  74.5 3.9 %collective-permute-start.20 = (bf16[256,768]{1,0:T(8,128)(2,1)S(1)}, bf16[256,768]{1,0:T(8,128)(2,1)S(1)}, u32[]{:S(2)}, u32[]{:S(2)}) collective-permute-start(bf16[256,768]{1,0:T(8,128)(2,1)S(1)} %get-tuple-element.54.other), channel_id=1, source_target_pairs={{0,4},{4,0},{8,12},{12,8},{16,20},{20,16},{24,28},{28,24},{1,5},{5... | collective-permute-start | bytes 1179656 | tf_op jit(solution)/shard_map/ppermute | solution.py:392
  77.1 7.8 %collective-permute-start.21 = (bf16[64,1152]{1,0:T(8,128)(2,1)S(1)}, bf16[64,1152]{1,0:T(8,128)(2,1)S(1)}, u32[]{:S(2)}, u32[]{:S(2)}) collective-permute-start(bf16[64,1152]{1,0:T(8,128)(2,1)S(1)} %get-tuple-element.59), channel_id=1, source_target_pairs={{0,8},{4,12},{8,0},{12,4},{16,24},{20,28},{24,16},{28,20},{1,9},{5... | collective-permute-start | bytes 442376 | tf_op jit(solution)/shard_map/ppermute | solution.py:392
  78.3 4.7 %copy-start.14 = (bf16[256,768]{1,0:T(8,128)(2,1)}, bf16[256,768]{1,0:T(8,128)(2,1)S(1)}, u32[]{:S(2)}) copy-start(bf16[256,768]{1,0:T(8,128)(2,1)S(1)} %collective-permute-done.20.got) | copy-start | bytes 1179652
  78.3 10.6 %collective-permute-start.22 = (bf16[64,1152]{1,0:T(8,128)(2,1)S(1)}, bf16[64,1152]{1,0:T(8,128)(2,1)S(1)}, u32[]{:S(2)}, u32[]{:S(2)}) collective-permute-start(bf16[64,1152]{1,0:T(8,128)(2,1)S(1)} %get-tuple-element.60), channel_id=1, source_target_pairs={{0,16},{4,20},{8,24},{12,28},{16,0},{20,4},{24,8},{28,12},{1,17},{... | collective-permute-start | bytes 442376 | tf_op jit(solution)/shard_map/ppermute | solution.py:392
  79.0 11.1 %collective-permute-start.23 = (bf16[64,1152]{1,0:T(8,128)(2,1)S(1)}, bf16[64,1152]{1,0:T(8,128)(2,1)S(1)}, u32[]{:S(2)}, u32[]{:S(2)}) collective-permute-start(bf16[64,1152]{1,0:T(8,128)(2,1)S(1)} %get-tuple-element.61), channel_id=1, source_target_pairs={{0,24},{4,28},{8,16},{12,20},{16,8},{20,12},{24,0},{28,4},{1,25},{... | collective-permute-start | bytes 442376 | tf_op jit(solution)/shard_map/ppermute | solution.py:392
  83.1 8.1 %collective-permute-start.24 = (bf16[64,1024]{1,0:T(8,128)(2,1)S(1)}, bf16[64,1024]{1,0:T(8,128)(2,1)S(1)}, u32[]{:S(2)}, u32[]{:S(2)}) collective-permute-start(bf16[64,1024]{1,0:T(8,128)(2,1)S(1)} %get-tuple-element.67), channel_id=1, source_target_pairs={{0,8},{4,12},{8,0},{12,4},{16,24},{20,28},{24,16},{28,20},{1,9},{5... | collective-permute-start | bytes 393224 | tf_op jit(solution)/shard_map/ppermute | solution.py:392
  84.3 8.6 %collective-permute-start.25 = (bf16[64,1024]{1,0:T(8,128)(2,1)S(1)}, bf16[64,1024]{1,0:T(8,128)(2,1)S(1)}, u32[]{:S(2)}, u32[]{:S(2)}) collective-permute-start(bf16[64,1024]{1,0:T(8,128)(2,1)S(1)} %get-tuple-element.68), channel_id=1, source_target_pairs={{0,16},{4,20},{8,24},{12,28},{16,0},{20,4},{24,8},{28,12},{1,17},{... | collective-permute-start | bytes 393224 | tf_op jit(solution)/shard_map/ppermute | solution.py:392
  85.0 11.7 %collective-permute-start.26 = (bf16[64,1024]{1,0:T(8,128)(2,1)S(1)}, bf16[64,1024]{1,0:T(8,128)(2,1)S(1)}, u32[]{:S(2)}, u32[]{:S(2)}) collective-permute-start(bf16[64,1024]{1,0:T(8,128)(2,1)S(1)} %get-tuple-element.69), channel_id=1, source_target_pairs={{0,24},{4,28},{8,16},{12,20},{16,8},{20,12},{24,0},{28,4},{1,25},{... | collective-permute-start | bytes 393224 | tf_op jit(solution)/shard_map/ppermute | solution.py:392
  89.0 18.3 %collective-permute-start.27 = (bf16[64,1024]{1,0:T(8,128)(2,1)S(1)}, bf16[64,1024]{1,0:T(8,128)(2,1)S(1)}, u32[]{:S(2)}, u32[]{:S(2)}) collective-permute-start(bf16[64,1024]{1,0:T(8,128)(2,1)S(1)} %get-tuple-element.74), channel_id=1, source_target_pairs={{0,8},{4,12},{8,0},{12,4},{16,24},{20,28},{24,16},{28,20},{1,9},{5... | collective-permute-start | bytes 393224 | tf_op jit(solution)/shard_map/ppermute | solution.py:392
  90.2 20.3 %collective-permute-start.28 = (bf16[64,1024]{1,0:T(8,128)(2,1)S(1)}, bf16[64,1024]{1,0:T(8,128)(2,1)S(1)}, u32[]{:S(2)}, u32[]{:S(2)}) collective-permute-start(bf16[64,1024]{1,0:T(8,128)(2,1)S(1)} %get-tuple-element.75), channel_id=1, source_target_pairs={{0,16},{4,20},{8,24},{12,28},{16,0},{20,4},{24,8},{28,12},{1,17},{... | collective-permute-start | bytes 393224 | tf_op jit(solution)/shard_map/ppermute | solution.py:392
  91.1 19.4 %collective-permute-start.29 = (bf16[64,1024]{1,0:T(8,128)(2,1)S(1)}, bf16[64,1024]{1,0:T(8,128)(2,1)S(1)}, u32[]{:S(2)}, u32[]{:S(2)}) collective-permute-start(bf16[64,1024]{1,0:T(8,128)(2,1)S(1)} %get-tuple-element.76), channel_id=1, source_target_pairs={{0,24},{4,28},{8,16},{12,20},{16,8},{20,12},{24,0},{28,4},{1,25},{... | collective-permute-start | bytes 393224 | tf_op jit(solution)/shard_map/ppermute | solution.py:392
  92.9 29.3 %collective-permute-start.33 = (bf16[64,1152]{1,0:T(8,128)(2,1)S(1)}, bf16[64,1152]{1,0:T(8,128)(2,1)S(1)}, u32[]{:S(2)}, u32[]{:S(2)}) collective-permute-start(bf16[64,1152]{1,0:T(8,128)(2,1)S(1)} %get-tuple-element.62), channel_id=1, source_target_pairs={{0,3},{1,2},{2,1},{3,0},{4,7},{5,6},{6,5},{7,4},{8,11},{9,10},{10,... | collective-permute-start | bytes 442376 | tf_op jit(solution)/shard_map/ppermute | solution.py:401
  99.1 14.0 %copy-start.15 = (s32[64,4]{0,1:T(4,128)S(1)}, s32[64,4]{0,1:T(4,128)}, u32[]{:S(2)}) copy-start(s32[64,4]{0,1:T(4,128)} %param.11) | copy-start | bytes 3076
  99.1 12.5 %collective-permute-start.30 = (bf16[64,1024]{1,0:T(8,128)(2,1)S(1)}, bf16[64,1024]{1,0:T(8,128)(2,1)S(1)}, u32[]{:S(2)}, u32[]{:S(2)}) collective-permute-start(bf16[64,1024]{1,0:T(8,128)(2,1)S(1)} %get-tuple-element.79), channel_id=1, source_target_pairs={{0,8},{4,12},{8,0},{12,4},{16,24},{20,28},{24,16},{28,20},{1,9},{5... | collective-permute-start | bytes 393224 | tf_op jit(solution)/shard_map/ppermute | solution.py:392
  107.3 14.9 %collective-permute-start.34 = (bf16[64,1152]{1,0:T(8,128)(2,1)S(1)}, bf16[64,1152]{1,0:T(8,128)(2,1)S(1)}, u32[]{:S(2)}, u32[]{:S(2)}) collective-permute-start(bf16[64,1152]{1,0:T(8,128)(2,1)S(1)} %slice_sum.4), channel_id=1, source_target_pairs={{0,2},{1,3},{2,0},{3,1},{4,6},{5,7},{6,4},{7,5},{8,10},{9,11},{10,... | collective-permute-start | bytes 442376 | tf_op jit(solution)/shard_map/ppermute | solution.py:401
  110.6 11.6 %collective-permute-start.35 = (bf16[64,1152]{1,0:T(8,128)(2,1)S(1)}, bf16[64,1152]{1,0:T(8,128)(2,1)S(1)}, u32[]{:S(2)}, u32[]{:S(2)}) collective-permute-start(bf16[64,1152]{1,0:T(8,128)(2,1)S(1)} %slice_sum.5), channel_id=1, source_target_pairs={{0,1},{1,0},{2,3},{3,2},{4,5},{5,4},{6,7},{7,6},{8,9},{9,8},{10,11... | collective-permute-start | bytes 442376 | tf_op jit(solution)/shard_map/ppermute | solution.py:401
  110.7 11.5 %collective-permute-start.31 = (bf16[64,1024]{1,0:T(8,128)(2,1)S(1)}, bf16[64,1024]{1,0:T(8,128)(2,1)S(1)}, u32[]{:S(2)}, u32[]{:S(2)}) collective-permute-start(bf16[64,1024]{1,0:T(8,128)(2,1)S(1)} %get-tuple-element.80), channel_id=1, source_target_pairs={{0,16},{4,20},{8,24},{12,28},{16,0},{20,4},{24,8},{28,12},{1,17},{... | collective-permute-start | bytes 393224 | tf_op jit(solution)/shard_map/ppermute | solution.py:392
  111.6 10.6 %collective-permute-start.32 = (bf16[64,1024]{1,0:T(8,128)(2,1)S(1)}, bf16[64,1024]{1,0:T(8,128)(2,1)S(1)}, u32[]{:S(2)}, u32[]{:S(2)}) collective-permute-start(bf16[64,1024]{1,0:T(8,128)(2,1)S(1)} %get-tuple-element.81), channel_id=1, source_target_pairs={{0,24},{4,28},{8,16},{12,20},{16,8},{20,12},{24,0},{28,4},{1,25},{... | collective-permute-start | bytes 393224 | tf_op jit(solution)/shard_map/ppermute | solution.py:392
  (4 other events, 9.2 us)

commit v3 on v2

v3 whole, which is shorter than its diff:
```python
import functools
import math

import jax
import jax.numpy as jnp
from jax import lax
from jax.experimental import pallas as pl
from jax.experimental.pallas import tpu as pltpu
from jax.sharding import PartitionSpec as P

BF = jnp.bfloat16
F32 = jnp.float32
LANES = 128
MIB = 1024 * 1024


def whole_block(shape):
    zeros = (0,) * len(shape)
    return pl.BlockSpec(shape, lambda *_: zeros, pipeline_mode=pl.Buffered(1))


def dot(a, b, a_dim, b_dim):
    return lax.dot_general(a, b, (((a_dim,), (b_dim,)), ((), ())), preferred_element_type=F32)


def after(value, *first):
    return lax.optimization_barrier((value, *first))[0]


def params(need):
    return pltpu.CompilerParams(vmem_limit_bytes=min(need + 12 * MIB, 58 * MIB))


def add_slice(x, dy, weights, before):
    values = []
    for number, weight in enumerate(weights):
        from_dy = number % 3 == 2
        part = dot(dy if from_dy else x, weight[...], 1, 1 if from_dy else 0)
        values.append(part if before is None else part + before[number])
    return values


def near_kernel(own_ref, near_ref, weights, out):
    width = weights[0].shape[0]
    step = pl.program_id(0)
    for at, (ref, base) in enumerate(((own_ref, 0), (near_ref, 0), (near_ref, 2))):

        @pl.when(step == at)
        def _(at=at, ref=ref, base=base):
            x = ref[:, base * width : (base + 1) * width]
            dy = ref[:, (base + 1) * width : (base + 2) * width]
            values = add_slice(x, dy, weights, out if at else None)
            for number in range(6):
                out[number] = values[number]


def forward_kernel(place, own_ref, near_ref, *refs):
    near_kernel(own_ref, near_ref, refs[:6], refs[6])


def rest_kernel(n_expert, slots, place, *refs):
    sources, refs = refs[: 2 * slots], refs[2 * slots :]
    weights, before, route_w = refs[:6], refs[6], refs[7]
    mine, other, route, held = refs[8:]
    units = weights[0].shape[1]
    step = pl.program_id(0)

    for at in range(slots - 1):

        @pl.when(step == at)
        def _(at=at):
            x, dy = sources[2 * at][...], sources[2 * at + 1][...]
            values = add_slice(x, dy, weights, held if at else before)
            for number in range(6):
                held[number] = values[number]

    @pl.when(step == slots - 1)
    def _():
        values = add_slice(
            sources[-2][...], sources[-1][...], weights, held if slots > 1 else before
        )
        lane = lax.broadcasted_iota(jnp.int32, route.shape, 1)
        total = jnp.zeros(route.shape, F32)
        for j, acts in enumerate((mine, other)):
            expert = jnp.bitwise_xor(place[1], j)
            gate_pre, up_pre, back = values[3 * j : 3 * j + 3]
            weight = jnp.sum(
                jnp.where(lane == expert, route_w[...].astype(F32), 0.0), axis=1, keepdims=True
            )
            logistic = jax.nn.sigmoid(gate_pre)
            active = gate_pre * logistic
            hidden = active * up_pre
            route_part = jnp.sum(back * hidden, axis=1, keepdims=True)
            high = route_part.astype(BF).astype(F32)
            total = total + jnp.where(lane == expert, high, 0.0)
            total = total + jnp.where(lane == expert + n_expert, route_part - high, 0.0)
            scaled = weight * back
            acts[:, :units] = (
                scaled * up_pre * logistic * (1.0 + gate_pre * (1.0 - logistic))
            ).astype(BF)
            acts[:, units : 2 * units] = (scaled * active).astype(BF)
            acts[:, 2 * units :] = (weight * hidden).astype(BF)
        route[...] = total.astype(BF)


def column_block(rows, width, column):
    return pl.BlockSpec(
        (rows, width), lambda i, p: (0, column), pipeline_mode=pl.Buffered(1)
    )


def forward_cost(rows, width, units, slots):
    return pl.CostEstimate(
        flops=12 * rows * width * units * slots,
        bytes_accessed=2 * width * (2 * rows + 6 * units) * slots + 24 * rows * units,
        transcendentals=2 * rows * units,
    )


def forward_near(place, own, near, weights, width):
    rows = own.shape[0]
    units = weights[0].shape[1]
    wide = pl.BlockSpec((width, units), lambda i, p: (p[0] ^ i, 0))
    tall = pl.BlockSpec((units, width), lambda i, p: (0, p[0] ^ i))
    return pl.pallas_call(
        forward_kernel,
        grid_spec=pltpu.PrefetchScalarGridSpec(
            num_scalar_prefetch=1,
            grid=(3,),
            in_specs=[whole_block(own.shape), whole_block(near.shape)]
            + [wide, wide, tall] * 2,
            out_specs=whole_block((6, rows, units)),
        ),
        out_shape=jax.ShapeDtypeStruct((6, rows, units), F32),
        compiler_params=params(14 * MIB),
        cost_estimate=forward_cost(rows, width, units, 3),
        name="forward_near",
    )(place, own, near, *weights)


def forward_rest(place, pairs, weights, before, route_w, n_expert, width, done):
    rows = pairs[0].shape[0]
    units = weights[0].shape[1]
    slots = len(pairs)
    wide = pl.BlockSpec((width, units), lambda i, p: (p[0] ^ (i + done), 0))
    tall = pl.BlockSpec((units, width), lambda i, p: (0, p[0] ^ (i + done)))
    return pl.pallas_call(
        functools.partial(rest_kernel, n_expert, slots),
        grid_spec=pltpu.PrefetchScalarGridSpec(
            num_scalar_prefetch=1,
            grid=(slots,),
            in_specs=[column_block(rows, width, column) for column in range(2)] * slots
            + [wide, wide, tall] * 2
            + [whole_block(before.shape), column_block(rows, LANES, 4 * width // LANES)],
            out_specs=[
                whole_block((rows, 3 * units)),
                whole_block((rows, 3 * units)),
                whole_block((rows, LANES)),
            ],
            scratch_shapes=[pltpu.VMEM((6, rows, units), F32)],
        ),
        out_shape=[
            jax.ShapeDtypeStruct((rows, 3 * units), BF),
            jax.ShapeDtypeStruct((rows, 3 * units), BF),
            jax.ShapeDtypeStruct((rows, LANES), BF),
        ],
        compiler_params=params(
            4 * rows * width * slots + 24 * width * units + 120 * rows * units
        ),
        cost_estimate=forward_cost(rows, width, units, slots),
        name="forward_rest",
    )(place, *[p for pair in pairs for p in (pair, pair)], *weights, before, route_w)


def unit_kernel(tokens, slots, with_route, place, mine, other, *refs):
    if with_route:
        route, refs = refs[0], refs[1:]
    weights, outs = refs[:4], refs[4:]
    width, units = weights[0].shape
    step = pl.program_id(0)
    total = None
    for number, weight in enumerate(weights):
        acts = mine if number < 2 else other
        at = (number % 2) * units
        part = dot(acts[:, at : at + units], weight[...], 1, 1)
        total = part if total is None else total + part
    for slot in range(slots):

        @pl.when(step == slot)
        def _(slot=slot):
            for block, out in enumerate(outs):
                rows = pl.ds(block * tokens, tokens)
                value = total[block * tokens : (block + 1) * tokens]
                out[:, slot * width : (slot + 1) * width] = value.astype(out.dtype)
                if with_route and slot == 0:
                    out[:, slots * width :] = route[rows, :].astype(out.dtype)


def unit_product(place, mine, other, weights, group, tokens, width, route=None):
    rows = mine.shape[0]
    units = weights[0].shape[1]
    slots, top = len(group), group[0]
    wide = pl.BlockSpec((width, units), lambda i, p: (p[0] ^ (top - i), 0))
    acts = column_block(rows, 2 * units, 0)
    columns = slots * width + (0 if route is None else LANES)
    shapes = [
        jax.ShapeDtypeStruct((tokens, columns), F32 if block == 0 else BF)
        for block in range(rows // tokens)
    ]
    extra = [] if route is None else [route]
    return pl.pallas_call(
        functools.partial(unit_kernel, tokens, slots, route is not None),
        grid_spec=pltpu.PrefetchScalarGridSpec(
            num_scalar_prefetch=1,
            grid=(slots,),
            in_specs=[acts, acts] + [whole_block(r.shape) for r in extra] + [wide] * 4,
            out_specs=[whole_block(s.shape) for s in shapes],
        ),
        out_shape=shapes,
        compiler_params=params(
            16 * width * units + 16 * rows * units + (8 + 4 * slots) * rows * width
        ),
        cost_estimate=pl.CostEstimate(
            flops=8 * rows * width * units * slots,
            bytes_accessed=8 * width * units * slots + 3 * rows * width * slots,
            transcendentals=0,
        ),
        name="unit_product",
    )(place, mine, other, *extra, *weights)


def outer_kernel(pieces, n_source, rows, down, place, acts, got, *refs):
    n_slice = len(pieces)
    sources, refs = refs[:n_source], refs[n_source:]
    if down:
        penalty, out = refs[:2]
    else:
        gate_out, up_out = refs[:2]
    held, grads, sems = refs[-3:]
    width = held.shape[2]
    units = acts.shape[1] // 3
    step = pl.program_id(0)

    def copies(slot):
        out = []
        for number, (source, index, column, at) in enumerate(pieces[slot]):
            ref = sources[source]
            ref = ref if index is None else ref.at[index]
            out.append(
                pltpu.make_async_copy(
                    ref.at[:, pl.ds(column * width, width)],
                    held.at[slot, pl.ds(at, ref.shape[0])],
                    sems.at[slot, number],
                )
            )
        return out

    @pl.when(step == 0)
    def _():
        for slot in range(n_slice):
            for copy in copies(slot):
                copy.start()
        grads[:rows] = acts[...]
        grads[rows:] = got[...]

    for slot in range(n_slice):

        @pl.when(step == slot)
        def _(slot=slot):
            for copy in copies(slot):
                copy.wait()

    block = held[step]
    if down:
        value = dot(grads[:, 2 * units :], block, 0, 0)
        out[...] = (value + penalty[...]).astype(BF)
    else:
        value = dot(block, grads[:, : 2 * units], 0, 0)
        gate_out[...] = value[:, :units].astype(BF)
        up_out[...] = value[:, units:].astype(BF)


def outer_products(place, sources, pieces, acts, got, width, penalty=None):
    n_slice = len(pieces)
    rows = acts.shape[0]
    units = acts.shape[1] // 3
    full = n_slice * width
    down = penalty is not None
    wide = pl.BlockSpec((width, units), lambda s, p: (p[0] ^ s, 0))
    tall = pl.BlockSpec((units, width), lambda s, p: (0, p[0] ^ s))
    anywhere = pl.BlockSpec(memory_space=pl.ANY)
    return pl.pallas_call(
        functools.partial(outer_kernel, pieces, len(sources), rows, down),
        grid_spec=pltpu.PrefetchScalarGridSpec(
            num_scalar_prefetch=1,
            grid=(n_slice,),
            in_specs=[whole_block(acts.shape), whole_block(got.shape)]
            + [anywhere] * len(sources)
            + [tall] * down,
            out_specs=[tall] if down else [wide, wide],
            scratch_shapes=[
                pltpu.VMEM((n_slice, 2 * rows, width), BF),
                pltpu.VMEM((2 * rows, 3 * units), BF),
                pltpu.SemaphoreType.DMA((n_slice, max(len(p) for p in pieces))),
            ],
        ),
        out_shape=[jax.ShapeDtypeStruct((units, full), BF)]
        if down
        else [jax.ShapeDtypeStruct((full, units), BF)] * 2,
        compiler_params=params(58 * MIB),
        cost_estimate=pl.CostEstimate(
            flops=4 * rows * full * units * (1 if down else 2),
            bytes_accessed=full * (4 * rows + units * (6 if down else 4)),
            transcendentals=0,
        ),
        name="outer_down" if down else "outer_gate_up",
    )(place, acts, got, *sources, *([penalty] if down else []))


def repack(tail, count):
    lane = lax.broadcasted_iota(jnp.int32, tail.shape, 1)
    value = tail + pltpu.roll(tail, LANES - count, 1)
    high = value.astype(BF).astype(F32)
    low = pltpu.roll(value - high, count, 1)
    return jnp.where(lane < count, high, jnp.where(lane < 2 * count, low, 0.0))


def call_small(kernel, name, shapes, *args):
    size = sum(4 * math.prod(a.shape) for a in args) + sum(4 * math.prod(s.shape) for s in shapes)
    return pl.pallas_call(
        kernel,
        grid=(1,),
        in_specs=[whole_block(a.shape) for a in args],
        out_specs=[whole_block(s.shape) for s in shapes],
        out_shape=shapes,
        compiler_params=params(2 * size),
        cost_estimate=pl.CostEstimate(flops=size, bytes_accessed=size, transcendentals=0),
        name=name,
    )(*args)


def group_sum_kernel(group, n_got, n_expert, first, own, *refs):
    gots, refs = refs[:n_got], refs[n_got:]
    value = own[...]
    for got in gots:
        value = value + got[...].astype(F32)
    if first:
        width = (value.shape[1] - LANES) // len(group)
        pair = repack(value[:, len(group) * width :], n_expert).astype(BF)
        refs[-1][...] = pair
    else:
        width = value.shape[1] // len(group)
        pair, refs = refs[0][...], refs[1:]
    for at, slot in enumerate(group):
        out = refs[at]
        out[:, :width] = value[:, at * width : (at + 1) * width].astype(out.dtype)
        if slot > 0:
            out[:, width:] = pair


def group_sum(group, own, gots, pair, n_expert, width):
    tokens = own.shape[0]
    shapes = [
        jax.ShapeDtypeStruct((tokens, width + LANES), BF)
        if slot > 0
        else jax.ShapeDtypeStruct((tokens, width), F32)
        for slot in group
    ]
    first = pair is None
    if first:
        shapes.append(jax.ShapeDtypeStruct((tokens, LANES), BF))
    kernel = functools.partial(group_sum_kernel, group, len(gots), n_expert, first)
    out = call_small(kernel, "group_sum", shapes, own, *gots, *([] if first else [pair]))
    return out[: len(group)], (out[-1] if first else pair)


def final_sum_kernel(n_expert, own, pair, ids, *refs):
    fars, (grad, route) = refs[:-2], refs[-2:]
    width = own.shape[1]
    value, tail = own[...], pair[...].astype(F32)
    for far in fars:
        value = value + far[:, :width].astype(F32)
        tail = tail + far[:, width:].astype(F32)
    grad[...] = value.astype(BF)
    tail = tail + pltpu.roll(tail, LANES - n_expert, 1)
    lane = lax.broadcasted_iota(jnp.int32, tail.shape, 1)
    for k in range(route.shape[1]):
        chosen = jnp.logical_and(lane == ids[:, k : k + 1], lane < n_expert)
        route[:, k : k + 1] = jnp.sum(jnp.where(chosen, tail, 0.0), axis=1, keepdims=True)


def final_sum(own, fars, pair, ids, n_expert):
    shapes = [jax.ShapeDtypeStruct(own.shape, BF), jax.ShapeDtypeStruct(ids.shape, F32)]
    kernel = functools.partial(final_sum_kernel, n_expert)
    return call_small(kernel, "final_sum", shapes, own, pair, ids, *fars)


def per_device(
    n_expert,
    n_slice,
    tokens,
    cotangent,
    route_ids,
    route_weights,
    gate_weight,
    up_weight,
    down_weight,
    fisher,
    anchor,
):
    count, width = tokens.shape
    chips = n_expert // 2
    rows = chips * count
    lo = 1 << ((chips.bit_length() - 1) // 2)
    hi = chips // lo
    own_e, own_f = lax.axis_index("expert"), lax.axis_index("ffn")
    place = jnp.stack([own_f, own_e]).astype(jnp.int32)

    def over_expert(value, mask):
        return lax.ppermute(value, "expert", [(i, i ^ mask) for i in range(n_expert)])

    def over_lo(value, mask):
        return over_expert(value, 2 * mask)

    def over_hi(value, mask):
        return over_expert(value, 2 * lo * mask)

    def over_slice(value, mask):
        return lax.ppermute(value, "ffn", [(i, i ^ mask) for i in range(n_slice)])

    def collect(value, send, number, axis):
        return jnp.stack([value] + [send(value, m) for m in range(1, number)], axis=axis)

    named = route_ids[:, :, None] == jnp.arange(LANES, dtype=jnp.int32)[None, None, :]
    route_row = jnp.sum(
        jnp.where(named, route_weights.astype(F32)[:, :, None], 0.0), axis=1
    ).astype(BF)

    together = lax.optimization_barrier
    both = jnp.concatenate([tokens, cotangent], axis=1)
    masks = range(2, n_expert, 2)

    def to_chips(part):
        return [over_expert(part, m) for m in masks]

    def assemble(part, hops):
        return jnp.stack([part] + hops).reshape(rows, -1)

    hops, parts, both = together(
        (to_chips(both), [over_slice(both, s) for s in range(1, 3)], both)
    )
    near = [assemble(both, hops)]
    part = jnp.concatenate([*parts, route_row], axis=1)
    gate, up, down = gate_weight[0], up_weight[0], down_weight[0]
    penalty = fisher[0] * (down.astype(F32) - anchor[0])
    other = [over_expert(after(gate, both), 1)]
    other.append(over_expert(after(up, both), 1))
    hops, more, part, other, near, penalty = together(
        (
            to_chips(part),
            [over_slice(both, s) for s in range(3, n_slice)],
            part,
            other,
            near,
            penalty,
        )
    )
    near.append(assemble(part, hops))
    more_hops = [to_chips(v) for v in more]
    other.append(over_expert(after(down, *other), 1))
    weights = (gate, up, down, *other)
    acc = forward_near(place, *near, weights, width)
    got_near = [over_expert(v, 1) for v in near]
    more_hops, more, acc, got_near = together((more_hops, more, acc, got_near))
    rest = [assemble(v, h) for v, h in zip(more, more_hops)]
    acts, acts_other, route = forward_rest(
        place, rest, weights, acc, near[1], n_expert, width, 3
    )

    got_acts = over_expert(acts_other, 1)
    got_rest = tuple(over_expert(v, 1) for v in rest)
    ready = after(place, *got_rest)
    sources = (*near, *rest, *got_near, *got_rest)
    pieces = [
        tuple(
            ((0 if s == 0 else 1 if s < 3 else s - 1, None, which + 2 * (s == 2), 0),)
            for s in range(n_slice)
        )
        for which in range(2)
    ]
    own_count = len(near) + len(rest)
    pieces = [
        tuple(one + ((one[0][0] + own_count, *one[0][1:3], rows),) for one in side)
        for side in pieces
    ]

    projections = (weights[0], weights[1], weights[3], weights[4])
    slots = list(reversed(range(n_slice)))
    groups = [slots[: n_slice // 2], slots[n_slice // 2 :]]
    parts, late = [], ready
    for group in groups:
        outs = unit_product(
            late, acts, acts_other, projections, group, count, width, None if parts else route
        )
        parts.append(
            (outs[0], [over_expert(v, 2 * (block + 1)) for block, v in enumerate(outs[1:])])
        )
        late = after(late, got_acts)
    sends, pair = group_sum(groups[0], *parts[0], None, n_expert, width)
    fars = [over_slice(v, s) for s, v in zip(groups[0], sends)]
    late = after(place, *sends)
    grad_gate, grad_up = outer_products(late, sources, pieces[0], acts, got_acts, width)
    own, got = parts[1]
    sends, _ = group_sum(groups[1], after(own, grad_gate), got, pair, n_expert, width)
    fars += [over_slice(v, s) for s, v in zip(groups[1], sends) if s > 0]
    late = after(place, *sends)
    (grad_down,) = outer_products(
        late, sources, pieces[1], acts, got_acts, width, penalty
    )
    own = after(sends[-1], grad_down)
    grad_tokens, grad_route = final_sum(own, fars, pair, route_ids, n_expert)
    return (grad_tokens, grad_route, grad_gate[None], grad_up[None], grad_down[None])


def solution(mesh):
    return jax.shard_map(
        functools.partial(per_device, mesh.shape["expert"], mesh.shape["ffn"]),
        mesh=mesh,
        in_specs=(
            P("expert", "ffn"),
            P("expert", "ffn"),
            P("expert", None),
            P("expert", None),
            P("expert", None, "ffn"),
            P("expert", None, "ffn"),
            P("expert", "ffn", None),
            P("expert", "ffn", None),
            P("expert", "ffn", None),
        ),
        out_specs=(
            P("expert", "ffn"),
            P("expert", None),
            P("expert", None, "ffn"),
            P("expert", None, "ffn"),
            P("expert", "ffn", None),
        ),
        check_vma=False,
    )
```

time: 124 us -> 115 us (0.927)
  Pallas kernels: 42.1 us -> 28.5 us
  starting transfers between devices: 42.5 us -> 30.7 us
  local copies, waits for them, and re-layouts: 4.51 us -> 13.2 us
  waiting for transfers between devices: 25.5 us -> 31.8 us
    pallas_call x8 -> x5, Pallas kernels: 36.5 us -> 24.2 us  [the longest x2 14.7 us: outer_products(): pl.pallas_call(functools.partial(outer_kernel, pieces, len(sources), rows...]
    unnamed x35 -> x39, local copies, waits for them, and re-layouts: 3.49 us -> 12.3 us
    ppermute x30 -> x22, waiting for transfers between devices: 11.1 us -> 18.5 us  [over_expert(): lax.ppermute(value, 'expert', [(i, i ^ mask) for i in range(n_expert)])]
    mul x0 -> x1, other arithmetic: none -> 7.22 us  [per_device(): penalty = fisher[0] * (down.astype(F32) - anchor[0])]
    ppermute x30 -> x22, starting transfers between devices: 27 us -> 20.3 us  [over_expert(): lax.ppermute(value, 'expert', [(i, i ^ mask) for i in range(n_expert)])]
    another operation x6 -> x3, other arithmetic: 6.24 us -> 0.59 us  [assemble(): return jnp.stack([part] + hops).reshape(rows, -1)]
    ppermute x6, starting transfers between devices: 15.5 us -> 10.4 us  [over_slice(): return lax.ppermute(value, 'ffn', [(i, i ^ mask) for i in range(n_slice)])]
  transfers between devices with their start and end apart: 36 -> 28, of which waited for: 9 -> 8; matrix products, arithmetic and copies ran while one was open for 5% -> 8% of each run, Pallas kernels for 33% -> 24%
where the time goes in v3:
time: 115 us
  waiting for transfers between devices  31.8 us (28%)
  starting transfers between devices  30.7 us (27%)
  Pallas kernels  28.5 us (25%)
  local copies, waits for them, and re-layouts  13.2 us (11%)
  other arithmetic  9.41 us (8%)
    ppermute x22, starting transfers between devices, over_expert(): lax.ppermute(value, 'expert', [(i, i ^ mask) for i in range(n_expert)])  20.3 us
    ppermute x22, waiting for transfers between devices, over_expert(): lax.ppermute(value, 'expert', [(i, i ^ mask) for i in range(n_expert)])  18.5 us
    pallas_call x2, Pallas kernels, outer_products(): pl.pallas_call(functools.partial(outer_kernel, pieces, len(sources), rows...  14.7 us
    ppermute x6, waiting for transfers between devices, over_slice(): return lax.ppermute(value, 'ffn', [(i, i ^ mask) for i in range(n_slice)])  13.3 us
    unnamed x39, local copies, waits for them, and re-layouts  12.3 us
    ppermute x6, starting transfers between devices, over_slice(): return lax.ppermute(value, 'ffn', [(i, i ^ mask) for i in range(n_slice)])  10.4 us
    mul x1, other arithmetic, per_device(): penalty = fisher[0] * (down.astype(F32) - anchor[0])  7.22 us
    pallas_call x1, Pallas kernels, forward_near(): pl.pallas_call(forward_kernel, grid_spec=pltpu.PrefetchScalarGridSpec(num...  5.1 us
  transfers between devices with their start and end apart: 28, of which 8 were waited for; matrix products, arithmetic and copies ran while one was open for 8% of the time, Pallas kernels for 24%

profile of v3, /device:TPU:0, one launch (start us, length us, event | category | flops | bytes accessed | tf_op | source)
XLA Modules:
  0.0 114.6 jit_solution(1268551233049993186)
XLA Ops:
  0.6 0.9 constant_dynamic-update-slice_fusion.1
  1.5 0.9 constant_dynamic-update-slice_fusion
  2.5 4.1 %collective-permute-start.4 = (bf16[64,2048]{1,0:T(8,128)(2,1)S(1)}, bf16[64,2048]{1,0:T(8,128)(2,1)S(1)}, u32[]{:S(2)}, u32[]{:S(2)}) collective-permute-start(bf16[64,2048]{1,0:T(8,128)(2,1)S(1)} %constant_dynamic-update-slice_fusion), channel_id=1, source_target_pairs={{0,2},{1,3},{2,0},{3,1},{4,6},{5,7},{6,4},{7,5},{8,10},{9,11},{10,... | collective-permute-start | bytes 786440 | tf_op jit(solution)/shard_map/ppermute | solution.py:429
  6.6 1.6 %collective-permute-start.3 = (bf16[64,2048]{1,0:T(8,128)(2,1)S(1)}, bf16[64,2048]{1,0:T(8,128)(2,1)S(1)}, u32[]{:S(2)}, u32[]{:S(2)}) collective-permute-start(bf16[64,2048]{1,0:T(8,128)(2,1)S(1)} %constant_dynamic-update-slice_fusion), channel_id=1, source_target_pairs={{0,1},{1,0},{2,3},{3,2},{4,5},{5,4},{6,7},{7,6},{8,9},{9,8},{10,11... | collective-permute-start | bytes 786440 | tf_op jit(solution)/shard_map/ppermute | solution.py:429
  8.1 2.4 %collective-permute-start.2 = (bf16[64,2048]{1,0:T(8,128)(2,1)S(1)}, bf16[64,2048]{1,0:T(8,128)(2,1)S(1)}, u32[]{:S(2)}, u32[]{:S(2)}) collective-permute-start(bf16[64,2048]{1,0:T(8,128)(2,1)S(1)} %constant_dynamic-update-slice_fusion), channel_id=1, source_target_pairs={{0,24},{4,28},{8,16},{12,20},{16,8},{20,12},{24,0},{28,4},{1,25},{... | collective-permute-start | bytes 786440 | tf_op jit(solution)/shard_map/ppermute | solution.py:420
  10.6 0.5 collective-permute-start.1
  11.1 0.5 collective-permute-start
  11.6 0.7 convert_element_type.9
  12.3 6.3 %collective-permute-done.4 = bf16[64,2048]{1,0:T(8,128)(2,1)S(1)} collective-permute-done((bf16[64,2048]{1,0:T(8,128)(2,1)S(1)}, bf16[64,2048]{1,0:T(8,128)(2,1)S(1)}, u32[]{:S(2)}, u32[]{:S(2)}) %collective-permute-start.4) | collective-permute-done | bytes 262176 | tf_op jit(solution)/shard_map/ppermute | solution.py:429
  18.8 3.4 %collective-permute-done.1 = bf16[64,2048]{1,0:T(8,128)(2,1)S(1)} collective-permute-done((bf16[64,2048]{1,0:T(8,128)(2,1)S(1)}, bf16[64,2048]{1,0:T(8,128)(2,1)S(1)}, u32[]{:S(2)}, u32[]{:S(2)}) %collective-permute-start.1) | collective-permute-done | bytes 262176 | tf_op jit(solution)/shard_map/ppermute | solution.py:420
  22.3 0.5 collective-permute-start.10
  22.8 0.8 select_reduce_fusion
  23.9 2.1 %collective-permute-start.7 = (bf16[64,4224]{1,0:T(8,128)(2,1)S(1)}, bf16[64,4224]{1,0:T(8,128)(2,1)S(1)}, u32[]{:S(2)}, u32[]{:S(2)}) collective-permute-start(bf16[64,4224]{1,0:T(8,128)(2,1)S(1)} %pad_maximum_fusion.3), channel_id=1, source_target_pairs={{0,24},{4,28},{8,16},{12,20},{16,8},{20,12},{24,0},{28,4},{1,25},{... | collective-permute-start | bytes 1622024 | tf_op jit(solution)/shard_map/ppermute | solution.py:420
  26.1 0.9 collective-permute-start.6
  26.9 6.8 %collective-permute-done.8 = bf16[64,2048]{1,0:T(8,128)(2,1)S(1)} collective-permute-done((bf16[64,2048]{1,0:T(8,128)(2,1)S(1)}, bf16[64,2048]{1,0:T(8,128)(2,1)S(1)}, u32[]{:S(2)}, u32[]{:S(2)}) %collective-permute-start.8) | collective-permute-done | bytes 262176 | tf_op jit(solution)/shard_map/ppermute | solution.py:429
  33.8 1.5 %collective-permute-start.5 = (bf16[64,4224]{1,0:T(8,128)(2,1)S(1)}, bf16[64,4224]{1,0:T(8,128)(2,1)S(1)}, u32[]{:S(2)}, u32[]{:S(2)}) collective-permute-start(bf16[64,4224]{1,0:T(8,128)(2,1)S(1)} %pad_maximum_fusion.3), channel_id=1, source_target_pairs={{0,8},{4,12},{8,0},{12,4},{16,24},{20,28},{24,16},{28,20},{1,9},{5... | collective-permute-start | bytes 1622024 | tf_op jit(solution)/shard_map/ppermute | solution.py:420
  35.3 7.2 %fusion.refs_6_ = f32[256,4096]{1,0:T(8,128)} fusion(f32[1,256,4096]{2,1,0:T(8,128)} %param.17, f32[1,256,4096]{2,1,0:T(8,128)} %param.16, bf16[1,256,4096]{2,1,0:T(8,128)(2,1)} %param.15), kind=kLoop, calls=%fused_computation.1 | loop fusion | flops 3145728 | bytes 14680064 | tf_op jit(solution)/shard_map/mul | solution.py:455
  42.6 7.8 %collective-permute-done.6 = bf16[64,4224]{1,0:T(8,128)(2,1)S(1)} collective-permute-done((bf16[64,4224]{1,0:T(8,128)(2,1)S(1)}, bf16[64,4224]{1,0:T(8,128)(2,1)S(1)}, u32[]{:S(2)}, u32[]{:S(2)}) %collective-permute-start.6) | collective-permute-done | bytes 540704 | tf_op jit(solution)/shard_map/ppermute | solution.py:420
  50.9 0.9 copy-done.5
  51.8 0.7 copy-done.8
  52.5 0.5 collective-permute-start.15
  53.0 1.7 %collective-permute-start.13 = (bf16[64,2048]{1,0:T(8,128)(2,1)S(1)}, bf16[64,2048]{1,0:T(8,128)(2,1)S(1)}, u32[]{:S(2)}, u32[]{:S(2)}) collective-permute-start(bf16[64,2048]{1,0:T(8,128)(2,1)S(1)} %collective-permute-done.8), channel_id=1, source_target_pairs={{0,24},{4,28},{8,16},{12,20},{16,8},{20,12},{24,0},{28,4},{1,25},{... | collective-permute-start | bytes 786440 | tf_op jit(solution)/shard_map/ppermute | solution.py:420
  54.7 1.2 %collective-permute-start.12 = (bf16[64,2048]{1,0:T(8,128)(2,1)S(1)}, bf16[64,2048]{1,0:T(8,128)(2,1)S(1)}, u32[]{:S(2)}, u32[]{:S(2)}) collective-permute-start(bf16[64,2048]{1,0:T(8,128)(2,1)S(1)} %collective-permute-done.8), channel_id=1, source_target_pairs={{0,16},{4,20},{8,24},{12,28},{16,0},{20,4},{24,8},{28,12},{1,17},{... | collective-permute-start | bytes 786440 | tf_op jit(solution)/shard_map/ppermute | solution.py:420
  55.9 0.6 collective-permute-start.11
  56.6 1.6 %copy-done.1 = bf16[1,4096,256]{2,1,0:T(8,128)(2,1)S(1)} copy-done((bf16[1,4096,256]{2,1,0:T(8,128)(2,1)S(1)}, bf16[1,4096,256]{2,1,0:T(8,128)(2,1)}, u32[]{:S(2)}) %copy-start.1) | copy-done | bytes 2097176
  58.2 1.6 %copy-done.3 = bf16[1,4096,256]{2,1,0:T(8,128)(2,1)S(1)} copy-done((bf16[1,4096,256]{2,1,0:T(8,128)(2,1)S(1)}, bf16[1,4096,256]{2,1,0:T(8,128)(2,1)}, u32[]{:S(2)}) %copy-start.3) | copy-done | bytes 2097176
  59.8 1.6 %copy-done.6 = bf16[4096,256]{1,0:T(8,128)(2,1)S(1)} copy-done((bf16[4096,256]{1,0:T(8,128)(2,1)S(1)}, bf16[4096,256]{1,0:T(8,128)(2,1)}, u32[]{:S(2)}) %copy-start.6) | copy-done | bytes 2097176
  61.4 1.6 %copy-done.9 = bf16[4096,256]{1,0:T(8,128)(2,1)S(1)} copy-done((bf16[4096,256]{1,0:T(8,128)(2,1)S(1)}, bf16[4096,256]{1,0:T(8,128)(2,1)}, u32[]{:S(2)}) %copy-start.9) | copy-done | bytes 2097176
  63.0 5.1 %forward_near.1.refs_8_ = f32[6,256,256]{2,1,0:T(8,128)S(1)} custom-call(s32[2]{0:T(128)S(1)} %pad_add_fusion.place, bf16[256,2048]{1,0:T(8,128)(2,1)S(1)} %bitcast.51, bf16[256,4224]{1,0:T(8,128)(2,1)S(1)} %bitcast.31, bf16[4096,256]{1,0:T(8,128)(2,1)S(1)} %bitcast.36, bf16[4096,256]{1,0:T(8,128)(2,1)S(1)} %bitcast.41, ...), custom_call_target="tpu_custom_call" | custom-call | flops 2415919104 | bytes 14155776 | tf_op jit(solution)/shard_map/forward_near/pallas_call | solution.py:125
  68.1 0.9 copy-done.12
  69.4 1.7 %copy-done.7 = bf16[4096,256]{1,0:T(8,128)(2,1)S(1)} copy-done((bf16[4096,256]{1,0:T(8,128)(2,1)S(1)}, bf16[4096,256]{1,0:T(8,128)(2,1)}, u32[]{:S(2)}) %copy-start.7) | copy-done | bytes 2097176
  71.0 3.1 %forward_rest.1 = (bf16[256,768]{1,0:T(8,128)(2,1)S(1)}, bf16[256,768]{1,0:T(8,128)(2,1)S(1)}, bf16[256,128]{1,0:T(8,128)(2,1)S(1)}) custom-call(s32[2]{0:T(128)S(1)} %pad_add_fusion.place, bf16[256,2048]{1,0:T(8,128)(2,1)S(1)} %bitcast.46, bf16[256,2048]{1,0:T(8,128)(2,1)S(1)} %bitcast.47, bf16[4096,256]{1,0:T(8,128)(2,1)S(1)} %bitcast.37, ...), custom_call_target="tpu_custom_call" | custom-call | flops 805306368 | bytes 5767168 | tf_op jit(solution)/shard_map/forward_rest/pallas_call | solution.py:147
  74.2 2.2 %unit_product.3 = (f32[64,2176]{1,0:T(8,128)S(1)}, bf16[64,2176]{1,0:T(8,128)(2,1)S(1)}, bf16[64,2176]{1,0:T(8,128)(2,1)S(1)}, bf16[64,2176]{1,0:T(8,128)(2,1)S(1)}) custom-call(s32[2]{0:T(128)S(1)} %pad_add_fusion.place, bf16[256,768]{1,0:T(8,128)(2,1)S(1)} %get-tuple-element.81.mine.acts, bf16[256,768]{1,0:T(8,128)(2,1)S(1)} %get-tuple-element.79.other, ...), custom_call_target="tpu_custom_call" | custom-call | flops 1073741824 | bytes 5767168 | tf_op jit(solution)/shard_map/unit_product/pallas_call | solution.py:211
  76.4 1.5 %collective-permute-start.19 = (bf16[64,2176]{1,0:T(8,128)(2,1)S(1)}, bf16[64,2176]{1,0:T(8,128)(2,1)S(1)}, u32[]{:S(2)}, u32[]{:S(2)}) collective-permute-start(bf16[64,2176]{1,0:T(8,128)(2,1)S(1)} %get-tuple-element.85), channel_id=1, source_target_pairs={{0,8},{4,12},{8,0},{12,4},{16,24},{20,28},{24,16},{28,20},{1,9},{5... | collective-permute-start | bytes 835592 | tf_op jit(solution)/shard_map/ppermute | solution.py:420
  77.9 0.8 collective-permute-start.20
  78.7 1.3 %collective-permute-start.21 = (bf16[64,2176]{1,0:T(8,128)(2,1)S(1)}, bf16[64,2176]{1,0:T(8,128)(2,1)S(1)}, u32[]{:S(2)}, u32[]{:S(2)}) collective-permute-start(bf16[64,2176]{1,0:T(8,128)(2,1)S(1)} %get-tuple-element.87), channel_id=1, source_target_pairs={{0,24},{4,28},{8,16},{12,20},{16,8},{20,12},{24,0},{28,4},{1,25},{... | collective-permute-start | bytes 835592 | tf_op jit(solution)/shard_map/ppermute | solution.py:420
  80.0 2.2 %unit_product.2 = (f32[64,2048]{1,0:T(8,128)S(1)}, bf16[64,2048]{1,0:T(8,128)(2,1)S(1)}, bf16[64,2048]{1,0:T(8,128)(2,1)S(1)}, bf16[64,2048]{1,0:T(8,128)(2,1)S(1)}) custom-call(s32[2]{0:T(128)S(1)} %pad_add_fusion.place, bf16[256,768]{1,0:T(8,128)(2,1)S(1)} %get-tuple-element.81.mine.acts, bf16[256,768]{1,0:T(8,128)(2,1)S(1)} %get-tuple-element.79.other, ...), custom_call_target="tpu_custom_call" | custom-call | flops 1073741824 | bytes 5767168 | tf_op jit(solution)/shard_map/unit_product/pallas_call | solution.py:211
  82.2 1.5 %collective-permute-start.22 = (bf16[64,2048]{1,0:T(8,128)(2,1)S(1)}, bf16[64,2048]{1,0:T(8,128)(2,1)S(1)}, u32[]{:S(2)}, u32[]{:S(2)}) collective-permute-start(bf16[64,2048]{1,0:T(8,128)(2,1)S(1)} %get-tuple-element.95), channel_id=1, source_target_pairs={{0,8},{4,12},{8,0},{12,4},{16,24},{20,28},{24,16},{28,20},{1,9},{5... | collective-permute-start | bytes 786440 | tf_op jit(solution)/shard_map/ppermute | solution.py:420
  83.7 0.8 collective-permute-start.23
  84.5 1.4 %collective-permute-done.19.refs_0_ = bf16[64,2176]{1,0:T(8,128)(2,1)S(1)} collective-permute-done((bf16[64,2176]{1,0:T(8,128)(2,1)S(1)}, bf16[64,2176]{1,0:T(8,128)(2,1)S(1)}, u32[]{:S(2)}, u32[]{:S(2)}) %collective-permute-start.19) | collective-permute-done | bytes 278560 | tf_op jit(solution)/shard_map/ppermute | solution.py:420
  86.0 1.7 %collective-permute-start.24 = (bf16[64,2048]{1,0:T(8,128)(2,1)S(1)}, bf16[64,2048]{1,0:T(8,128)(2,1)S(1)}, u32[]{:S(2)}, u32[]{:S(2)}) collective-permute-start(bf16[64,2048]{1,0:T(8,128)(2,1)S(1)} %get-tuple-element.97), channel_id=1, source_target_pairs={{0,24},{4,28},{8,16},{12,20},{16,8},{20,12},{24,0},{28,4},{1,25},{... | collective-permute-start | bytes 786440 | tf_op jit(solution)/shard_map/ppermute | solution.py:420
  87.6 5.8 %collective-permute-done.20.refs_1_ = bf16[64,2176]{1,0:T(8,128)(2,1)S(1)} collective-permute-done((bf16[64,2176]{1,0:T(8,128)(2,1)S(1)}, bf16[64,2176]{1,0:T(8,128)(2,1)S(1)}, u32[]{:S(2)}, u32[]{:S(2)}) %collective-permute-start.20) | collective-permute-done | bytes 278560 | tf_op jit(solution)/shard_map/ppermute | solution.py:420
  93.6 3.6 %collective-permute-start.25 = (bf16[64,1152]{1,0:T(8,128)(2,1)S(1)}, bf16[64,1152]{1,0:T(8,128)(2,1)S(1)}, u32[]{:S(2)}, u32[]{:S(2)}) collective-permute-start(bf16[64,1152]{1,0:T(8,128)(2,1)S(1)} %get-tuple-element.88), channel_id=1, source_target_pairs={{0,3},{1,2},{2,1},{3,0},{4,7},{5,6},{6,5},{7,4},{8,11},{9,10},{10,... | collective-permute-start | bytes 442376 | tf_op jit(solution)/shard_map/ppermute | solution.py:429
  97.2 7.4 %outer_gate_up.1 = (bf16[4096,256]{1,0:T(8,128)(2,1)}, bf16[4096,256]{1,0:T(8,128)(2,1)}) custom-call(s32[2]{0:T(128)} %copy-done.14, bf16[256,768]{1,0:T(8,128)(2,1)} %copy-done.13, bf16[256,768]{1,0:T(8,128)(2,1)} %copy-done.16, bf16[256,2048]{1,0:T(8,128)(2,1)} %bitcast.52, bf16[256,4224]{1,0:T(8,128)(2,1)} %bitcast.33, bf16[256,2048]{1,0:T(8,128)(2,1)} %bitcast.48, ...), custom_call_target="tpu_custom_call" | custom-call | flops 2147483648 | bytes 8388608 | tf_op jit(solution)/shard_map/outer_gate_up/pallas_call | solution.py:292
  104.8 0.8 collective-permute-start.27
  105.7 7.3 %outer_down.1 = bf16[256,4096]{1,0:T(8,128)(2,1)} custom-call(s32[2]{0:T(128)} %copy-done.14, bf16[256,768]{1,0:T(8,128)(2,1)} %copy-done.13, bf16[256,768]{1,0:T(8,128)(2,1)} %copy-done.16, bf16[256,2048]{1,0:T(8,128)(2,1)} %bitcast.53, bf16[256,4224]{1,0:T(8,128)(2,1)} %bitcast.34, bf16[256,2048]{1,0:T(8,128)(2,1)} %bitcast.49, ...), custom_call_target="tpu_custom_call" | custom-call | flops 1073741824 | bytes 10485760 | tf_op jit(solution)/shard_map/outer_down/pallas_call | solution.py:292
  113.0 0.9 final_sum.1
  114.0 0.7 copy.19
  (65 shorter events, 2.1 us)
Async XLA Ops:
  2.5 16.1 %collective-permute-start.4 = (bf16[64,2048]{1,0:T(8,128)(2,1)S(1)}, bf16[64,2048]{1,0:T(8,128)(2,1)S(1)}, u32[]{:S(2)}, u32[]{:S(2)}) collective-permute-start(bf16[64,2048]{1,0:T(8,128)(2,1)S(1)} %constant_dynamic-update-slice_fusion), channel_id=1, source_target_pairs={{0,2},{1,3},{2,0},{3,1},{4,6},{5,7},{6,4},{7,5},{8,10},{9,11},{10,... | collective-permute-start | bytes 786440 | tf_op jit(solution)/shard_map/ppermute | solution.py:429
  6.6 12.2 %collective-permute-start.3 = (bf16[64,2048]{1,0:T(8,128)(2,1)S(1)}, bf16[64,2048]{1,0:T(8,128)(2,1)S(1)}, u32[]{:S(2)}, u32[]{:S(2)}) collective-permute-start(bf16[64,2048]{1,0:T(8,128)(2,1)S(1)} %constant_dynamic-update-slice_fusion), channel_id=1, source_target_pairs={{0,1},{1,0},{2,3},{3,2},{4,5},{5,4},{6,7},{7,6},{8,9},{9,8},{10,11... | collective-permute-start | bytes 786440 | tf_op jit(solution)/shard_map/ppermute | solution.py:429
  8.1 10.6 %collective-permute-start.2 = (bf16[64,2048]{1,0:T(8,128)(2,1)S(1)}, bf16[64,2048]{1,0:T(8,128)(2,1)S(1)}, u32[]{:S(2)}, u32[]{:S(2)}) collective-permute-start(bf16[64,2048]{1,0:T(8,128)(2,1)S(1)} %constant_dynamic-update-slice_fusion), channel_id=1, source_target_pairs={{0,24},{4,28},{8,16},{12,20},{16,8},{20,12},{24,0},{28,4},{1,25},{... | collective-permute-start | bytes 786440 | tf_op jit(solution)/shard_map/ppermute | solution.py:420
  10.6 11.6 %collective-permute-start.1 = (bf16[64,2048]{1,0:T(8,128)(2,1)S(1)}, bf16[64,2048]{1,0:T(8,128)(2,1)S(1)}, u32[]{:S(2)}, u32[]{:S(2)}) collective-permute-start(bf16[64,2048]{1,0:T(8,128)(2,1)S(1)} %constant_dynamic-update-slice_fusion), channel_id=1, source_target_pairs={{0,16},{4,20},{8,24},{12,28},{16,0},{20,4},{24,8},{28,12},{1,17},{... | collective-permute-start | bytes 786440 | tf_op jit(solution)/shard_map/ppermute | solution.py:420
  11.1 11.1 %collective-permute-start = (bf16[64,2048]{1,0:T(8,128)(2,1)S(1)}, bf16[64,2048]{1,0:T(8,128)(2,1)S(1)}, u32[]{:S(2)}, u32[]{:S(2)}) collective-permute-start(bf16[64,2048]{1,0:T(8,128)(2,1)S(1)} %constant_dynamic-update-slice_fusion), channel_id=1, source_target_pairs={{0,8},{4,12},{8,0},{12,4},{16,24},{20,28},{24,16},{28,20},{1,9},{5... | collective-permute-start | bytes 786440 | tf_op jit(solution)/shard_map/ppermute | solution.py:420
  22.2 28.2 %collective-permute-start.9 = (bf16[4096,256]{1,0:T(8,128)(2,1)}, bf16[4096,256]{1,0:T(8,128)(2,1)S(1)}, u32[]{:S(2)}, u32[]{:S(2)}) collective-permute-start(bf16[4096,256]{1,0:T(8,128)(2,1)} %bitcast.35), channel_id=1, source_target_pairs={{0,4},{4,0},{8,12},{12,8},{16,20},{20,16},{24,28},{28,24},{1,5},{5... | collective-permute-start | bytes 6291464 | tf_op jit(solution)/shard_map/ppermute | solution.py:420
  22.3 28.2 %collective-permute-start.10 = (bf16[4096,256]{1,0:T(8,128)(2,1)}, bf16[4096,256]{1,0:T(8,128)(2,1)S(1)}, u32[]{:S(2)}, u32[]{:S(2)}) collective-permute-start(bf16[4096,256]{1,0:T(8,128)(2,1)} %bitcast.40), channel_id=1, source_target_pairs={{0,4},{4,0},{8,12},{12,8},{16,20},{20,16},{24,28},{28,24},{1,5},{5... | collective-permute-start | bytes 6291464 | tf_op jit(solution)/shard_map/ppermute | solution.py:420
  23.6 10.2 %collective-permute-start.8 = (bf16[64,2048]{1,0:T(8,128)(2,1)S(1)}, bf16[64,2048]{1,0:T(8,128)(2,1)S(1)}, u32[]{:S(2)}, u32[]{:S(2)}) collective-permute-start(bf16[64,2048]{1,0:T(8,128)(2,1)S(1)} %constant_dynamic-update-slice_fusion), channel_id=1, source_target_pairs={{0,3},{1,2},{2,1},{3,0},{4,7},{5,6},{6,5},{7,4},{8,11},{9,10},{10,... | collective-permute-start | bytes 786440 | tf_op jit(solution)/shard_map/ppermute | solution.py:429
  23.9 18.7 %collective-permute-start.7 = (bf16[64,4224]{1,0:T(8,128)(2,1)S(1)}, bf16[64,4224]{1,0:T(8,128)(2,1)S(1)}, u32[]{:S(2)}, u32[]{:S(2)}) collective-permute-start(bf16[64,4224]{1,0:T(8,128)(2,1)S(1)} %pad_maximum_fusion.3), channel_id=1, source_target_pairs={{0,24},{4,28},{8,16},{12,20},{16,8},{20,12},{24,0},{28,4},{1,25},{... | collective-permute-start | bytes 1622024 | tf_op jit(solution)/shard_map/ppermute | solution.py:420
  26.1 24.4 %collective-permute-start.6 = (bf16[64,4224]{1,0:T(8,128)(2,1)S(1)}, bf16[64,4224]{1,0:T(8,128)(2,1)S(1)}, u32[]{:S(2)}, u32[]{:S(2)}) collective-permute-start(bf16[64,4224]{1,0:T(8,128)(2,1)S(1)} %pad_maximum_fusion.3), channel_id=1, source_target_pairs={{0,16},{4,20},{8,24},{12,28},{16,0},{20,4},{24,8},{28,12},{1,17},{... | collective-permute-start | bytes 1622024 | tf_op jit(solution)/shard_map/ppermute | solution.py:420
  33.8 16.7 %collective-permute-start.5 = (bf16[64,4224]{1,0:T(8,128)(2,1)S(1)}, bf16[64,4224]{1,0:T(8,128)(2,1)S(1)}, u32[]{:S(2)}, u32[]{:S(2)}) collective-permute-start(bf16[64,4224]{1,0:T(8,128)(2,1)S(1)} %pad_maximum_fusion.3), channel_id=1, source_target_pairs={{0,8},{4,12},{8,0},{12,4},{16,24},{20,28},{24,16},{28,20},{1,9},{5... | collective-permute-start | bytes 1622024 | tf_op jit(solution)/shard_map/ppermute | solution.py:420
  50.5 1.3 %copy-start.5 = (bf16[4096,256]{1,0:T(8,128)(2,1)}, bf16[4096,256]{1,0:T(8,128)(2,1)S(1)}, u32[]{:S(2)}) copy-start(bf16[4096,256]{1,0:T(8,128)(2,1)S(1)} %collective-permute-done.9.refs_3_.refs_5_.refs_2_) | copy-start | bytes 6291460
  50.5 2.0 %copy-start.8 = (bf16[4096,256]{1,0:T(8,128)(2,1)}, bf16[4096,256]{1,0:T(8,128)(2,1)S(1)}, u32[]{:S(2)}) copy-start(bf16[4096,256]{1,0:T(8,128)(2,1)S(1)} %collective-permute-done.10.refs_4_.refs_6_.refs_3_) | copy-start | bytes 6291460
  50.5 5.4 %collective-permute-start.14 = (bf16[256,4096]{1,0:T(8,128)(2,1)}, bf16[256,4096]{1,0:T(8,128)(2,1)}, u32[]{:S(2)}, u32[]{:S(2)}) collective-permute-start(bf16[256,4096]{1,0:T(8,128)(2,1)} %bitcast.10.refs_2_.refs_4_), channel_id=1, source_target_pairs={{0,4},{4,0},{8,12},{12,8},{16,20},{20,16},{24,28},{28,24},{1,5},{5... | collective-permute-start | bytes 6291464 | tf_op jit(solution)/shard_map/ppermute | solution.py:420
  52.5 16.9 %copy-start = (bf16[4,64,4224]{2,1,0:T(8,128)(2,1)}, bf16[4,64,4224]{2,1,0:T(8,128)(2,1)S(1)}, u32[]{:S(2)}) copy-start(bf16[4,64,4224]{2,1,0:T(8,128)(2,1)S(1)} %pad_maximum_fusion) | copy-start | bytes 6488068
  52.5 16.6 %collective-permute-start.16 = (bf16[256,4224]{1,0:T(8,128)(2,1)S(1)}, bf16[256,4224]{1,0:T(8,128)(2,1)}, u32[]{:S(2)}, u32[]{:S(2)}) collective-permute-start(bf16[256,4224]{1,0:T(8,128)(2,1)S(1)} %bitcast.30), channel_id=1, source_target_pairs={{0,4},{4,0},{8,12},{12,8},{16,20},{20,16},{24,28},{28,24},{1,5},{5... | collective-permute-start | bytes 6488072 | tf_op jit(solution)/shard_map/ppermute | solution.py:420
  52.5 16.6 %collective-permute-start.15 = (bf16[256,2048]{1,0:T(8,128)(2,1)S(1)}, bf16[256,2048]{1,0:T(8,128)(2,1)}, u32[]{:S(2)}, u32[]{:S(2)}) collective-permute-start(bf16[256,2048]{1,0:T(8,128)(2,1)S(1)} %bitcast.50), channel_id=1, source_target_pairs={{0,4},{4,0},{8,12},{12,8},{16,20},{20,16},{24,28},{28,24},{1,5},{5... | collective-permute-start | bytes 3145736 | tf_op jit(solution)/shard_map/ppermute | solution.py:420
  53.0 16.1 %collective-permute-start.13 = (bf16[64,2048]{1,0:T(8,128)(2,1)S(1)}, bf16[64,2048]{1,0:T(8,128)(2,1)S(1)}, u32[]{:S(2)}, u32[]{:S(2)}) collective-permute-start(bf16[64,2048]{1,0:T(8,128)(2,1)S(1)} %collective-permute-done.8), channel_id=1, source_target_pairs={{0,24},{4,28},{8,16},{12,20},{16,8},{20,12},{24,0},{28,4},{1,25},{... | collective-permute-start | bytes 786440 | tf_op jit(solution)/shard_map/ppermute | solution.py:420
  54.7 14.3 %collective-permute-start.12 = (bf16[64,2048]{1,0:T(8,128)(2,1)S(1)}, bf16[64,2048]{1,0:T(8,128)(2,1)S(1)}, u32[]{:S(2)}, u32[]{:S(2)}) collective-permute-start(bf16[64,2048]{1,0:T(8,128)(2,1)S(1)} %collective-permute-done.8), channel_id=1, source_target_pairs={{0,16},{4,20},{8,24},{12,28},{16,0},{20,4},{24,8},{28,12},{1,17},{... | collective-permute-start | bytes 786440 | tf_op jit(solution)/shard_map/ppermute | solution.py:420
  55.9 13.1 %collective-permute-start.11 = (bf16[64,2048]{1,0:T(8,128)(2,1)S(1)}, bf16[64,2048]{1,0:T(8,128)(2,1)S(1)}, u32[]{:S(2)}, u32[]{:S(2)}) collective-permute-start(bf16[64,2048]{1,0:T(8,128)(2,1)S(1)} %collective-permute-done.8), channel_id=1, source_target_pairs={{0,8},{4,12},{8,0},{12,4},{16,24},{20,28},{24,16},{28,20},{1,9},{5... | collective-permute-start | bytes 786440 | tf_op jit(solution)/shard_map/ppermute | solution.py:420
  56.6 1.6 %copy-start.1 = (bf16[1,4096,256]{2,1,0:T(8,128)(2,1)S(1)}, bf16[1,4096,256]{2,1,0:T(8,128)(2,1)}, u32[]{:S(2)}) copy-start(bf16[1,4096,256]{2,1,0:T(8,128)(2,1)} %param.13) | copy-start | bytes 6291460
  58.2 1.6 %copy-start.3 = (bf16[1,4096,256]{2,1,0:T(8,128)(2,1)S(1)}, bf16[1,4096,256]{2,1,0:T(8,128)(2,1)}, u32[]{:S(2)}) copy-start(bf16[1,4096,256]{2,1,0:T(8,128)(2,1)} %param.14) | copy-start | bytes 6291460
  59.8 1.6 %copy-start.6 = (bf16[4096,256]{1,0:T(8,128)(2,1)S(1)}, bf16[4096,256]{1,0:T(8,128)(2,1)}, u32[]{:S(2)}) copy-start(bf16[4096,256]{1,0:T(8,128)(2,1)} %copy-done.5) | copy-start | bytes 6291460
  61.4 1.6 %copy-start.9 = (bf16[4096,256]{1,0:T(8,128)(2,1)S(1)}, bf16[4096,256]{1,0:T(8,128)(2,1)}, u32[]{:S(2)}) copy-start(bf16[4096,256]{1,0:T(8,128)(2,1)} %copy-done.8) | copy-start | bytes 6291460
  63.0 17.0 %copy-start.14 = (s32[2]{0:T(128)}, s32[2]{0:T(128)S(1)}, u32[]{:S(2)}) copy-start(s32[2]{0:T(128)S(1)} %pad_add_fusion.place) | copy-start | bytes 28
  63.0 6.4 %copy-start.10 = (bf16[4096,256]{1,0:T(8,128)(2,1)S(1)}, bf16[4096,256]{1,0:T(8,128)(2,1)}, u32[]{:S(2)}) copy-start(bf16[4096,256]{1,0:T(8,128)(2,1)} %copy-done.8) | copy-start | bytes 6291460
  68.1 1.0 copy-start.12
  69.0 2.0 %copy-start.7 = (bf16[4096,256]{1,0:T(8,128)(2,1)S(1)}, bf16[4096,256]{1,0:T(8,128)(2,1)}, u32[]{:S(2)}) copy-start(bf16[4096,256]{1,0:T(8,128)(2,1)} %copy-done.5) | copy-start | bytes 6291460
  69.2 4.9 %copy-start.11 = (bf16[4,64,2048]{2,1,0:T(8,128)(2,1)}, bf16[4,64,2048]{2,1,0:T(8,128)(2,1)S(1)}, u32[]{:S(2)}) copy-start(bf16[4,64,2048]{2,1,0:T(8,128)(2,1)S(1)} %pad_maximum_fusion.2) | copy-start | bytes 3145732
  69.2 5.0 %copy-start.2 = (bf16[1,4096,256]{2,1,0:T(8,128)(2,1)S(1)}, bf16[1,4096,256]{2,1,0:T(8,128)(2,1)}, u32[]{:S(2)}) copy-start(bf16[1,4096,256]{2,1,0:T(8,128)(2,1)} %param.13) | copy-start | bytes 6291460
  69.2 5.0 %copy-start.4 = (bf16[1,4096,256]{2,1,0:T(8,128)(2,1)S(1)}, bf16[1,4096,256]{2,1,0:T(8,128)(2,1)}, u32[]{:S(2)}) copy-start(bf16[1,4096,256]{2,1,0:T(8,128)(2,1)} %param.14) | copy-start | bytes 6291460
  69.3 4.9 %collective-permute-start.17 = (bf16[256,2048]{1,0:T(8,128)(2,1)S(1)}, bf16[256,2048]{1,0:T(8,128)(2,1)S(1)}, u32[]{:S(2)}, u32[]{:S(2)}) collective-permute-start(bf16[256,2048]{1,0:T(8,128)(2,1)S(1)} %bitcast.45), channel_id=1, source_target_pairs={{0,4},{4,0},{8,12},{12,8},{16,20},{20,16},{24,28},{28,24},{1,5},{5... | collective-permute-start | bytes 3145736 | tf_op jit(solution)/shard_map/ppermute | solution.py:420
  74.1 5.9 %copy-start.13 = (bf16[256,768]{1,0:T(8,128)(2,1)}, bf16[256,768]{1,0:T(8,128)(2,1)S(1)}, u32[]{:S(2)}) copy-start(bf16[256,768]{1,0:T(8,128)(2,1)S(1)} %get-tuple-element.81.mine.acts) | copy-start | bytes 1179652
  74.1 5.9 %collective-permute-start.18 = (bf16[256,768]{1,0:T(8,128)(2,1)S(1)}, bf16[256,768]{1,0:T(8,128)(2,1)S(1)}, u32[]{:S(2)}, u32[]{:S(2)}) collective-permute-start(bf16[256,768]{1,0:T(8,128)(2,1)S(1)} %get-tuple-element.79.other), channel_id=1, source_target_pairs={{0,4},{4,0},{8,12},{12,8},{16,20},{20,16},{24,28},{28,24},{1,5},{5... | collective-permute-start | bytes 1179656 | tf_op jit(solution)/shard_map/ppermute | solution.py:420
  74.2 2.2 %copy-start.15 = (bf16[256,2048]{1,0:T(8,128)(2,1)}, bf16[256,2048]{1,0:T(8,128)(2,1)S(1)}, u32[]{:S(2)}) copy-start(bf16[256,2048]{1,0:T(8,128)(2,1)S(1)} %collective-permute-done.17.refs_5_) | copy-start | bytes 3145732
  76.4 9.5 %collective-permute-start.19 = (bf16[64,2176]{1,0:T(8,128)(2,1)S(1)}, bf16[64,2176]{1,0:T(8,128)(2,1)S(1)}, u32[]{:S(2)}, u32[]{:S(2)}) collective-permute-start(bf16[64,2176]{1,0:T(8,128)(2,1)S(1)} %get-tuple-element.85), channel_id=1, source_target_pairs={{0,8},{4,12},{8,0},{12,4},{16,24},{20,28},{24,16},{28,20},{1,9},{5... | collective-permute-start | bytes 835592 | tf_op jit(solution)/shard_map/ppermute | solution.py:420
  77.9 15.5 %collective-permute-start.20 = (bf16[64,2176]{1,0:T(8,128)(2,1)S(1)}, bf16[64,2176]{1,0:T(8,128)(2,1)S(1)}, u32[]{:S(2)}, u32[]{:S(2)}) collective-permute-start(bf16[64,2176]{1,0:T(8,128)(2,1)S(1)} %get-tuple-element.86), channel_id=1, source_target_pairs={{0,16},{4,20},{8,24},{12,28},{16,0},{20,4},{24,8},{28,12},{1,17},{... | collective-permute-start | bytes 835592 | tf_op jit(solution)/shard_map/ppermute | solution.py:420
  78.7 14.7 %collective-permute-start.21 = (bf16[64,2176]{1,0:T(8,128)(2,1)S(1)}, bf16[64,2176]{1,0:T(8,128)(2,1)S(1)}, u32[]{:S(2)}, u32[]{:S(2)}) collective-permute-start(bf16[64,2176]{1,0:T(8,128)(2,1)S(1)} %get-tuple-element.87), channel_id=1, source_target_pairs={{0,24},{4,28},{8,16},{12,20},{16,8},{20,12},{24,0},{28,4},{1,25},{... | collective-permute-start | bytes 835592 | tf_op jit(solution)/shard_map/ppermute | solution.py:420
  80.0 2.2 %copy-start.16 = (bf16[256,768]{1,0:T(8,128)(2,1)}, bf16[256,768]{1,0:T(8,128)(2,1)S(1)}, u32[]{:S(2)}) copy-start(bf16[256,768]{1,0:T(8,128)(2,1)S(1)} %collective-permute-done.18.got) | copy-start | bytes 1179652
  82.2 22.4 %collective-permute-start.22 = (bf16[64,2048]{1,0:T(8,128)(2,1)S(1)}, bf16[64,2048]{1,0:T(8,128)(2,1)S(1)}, u32[]{:S(2)}, u32[]{:S(2)}) collective-permute-start(bf16[64,2048]{1,0:T(8,128)(2,1)S(1)} %get-tuple-element.95), channel_id=1, source_target_pairs={{0,8},{4,12},{8,0},{12,4},{16,24},{20,28},{24,16},{28,20},{1,9},{5... | collective-permute-start | bytes 786440 | tf_op jit(solution)/shard_map/ppermute | solution.py:420
  83.7 21.0 %collective-permute-start.23 = (bf16[64,2048]{1,0:T(8,128)(2,1)S(1)}, bf16[64,2048]{1,0:T(8,128)(2,1)S(1)}, u32[]{:S(2)}, u32[]{:S(2)}) collective-permute-start(bf16[64,2048]{1,0:T(8,128)(2,1)S(1)} %get-tuple-element.96), channel_id=1, source_target_pairs={{0,16},{4,20},{8,24},{12,28},{16,0},{20,4},{24,8},{28,12},{1,17},{... | collective-permute-start | bytes 786440 | tf_op jit(solution)/shard_map/ppermute | solution.py:420
  86.0 18.7 %collective-permute-start.24 = (bf16[64,2048]{1,0:T(8,128)(2,1)S(1)}, bf16[64,2048]{1,0:T(8,128)(2,1)S(1)}, u32[]{:S(2)}, u32[]{:S(2)}) collective-permute-start(bf16[64,2048]{1,0:T(8,128)(2,1)S(1)} %get-tuple-element.97), channel_id=1, source_target_pairs={{0,24},{4,28},{8,16},{12,20},{16,8},{20,12},{24,0},{28,4},{1,25},{... | collective-permute-start | bytes 786440 | tf_op jit(solution)/shard_map/ppermute | solution.py:420
  93.6 19.4 %collective-permute-start.25 = (bf16[64,1152]{1,0:T(8,128)(2,1)S(1)}, bf16[64,1152]{1,0:T(8,128)(2,1)S(1)}, u32[]{:S(2)}, u32[]{:S(2)}) collective-permute-start(bf16[64,1152]{1,0:T(8,128)(2,1)S(1)} %get-tuple-element.88), channel_id=1, source_target_pairs={{0,3},{1,2},{2,1},{3,0},{4,7},{5,6},{6,5},{7,4},{8,11},{9,10},{10,... | collective-permute-start | bytes 442376 | tf_op jit(solution)/shard_map/ppermute | solution.py:429
  97.2 8.4 %copy-start.17 = (s32[64,4]{0,1:T(4,128)S(1)}, s32[64,4]{0,1:T(4,128)}, u32[]{:S(2)}) copy-start(s32[64,4]{0,1:T(4,128)} %param.11) | copy-start | bytes 3076
  97.2 15.8 %collective-permute-start.26 = (bf16[64,1152]{1,0:T(8,128)(2,1)S(1)}, bf16[64,1152]{1,0:T(8,128)(2,1)S(1)}, u32[]{:S(2)}, u32[]{:S(2)}) collective-permute-start(bf16[64,1152]{1,0:T(8,128)(2,1)S(1)} %get-tuple-element.89), channel_id=1, source_target_pairs={{0,2},{1,3},{2,0},{3,1},{4,6},{5,7},{6,4},{7,5},{8,10},{9,11},{10,... | collective-permute-start | bytes 442376 | tf_op jit(solution)/shard_map/ppermute | solution.py:429
  104.8 8.2 %collective-permute-start.27 = (bf16[64,1152]{1,0:T(8,128)(2,1)S(1)}, bf16[64,1152]{1,0:T(8,128)(2,1)S(1)}, u32[]{:S(2)}, u32[]{:S(2)}) collective-permute-start(bf16[64,1152]{1,0:T(8,128)(2,1)S(1)} %get-tuple-element.100), channel_id=1, source_target_pairs={{0,1},{1,0},{2,3},{3,2},{4,5},{5,4},{6,7},{7,6},{8,9},{9,8},{10,11... | collective-permute-start | bytes 442376 | tf_op jit(solution)/shard_map/ppermute | solution.py:429

commit v4 on v3

--- a/solution.py
+++ b/solution.py
@@ -440,15 +440,15 @@
     both = jnp.concatenate([tokens, cotangent], axis=1)
     masks = range(2, n_expert, 2)
 
-    def to_chips(part):
-        return [over_expert(part, m) for m in masks]
+    def to_chips(part, before=()):
+        near = [over_expert(part, m) for m in masks[:-1]]
+        return near + [over_expert(after(part, *before) if before else part, masks[-1])]
 
     def assemble(part, hops):
         return jnp.stack([part] + hops).reshape(rows, -1)
 
-    hops, parts, both = together(
-        (to_chips(both), [over_slice(both, s) for s in range(1, 3)], both)
-    )
+    parts = [over_slice(both, s) for s in range(2, 0, -1)][::-1]
+    hops, parts, both = together((to_chips(both), parts, both))
     near = [assemble(both, hops)]
     part = jnp.concatenate([*parts, route_row], axis=1)
     gate, up, down = gate_weight[0], up_weight[0], down_weight[0]
@@ -457,7 +457,7 @@
     other.append(over_expert(after(up, both), 1))
     hops, more, part, other, near, penalty = together(
         (
-            to_chips(part),
+            to_chips(part, other),
             [over_slice(both, s) for s in range(3, n_slice)],
             part,
             other,
@@ -506,18 +506,17 @@
             (outs[0], [over_expert(v, 2 * (block + 1)) for block, v in enumerate(outs[1:])])
         )
         late = after(late, got_acts)
-    sends, pair = group_sum(groups[0], *parts[0], None, n_expert, width)
+    late = after(place, parts[1][0])
+    (grad_down,) = outer_products(late, sources, pieces[1], acts, got_acts, width, penalty)
+    own, got = parts[0]
+    sends, pair = group_sum(groups[0], after(own, grad_down), got, None, n_expert, width)
     fars = [over_slice(v, s) for s, v in zip(groups[0], sends)]
+    own, got = parts[1]
+    sends, _ = group_sum(groups[1], after(own, *sends), got, pair, n_expert, width)
+    fars += [over_slice(v, s) for s, v in zip(groups[1], sends) if s > 0]
     late = after(place, *sends)
     grad_gate, grad_up = outer_products(late, sources, pieces[0], acts, got_acts, width)
-    own, got = parts[1]
-    sends, _ = group_sum(groups[1], after(own, grad_gate), got, pair, n_expert, width)
-    fars += [over_slice(v, s) for s, v in zip(groups[1], sends) if s > 0]
-    late = after(place, *sends)
-    (grad_down,) = outer_products(
-        late, sources, pieces[1], acts, got_acts, width, penalty
-    )
-    own = after(sends[-1], grad_down)
+    own = after(sends[-1], grad_gate)
     grad_tokens, grad_route = final_sum(own, fars, pair, route_ids, n_expert)
     return (grad_tokens, grad_route, grad_gate[None], grad_up[None], grad_down[None])
 

time: 115 us -> 114 us (level)
  waiting for transfers between devices: 31.8 us -> 29.8 us
    ppermute x6, waiting for transfers between devices: 13.3 us -> 7.69 us  [over_slice(): return lax.ppermute(value, 'ffn', [(i, i ^ mask) for i in range(n_slice)])]
    ppermute x22, waiting for transfers between devices: 18.5 us -> 22.2 us  [over_expert(): lax.ppermute(value, 'expert', [(i, i ^ mask) for i in range(n_expert)])]
  transfers between devices with their start and end apart: 28 -> 28, of which waited for: 8 -> 11; matrix products, arithmetic and copies ran while one was open for 8% -> 8% of each run, Pallas kernels for 24% -> 25%
where the time goes in v4:
time: 114 us; the launch traced here: 113 us
  starting transfers between devices  30.4 us (27%)
  waiting for transfers between devices  29.8 us (26%)
  Pallas kernels  29.3 us (26%)
  local copies, waits for them, and re-layouts  13.3 us (12%)
  other arithmetic  9.41 us (8%)
    ppermute x22, waiting for transfers between devices, over_expert(): lax.ppermute(value, 'expert', [(i, i ^ mask) for i in range(n_expert)])  22.2 us
    ppermute x22, starting transfers between devices, over_expert(): lax.ppermute(value, 'expert', [(i, i ^ mask) for i in range(n_expert)])  20.5 us
    pallas_call x2, Pallas kernels, outer_products(): pl.pallas_call(functools.partial(outer_kernel, pieces, len(sources), rows...  14.6 us
    unnamed x39, local copies, waits for them, and re-layouts  12.3 us
    ppermute x6, starting transfers between devices, over_slice(): return lax.ppermute(value, 'ffn', [(i, i ^ mask) for i in range(n_slice)])  9.88 us
    ppermute x6, waiting for transfers between devices, over_slice(): return lax.ppermute(value, 'ffn', [(i, i ^ mask) for i in range(n_slice)])  7.69 us
    mul x1, other arithmetic, per_device(): penalty = fisher[0] * (down.astype(F32) - anchor[0])  7.22 us
    pallas_call x2, Pallas kernels, unit_product(): pl.pallas_call(functools.partial(unit_kernel, tokens, slots, route is not...  5.26 us
  transfers between devices with their start and end apart: 28, of which 11 were waited for; matrix products, arithmetic and copies ran while one was open for 8% of the time, Pallas kernels for 25%

profile of v4, /device:TPU:0, one launch (start us, length us, event | category | flops | bytes accessed | tf_op | source)
XLA Modules:
  0.0 113.2 jit_solution(3637431928212480026)
XLA Ops:
  0.6 0.9 constant_dynamic-update-slice_fusion.1
  1.5 0.9 constant_dynamic-update-slice_fusion
  2.5 4.1 %collective-permute-start.4 = (bf16[64,2048]{1,0:T(8,128)(2,1)S(1)}, bf16[64,2048]{1,0:T(8,128)(2,1)S(1)}, u32[]{:S(2)}, u32[]{:S(2)}) collective-permute-start(bf16[64,2048]{1,0:T(8,128)(2,1)S(1)} %constant_dynamic-update-slice_fusion), channel_id=1, source_target_pairs={{0,2},{1,3},{2,0},{3,1},{4,6},{5,7},{6,4},{7,5},{8,10},{9,11},{10,... | collective-permute-start | bytes 786440 | tf_op jit(solution)/shard_map/ppermute | solution.py:429
  6.6 1.6 %collective-permute-start.3 = (bf16[64,2048]{1,0:T(8,128)(2,1)S(1)}, bf16[64,2048]{1,0:T(8,128)(2,1)S(1)}, u32[]{:S(2)}, u32[]{:S(2)}) collective-permute-start(bf16[64,2048]{1,0:T(8,128)(2,1)S(1)} %constant_dynamic-update-slice_fusion), channel_id=1, source_target_pairs={{0,1},{1,0},{2,3},{3,2},{4,5},{5,4},{6,7},{7,6},{8,9},{9,8},{10,11... | collective-permute-start | bytes 786440 | tf_op jit(solution)/shard_map/ppermute | solution.py:429
  8.1 2.4 %collective-permute-start.2 = (bf16[64,2048]{1,0:T(8,128)(2,1)S(1)}, bf16[64,2048]{1,0:T(8,128)(2,1)S(1)}, u32[]{:S(2)}, u32[]{:S(2)}) collective-permute-start(bf16[64,2048]{1,0:T(8,128)(2,1)S(1)} %constant_dynamic-update-slice_fusion), channel_id=1, source_target_pairs={{0,24},{4,28},{8,16},{12,20},{16,8},{20,12},{24,0},{28,4},{1,25},{... | collective-permute-start | bytes 786440 | tf_op jit(solution)/shard_map/ppermute | solution.py:420
  11.1 0.5 collective-permute-start
  11.6 7.0 %collective-permute-done.4 = bf16[64,2048]{1,0:T(8,128)(2,1)S(1)} collective-permute-done((bf16[64,2048]{1,0:T(8,128)(2,1)S(1)}, bf16[64,2048]{1,0:T(8,128)(2,1)S(1)}, u32[]{:S(2)}, u32[]{:S(2)}) %collective-permute-start.4) | collective-permute-done | bytes 262176 | tf_op jit(solution)/shard_map/ppermute | solution.py:429
  18.8 3.4 %collective-permute-done.1 = bf16[64,2048]{1,0:T(8,128)(2,1)S(1)} collective-permute-done((bf16[64,2048]{1,0:T(8,128)(2,1)S(1)}, bf16[64,2048]{1,0:T(8,128)(2,1)S(1)}, u32[]{:S(2)}, u32[]{:S(2)}) %collective-permute-start.1) | collective-permute-done | bytes 262176 | tf_op jit(solution)/shard_map/ppermute | solution.py:420
  22.3 0.5 collective-permute-start.8
  22.8 0.7 convert_element_type.9
  23.4 0.8 select_reduce_fusion
  24.6 1.5 %collective-permute-start.6 = (bf16[64,4224]{1,0:T(8,128)(2,1)S(1)}, bf16[64,4224]{1,0:T(8,128)(2,1)S(1)}, u32[]{:S(2)}, u32[]{:S(2)}) collective-permute-start(bf16[64,4224]{1,0:T(8,128)(2,1)S(1)} %pad_maximum_fusion.3), channel_id=1, source_target_pairs={{0,16},{4,20},{8,24},{12,28},{16,0},{20,4},{24,8},{28,12},{1,17},{... | collective-permute-start | bytes 1622024 | tf_op jit(solution)/shard_map/ppermute | solution.py:420
  26.1 1.2 %collective-permute-start.5 = (bf16[64,4224]{1,0:T(8,128)(2,1)S(1)}, bf16[64,4224]{1,0:T(8,128)(2,1)S(1)}, u32[]{:S(2)}, u32[]{:S(2)}) collective-permute-start(bf16[64,4224]{1,0:T(8,128)(2,1)S(1)} %pad_maximum_fusion.3), channel_id=1, source_target_pairs={{0,8},{4,12},{8,0},{12,4},{16,24},{20,28},{24,16},{28,20},{1,9},{5... | collective-permute-start | bytes 1622024 | tf_op jit(solution)/shard_map/ppermute | solution.py:420
  27.3 1.3 %copy-done.5 = bf16[4096,256]{1,0:T(8,128)(2,1)} copy-done((bf16[4096,256]{1,0:T(8,128)(2,1)}, bf16[4096,256]{1,0:T(8,128)(2,1)S(1)}, u32[]{:S(2)}) %copy-start.5) | copy-done | bytes 2097176
  28.6 1.0 collective-permute-done.8.refs_4_.refs_6_.refs_3_
  29.6 1.3 %copy-done.8 = bf16[4096,256]{1,0:T(8,128)(2,1)} copy-done((bf16[4096,256]{1,0:T(8,128)(2,1)}, bf16[4096,256]{1,0:T(8,128)(2,1)S(1)}, u32[]{:S(2)}) %copy-start.8) | copy-done | bytes 2097176
  30.9 1.6 %collective-permute-start.9 = (bf16[64,4224]{1,0:T(8,128)(2,1)S(1)}, bf16[64,4224]{1,0:T(8,128)(2,1)S(1)}, u32[]{:S(2)}, u32[]{:S(2)}) collective-permute-start(bf16[64,4224]{1,0:T(8,128)(2,1)S(1)} %pad_maximum_fusion.3), channel_id=1, source_target_pairs={{0,24},{4,28},{8,16},{12,20},{16,8},{20,12},{24,0},{28,4},{1,25},{... | collective-permute-start | bytes 1622024 | tf_op jit(solution)/shard_map/ppermute | solution.py:420
  32.6 7.2 %fusion.refs_6_ = f32[256,4096]{1,0:T(8,128)} fusion(f32[1,256,4096]{2,1,0:T(8,128)} %param.17, f32[1,256,4096]{2,1,0:T(8,128)} %param.16, bf16[1,256,4096]{2,1,0:T(8,128)(2,1)} %param.15), kind=kLoop, calls=%fused_computation.1 | loop fusion | flops 3145728 | bytes 14680064 | tf_op jit(solution)/shard_map/mul | solution.py:455
  40.0 1.3 %collective-permute-done.5 = bf16[64,4224]{1,0:T(8,128)(2,1)S(1)} collective-permute-done((bf16[64,4224]{1,0:T(8,128)(2,1)S(1)}, bf16[64,4224]{1,0:T(8,128)(2,1)S(1)}, u32[]{:S(2)}, u32[]{:S(2)}) %collective-permute-start.5) | collective-permute-done | bytes 540704 | tf_op jit(solution)/shard_map/ppermute | solution.py:420
  41.3 10.1 %collective-permute-done.9 = bf16[64,4224]{1,0:T(8,128)(2,1)S(1)} collective-permute-done((bf16[64,4224]{1,0:T(8,128)(2,1)S(1)}, bf16[64,4224]{1,0:T(8,128)(2,1)S(1)}, u32[]{:S(2)}, u32[]{:S(2)}) %collective-permute-start.9) | collective-permute-done | bytes 540704 | tf_op jit(solution)/shard_map/ppermute | solution.py:420
  51.7 0.6 collective-permute-start.16
  52.4 2.1 %collective-permute-start.13 = (bf16[64,2048]{1,0:T(8,128)(2,1)S(1)}, bf16[64,2048]{1,0:T(8,128)(2,1)S(1)}, u32[]{:S(2)}, u32[]{:S(2)}) collective-permute-start(bf16[64,2048]{1,0:T(8,128)(2,1)S(1)} %collective-permute-done.10), channel_id=1, source_target_pairs={{0,24},{4,28},{8,16},{12,20},{16,8},{20,12},{24,0},{28,4},{1,25},{... | collective-permute-start | bytes 786440 | tf_op jit(solution)/shard_map/ppermute | solution.py:420
  54.5 0.9 collective-permute-start.12
  55.3 0.6 collective-permute-done.14.refs_5_.refs_7_
  55.9 1.5 %collective-permute-start.11 = (bf16[64,2048]{1,0:T(8,128)(2,1)S(1)}, bf16[64,2048]{1,0:T(8,128)(2,1)S(1)}, u32[]{:S(2)}, u32[]{:S(2)}) collective-permute-start(bf16[64,2048]{1,0:T(8,128)(2,1)S(1)} %collective-permute-done.10), channel_id=1, source_target_pairs={{0,8},{4,12},{8,0},{12,4},{16,24},{20,28},{24,16},{28,20},{1,9},{5... | collective-permute-start | bytes 786440 | tf_op jit(solution)/shard_map/ppermute | solution.py:420
  57.5 1.6 %copy-done.1 = bf16[1,4096,256]{2,1,0:T(8,128)(2,1)S(1)} copy-done((bf16[1,4096,256]{2,1,0:T(8,128)(2,1)S(1)}, bf16[1,4096,256]{2,1,0:T(8,128)(2,1)}, u32[]{:S(2)}) %copy-start.1) | copy-done | bytes 2097176
  59.1 1.6 %copy-done.3 = bf16[1,4096,256]{2,1,0:T(8,128)(2,1)S(1)} copy-done((bf16[1,4096,256]{2,1,0:T(8,128)(2,1)S(1)}, bf16[1,4096,256]{2,1,0:T(8,128)(2,1)}, u32[]{:S(2)}) %copy-start.3) | copy-done | bytes 2097176
  60.7 1.6 %copy-done.6 = bf16[4096,256]{1,0:T(8,128)(2,1)S(1)} copy-done((bf16[4096,256]{1,0:T(8,128)(2,1)S(1)}, bf16[4096,256]{1,0:T(8,128)(2,1)}, u32[]{:S(2)}) %copy-start.6) | copy-done | bytes 2097176
  62.3 1.6 %copy-done.9 = bf16[4096,256]{1,0:T(8,128)(2,1)S(1)} copy-done((bf16[4096,256]{1,0:T(8,128)(2,1)S(1)}, bf16[4096,256]{1,0:T(8,128)(2,1)}, u32[]{:S(2)}) %copy-start.9) | copy-done | bytes 2097176
  63.8 5.1 %forward_near.1.refs_8_ = f32[6,256,256]{2,1,0:T(8,128)S(1)} custom-call(s32[2]{0:T(128)S(1)} %pad_add_fusion.place, bf16[256,2048]{1,0:T(8,128)(2,1)S(1)} %bitcast.51, bf16[256,4224]{1,0:T(8,128)(2,1)S(1)} %bitcast.31, bf16[4096,256]{1,0:T(8,128)(2,1)S(1)} %bitcast.36, bf16[4096,256]{1,0:T(8,128)(2,1)S(1)} %bitcast.41, ...), custom_call_target="tpu_custom_call" | custom-call | flops 2415919104 | bytes 14155776 | tf_op jit(solution)/shard_map/forward_near/pallas_call | solution.py:125
  69.3 1.6 %copy-done.7 = bf16[4096,256]{1,0:T(8,128)(2,1)S(1)} copy-done((bf16[4096,256]{1,0:T(8,128)(2,1)S(1)}, bf16[4096,256]{1,0:T(8,128)(2,1)}, u32[]{:S(2)}) %copy-start.7) | copy-done | bytes 2097176
  70.9 3.1 %forward_rest.1 = (bf16[256,768]{1,0:T(8,128)(2,1)S(1)}, bf16[256,768]{1,0:T(8,128)(2,1)S(1)}, bf16[256,128]{1,0:T(8,128)(2,1)S(1)}) custom-call(s32[2]{0:T(128)S(1)} %pad_add_fusion.place, bf16[256,2048]{1,0:T(8,128)(2,1)S(1)} %bitcast.46, bf16[256,2048]{1,0:T(8,128)(2,1)S(1)} %bitcast.47, bf16[4096,256]{1,0:T(8,128)(2,1)S(1)} %bitcast.37, ...), custom_call_target="tpu_custom_call" | custom-call | flops 805306368 | bytes 5767168 | tf_op jit(solution)/shard_map/forward_rest/pallas_call | solution.py:147
  74.1 2.2 %unit_product.3 = (f32[64,2176]{1,0:T(8,128)S(1)}, bf16[64,2176]{1,0:T(8,128)(2,1)S(1)}, bf16[64,2176]{1,0:T(8,128)(2,1)S(1)}, bf16[64,2176]{1,0:T(8,128)(2,1)S(1)}) custom-call(s32[2]{0:T(128)S(1)} %pad_add_fusion.place, bf16[256,768]{1,0:T(8,128)(2,1)S(1)} %get-tuple-element.84.mine.acts, bf16[256,768]{1,0:T(8,128)(2,1)S(1)} %get-tuple-element.82.other, ...), custom_call_target="tpu_custom_call" | custom-call | flops 1073741824 | bytes 5767168 | tf_op jit(solution)/shard_map/unit_product/pallas_call | solution.py:211
  76.4 0.6 collective-permute-start.19
  77.0 1.4 %collective-permute-start.20 = (bf16[64,2176]{1,0:T(8,128)(2,1)S(1)}, bf16[64,2176]{1,0:T(8,128)(2,1)S(1)}, u32[]{:S(2)}, u32[]{:S(2)}) collective-permute-start(bf16[64,2176]{1,0:T(8,128)(2,1)S(1)} %get-tuple-element.94), channel_id=1, source_target_pairs={{0,16},{4,20},{8,24},{12,28},{16,0},{20,4},{24,8},{28,12},{1,17},{... | collective-permute-start | bytes 835592 | tf_op jit(solution)/shard_map/ppermute | solution.py:420
  78.4 1.5 %collective-permute-start.21 = (bf16[64,2176]{1,0:T(8,128)(2,1)S(1)}, bf16[64,2176]{1,0:T(8,128)(2,1)S(1)}, u32[]{:S(2)}, u32[]{:S(2)}) collective-permute-start(bf16[64,2176]{1,0:T(8,128)(2,1)S(1)} %get-tuple-element.95), channel_id=1, source_target_pairs={{0,24},{4,28},{8,16},{12,20},{16,8},{20,12},{24,0},{28,4},{1,25},{... | collective-permute-start | bytes 835592 | tf_op jit(solution)/shard_map/ppermute | solution.py:420
  79.9 3.1 %unit_product.2 = (f32[64,2048]{1,0:T(8,128)S(1)}, bf16[64,2048]{1,0:T(8,128)(2,1)}, bf16[64,2048]{1,0:T(8,128)(2,1)}, bf16[64,2048]{1,0:T(8,128)(2,1)}) custom-call(s32[2]{0:T(128)S(1)} %pad_add_fusion.place, bf16[256,768]{1,0:T(8,128)(2,1)S(1)} %get-tuple-element.84.mine.acts, bf16[256,768]{1,0:T(8,128)(2,1)S(1)} %get-tuple-element.82.other, ...), custom_call_target="tpu_custom_call" | custom-call | flops 1073741824 | bytes 5767168 | tf_op jit(solution)/shard_map/unit_product/pallas_call | solution.py:211
  83.0 0.7 collective-permute-start.22
  83.7 1.3 %collective-permute-start.23 = (bf16[64,2048]{1,0:T(8,128)(2,1)}, bf16[64,2048]{1,0:T(8,128)(2,1)S(1)}, u32[]{:S(2)}, u32[]{:S(2)}) collective-permute-start(bf16[64,2048]{1,0:T(8,128)(2,1)} %get-tuple-element.100), channel_id=1, source_target_pairs={{0,16},{4,20},{8,24},{12,28},{16,0},{20,4},{24,8},{28,12},{1,17},{... | collective-permute-start | bytes 786440 | tf_op jit(solution)/shard_map/ppermute | solution.py:420
  85.0 0.9 collective-permute-done.19.refs_0_
  85.9 1.4 %collective-permute-start.24 = (bf16[64,2048]{1,0:T(8,128)(2,1)}, bf16[64,2048]{1,0:T(8,128)(2,1)S(1)}, u32[]{:S(2)}, u32[]{:S(2)}) collective-permute-start(bf16[64,2048]{1,0:T(8,128)(2,1)} %get-tuple-element.101), channel_id=1, source_target_pairs={{0,24},{4,28},{8,16},{12,20},{16,8},{20,12},{24,0},{28,4},{1,25},{... | collective-permute-start | bytes 786440 | tf_op jit(solution)/shard_map/ppermute | solution.py:420
  87.4 7.3 %outer_down.1 = bf16[256,4096]{1,0:T(8,128)(2,1)} custom-call(s32[2]{0:T(128)} %copy-done.14, bf16[256,768]{1,0:T(8,128)(2,1)} %copy-done.13, bf16[256,768]{1,0:T(8,128)(2,1)} %copy-done.16, bf16[256,2048]{1,0:T(8,128)(2,1)} %bitcast.52, bf16[256,4224]{1,0:T(8,128)(2,1)} %bitcast.33, bf16[256,2048]{1,0:T(8,128)(2,1)} %bitcast.48, ...), custom_call_target="tpu_custom_call" | custom-call | flops 1073741824 | bytes 10485760 | tf_op jit(solution)/shard_map/outer_down/pallas_call | solution.py:292
  94.9 3.6 %collective-permute-start.25 = (bf16[64,1152]{1,0:T(8,128)(2,1)S(1)}, bf16[64,1152]{1,0:T(8,128)(2,1)S(1)}, u32[]{:S(2)}, u32[]{:S(2)}) collective-permute-start(bf16[64,1152]{1,0:T(8,128)(2,1)S(1)} %get-tuple-element.96), channel_id=1, source_target_pairs={{0,3},{1,2},{2,1},{3,0},{4,7},{5,6},{6,5},{7,4},{8,11},{9,10},{10,... | collective-permute-start | bytes 442376 | tf_op jit(solution)/shard_map/ppermute | solution.py:429
  98.5 4.8 %collective-permute-done.24.refs_2_ = bf16[64,2048]{1,0:T(8,128)(2,1)S(1)} collective-permute-done((bf16[64,2048]{1,0:T(8,128)(2,1)}, bf16[64,2048]{1,0:T(8,128)(2,1)S(1)}, u32[]{:S(2)}, u32[]{:S(2)}) %collective-permute-start.24) | collective-permute-done | bytes 262176 | tf_op jit(solution)/shard_map/ppermute | solution.py:420
  103.7 7.3 %outer_gate_up.1 = (bf16[4096,256]{1,0:T(8,128)(2,1)}, bf16[4096,256]{1,0:T(8,128)(2,1)}) custom-call(s32[2]{0:T(128)} %copy-done.14, bf16[256,768]{1,0:T(8,128)(2,1)} %copy-done.13, bf16[256,768]{1,0:T(8,128)(2,1)} %copy-done.16, bf16[256,2048]{1,0:T(8,128)(2,1)} %bitcast.53, bf16[256,4224]{1,0:T(8,128)(2,1)} %bitcast.34, bf16[256,2048]{1,0:T(8,128)(2,1)} %bitcast.49, ...), custom_call_target="tpu_custom_call" | custom-call | flops 2147483648 | bytes 8388608 | tf_op jit(solution)/shard_map/outer_gate_up/pallas_call | solution.py:292
  111.0 0.5 collective-permute-done.27.refs_2_
  111.6 0.9 final_sum.1
  112.5 0.7 copy.19
  (65 shorter events, 2.9 us)
Async XLA Ops:
  2.5 16.1 %collective-permute-start.4 = (bf16[64,2048]{1,0:T(8,128)(2,1)S(1)}, bf16[64,2048]{1,0:T(8,128)(2,1)S(1)}, u32[]{:S(2)}, u32[]{:S(2)}) collective-permute-start(bf16[64,2048]{1,0:T(8,128)(2,1)S(1)} %constant_dynamic-update-slice_fusion), channel_id=1, source_target_pairs={{0,2},{1,3},{2,0},{3,1},{4,6},{5,7},{6,4},{7,5},{8,10},{9,11},{10,... | collective-permute-start | bytes 786440 | tf_op jit(solution)/shard_map/ppermute | solution.py:429
  6.6 12.2 %collective-permute-start.3 = (bf16[64,2048]{1,0:T(8,128)(2,1)S(1)}, bf16[64,2048]{1,0:T(8,128)(2,1)S(1)}, u32[]{:S(2)}, u32[]{:S(2)}) collective-permute-start(bf16[64,2048]{1,0:T(8,128)(2,1)S(1)} %constant_dynamic-update-slice_fusion), channel_id=1, source_target_pairs={{0,1},{1,0},{2,3},{3,2},{4,5},{5,4},{6,7},{7,6},{8,9},{9,8},{10,11... | collective-permute-start | bytes 786440 | tf_op jit(solution)/shard_map/ppermute | solution.py:429
  8.1 10.6 %collective-permute-start.2 = (bf16[64,2048]{1,0:T(8,128)(2,1)S(1)}, bf16[64,2048]{1,0:T(8,128)(2,1)S(1)}, u32[]{:S(2)}, u32[]{:S(2)}) collective-permute-start(bf16[64,2048]{1,0:T(8,128)(2,1)S(1)} %constant_dynamic-update-slice_fusion), channel_id=1, source_target_pairs={{0,24},{4,28},{8,16},{12,20},{16,8},{20,12},{24,0},{28,4},{1,25},{... | collective-permute-start | bytes 786440 | tf_op jit(solution)/shard_map/ppermute | solution.py:420
  10.6 11.6 %collective-permute-start.1 = (bf16[64,2048]{1,0:T(8,128)(2,1)S(1)}, bf16[64,2048]{1,0:T(8,128)(2,1)S(1)}, u32[]{:S(2)}, u32[]{:S(2)}) collective-permute-start(bf16[64,2048]{1,0:T(8,128)(2,1)S(1)} %constant_dynamic-update-slice_fusion), channel_id=1, source_target_pairs={{0,16},{4,20},{8,24},{12,28},{16,0},{20,4},{24,8},{28,12},{1,17},{... | collective-permute-start | bytes 786440 | tf_op jit(solution)/shard_map/ppermute | solution.py:420
  11.1 11.1 %collective-permute-start = (bf16[64,2048]{1,0:T(8,128)(2,1)S(1)}, bf16[64,2048]{1,0:T(8,128)(2,1)S(1)}, u32[]{:S(2)}, u32[]{:S(2)}) collective-permute-start(bf16[64,2048]{1,0:T(8,128)(2,1)S(1)} %constant_dynamic-update-slice_fusion), channel_id=1, source_target_pairs={{0,8},{4,12},{8,0},{12,4},{16,24},{20,28},{24,16},{28,20},{1,9},{5... | collective-permute-start | bytes 786440 | tf_op jit(solution)/shard_map/ppermute | solution.py:420
  22.2 5.1 %collective-permute-start.7 = (bf16[4096,256]{1,0:T(8,128)(2,1)}, bf16[4096,256]{1,0:T(8,128)(2,1)S(1)}, u32[]{:S(2)}, u32[]{:S(2)}) collective-permute-start(bf16[4096,256]{1,0:T(8,128)(2,1)} %bitcast.35), channel_id=1, source_target_pairs={{0,4},{4,0},{8,12},{12,8},{16,20},{20,16},{24,28},{28,24},{1,5},{5... | collective-permute-start | bytes 6291464 | tf_op jit(solution)/shard_map/ppermute | solution.py:420
  22.3 7.4 %collective-permute-start.8 = (bf16[4096,256]{1,0:T(8,128)(2,1)}, bf16[4096,256]{1,0:T(8,128)(2,1)S(1)}, u32[]{:S(2)}, u32[]{:S(2)}) collective-permute-start(bf16[4096,256]{1,0:T(8,128)(2,1)} %bitcast.40), channel_id=1, source_target_pairs={{0,4},{4,0},{8,12},{12,8},{16,20},{20,16},{24,28},{28,24},{1,5},{5... | collective-permute-start | bytes 6291464 | tf_op jit(solution)/shard_map/ppermute | solution.py:420
  24.3 15.7 %collective-permute-start.10 = (bf16[64,2048]{1,0:T(8,128)(2,1)S(1)}, bf16[64,2048]{1,0:T(8,128)(2,1)S(1)}, u32[]{:S(2)}, u32[]{:S(2)}) collective-permute-start(bf16[64,2048]{1,0:T(8,128)(2,1)S(1)} %constant_dynamic-update-slice_fusion), channel_id=1, source_target_pairs={{0,3},{1,2},{2,1},{3,0},{4,7},{5,6},{6,5},{7,4},{8,11},{9,10},{10,... | collective-permute-start | bytes 786440 | tf_op jit(solution)/shard_map/ppermute | solution.py:429
  24.6 15.4 %collective-permute-start.6 = (bf16[64,4224]{1,0:T(8,128)(2,1)S(1)}, bf16[64,4224]{1,0:T(8,128)(2,1)S(1)}, u32[]{:S(2)}, u32[]{:S(2)}) collective-permute-start(bf16[64,4224]{1,0:T(8,128)(2,1)S(1)} %pad_maximum_fusion.3), channel_id=1, source_target_pairs={{0,16},{4,20},{8,24},{12,28},{16,0},{20,4},{24,8},{28,12},{1,17},{... | collective-permute-start | bytes 1622024 | tf_op jit(solution)/shard_map/ppermute | solution.py:420
  26.1 15.2 %collective-permute-start.5 = (bf16[64,4224]{1,0:T(8,128)(2,1)S(1)}, bf16[64,4224]{1,0:T(8,128)(2,1)S(1)}, u32[]{:S(2)}, u32[]{:S(2)}) collective-permute-start(bf16[64,4224]{1,0:T(8,128)(2,1)S(1)} %pad_maximum_fusion.3), channel_id=1, source_target_pairs={{0,8},{4,12},{8,0},{12,4},{16,24},{20,28},{24,16},{28,20},{1,9},{5... | collective-permute-start | bytes 1622024 | tf_op jit(solution)/shard_map/ppermute | solution.py:420
  27.3 1.3 %copy-start.5 = (bf16[4096,256]{1,0:T(8,128)(2,1)}, bf16[4096,256]{1,0:T(8,128)(2,1)S(1)}, u32[]{:S(2)}) copy-start(bf16[4096,256]{1,0:T(8,128)(2,1)S(1)} %collective-permute-done.7.refs_3_.refs_5_.refs_2_) | copy-start | bytes 6291460
  29.6 1.3 %copy-start.8 = (bf16[4096,256]{1,0:T(8,128)(2,1)}, bf16[4096,256]{1,0:T(8,128)(2,1)S(1)}, u32[]{:S(2)}) copy-start(bf16[4096,256]{1,0:T(8,128)(2,1)S(1)} %collective-permute-done.8.refs_4_.refs_6_.refs_3_) | copy-start | bytes 6291460
  30.9 20.5 %collective-permute-start.9 = (bf16[64,4224]{1,0:T(8,128)(2,1)S(1)}, bf16[64,4224]{1,0:T(8,128)(2,1)S(1)}, u32[]{:S(2)}, u32[]{:S(2)}) collective-permute-start(bf16[64,4224]{1,0:T(8,128)(2,1)S(1)} %pad_maximum_fusion.3), channel_id=1, source_target_pairs={{0,24},{4,28},{8,16},{12,20},{16,8},{20,12},{24,0},{28,4},{1,25},{... | collective-permute-start | bytes 1622024 | tf_op jit(solution)/shard_map/ppermute | solution.py:420
  39.9 17.5 %copy-start.12 = (bf16[4,64,2048]{2,1,0:T(8,128)(2,1)}, bf16[4,64,2048]{2,1,0:T(8,128)(2,1)S(1)}, u32[]{:S(2)}) copy-start(bf16[4,64,2048]{2,1,0:T(8,128)(2,1)S(1)} %pad_maximum_fusion.1) | copy-start | bytes 3145732
  51.4 4.5 %collective-permute-start.14 = (bf16[256,4096]{1,0:T(8,128)(2,1)}, bf16[256,4096]{1,0:T(8,128)(2,1)}, u32[]{:S(2)}, u32[]{:S(2)}) collective-permute-start(bf16[256,4096]{1,0:T(8,128)(2,1)} %bitcast.10.refs_2_.refs_4_), channel_id=1, source_target_pairs={{0,4},{4,0},{8,12},{12,8},{16,20},{20,16},{24,28},{28,24},{1,5},{5... | collective-permute-start | bytes 6291464 | tf_op jit(solution)/shard_map/ppermute | solution.py:420
  51.7 17.5 %copy-start = (bf16[4,64,4224]{2,1,0:T(8,128)(2,1)}, bf16[4,64,4224]{2,1,0:T(8,128)(2,1)S(1)}, u32[]{:S(2)}) copy-start(bf16[4,64,4224]{2,1,0:T(8,128)(2,1)S(1)} %pad_maximum_fusion) | copy-start | bytes 6488068
  51.7 17.3 %collective-permute-start.16 = (bf16[256,4224]{1,0:T(8,128)(2,1)S(1)}, bf16[256,4224]{1,0:T(8,128)(2,1)}, u32[]{:S(2)}, u32[]{:S(2)}) collective-permute-start(bf16[256,4224]{1,0:T(8,128)(2,1)S(1)} %bitcast.30), channel_id=1, source_target_pairs={{0,4},{4,0},{8,12},{12,8},{16,20},{20,16},{24,28},{28,24},{1,5},{5... | collective-permute-start | bytes 6488072 | tf_op jit(solution)/shard_map/ppermute | solution.py:420
  52.3 16.7 %collective-permute-start.15 = (bf16[256,2048]{1,0:T(8,128)(2,1)S(1)}, bf16[256,2048]{1,0:T(8,128)(2,1)}, u32[]{:S(2)}, u32[]{:S(2)}) collective-permute-start(bf16[256,2048]{1,0:T(8,128)(2,1)S(1)} %bitcast.50), channel_id=1, source_target_pairs={{0,4},{4,0},{8,12},{12,8},{16,20},{20,16},{24,28},{28,24},{1,5},{5... | collective-permute-start | bytes 3145736 | tf_op jit(solution)/shard_map/ppermute | solution.py:420
  52.4 16.6 %collective-permute-start.13 = (bf16[64,2048]{1,0:T(8,128)(2,1)S(1)}, bf16[64,2048]{1,0:T(8,128)(2,1)S(1)}, u32[]{:S(2)}, u32[]{:S(2)}) collective-permute-start(bf16[64,2048]{1,0:T(8,128)(2,1)S(1)} %collective-permute-done.10), channel_id=1, source_target_pairs={{0,24},{4,28},{8,16},{12,20},{16,8},{20,12},{24,0},{28,4},{1,25},{... | collective-permute-start | bytes 786440 | tf_op jit(solution)/shard_map/ppermute | solution.py:420
  54.5 14.5 %collective-permute-start.12 = (bf16[64,2048]{1,0:T(8,128)(2,1)S(1)}, bf16[64,2048]{1,0:T(8,128)(2,1)S(1)}, u32[]{:S(2)}, u32[]{:S(2)}) collective-permute-start(bf16[64,2048]{1,0:T(8,128)(2,1)S(1)} %collective-permute-done.10), channel_id=1, source_target_pairs={{0,16},{4,20},{8,24},{12,28},{16,0},{20,4},{24,8},{28,12},{1,17},{... | collective-permute-start | bytes 786440 | tf_op jit(solution)/shard_map/ppermute | solution.py:420
  55.9 13.1 %collective-permute-start.11 = (bf16[64,2048]{1,0:T(8,128)(2,1)S(1)}, bf16[64,2048]{1,0:T(8,128)(2,1)S(1)}, u32[]{:S(2)}, u32[]{:S(2)}) collective-permute-start(bf16[64,2048]{1,0:T(8,128)(2,1)S(1)} %collective-permute-done.10), channel_id=1, source_target_pairs={{0,8},{4,12},{8,0},{12,4},{16,24},{20,28},{24,16},{28,20},{1,9},{5... | collective-permute-start | bytes 786440 | tf_op jit(solution)/shard_map/ppermute | solution.py:420
  57.5 1.6 %copy-start.1 = (bf16[1,4096,256]{2,1,0:T(8,128)(2,1)S(1)}, bf16[1,4096,256]{2,1,0:T(8,128)(2,1)}, u32[]{:S(2)}) copy-start(bf16[1,4096,256]{2,1,0:T(8,128)(2,1)} %param.13) | copy-start | bytes 6291460
  59.1 1.6 %copy-start.3 = (bf16[1,4096,256]{2,1,0:T(8,128)(2,1)S(1)}, bf16[1,4096,256]{2,1,0:T(8,128)(2,1)}, u32[]{:S(2)}) copy-start(bf16[1,4096,256]{2,1,0:T(8,128)(2,1)} %param.14) | copy-start | bytes 6291460
  60.7 1.6 %copy-start.6 = (bf16[4096,256]{1,0:T(8,128)(2,1)S(1)}, bf16[4096,256]{1,0:T(8,128)(2,1)}, u32[]{:S(2)}) copy-start(bf16[4096,256]{1,0:T(8,128)(2,1)} %copy-done.5) | copy-start | bytes 6291460
  62.3 1.6 %copy-start.9 = (bf16[4096,256]{1,0:T(8,128)(2,1)S(1)}, bf16[4096,256]{1,0:T(8,128)(2,1)}, u32[]{:S(2)}) copy-start(bf16[4096,256]{1,0:T(8,128)(2,1)} %copy-done.8) | copy-start | bytes 6291460
  63.8 16.1 %copy-start.14 = (s32[2]{0:T(128)}, s32[2]{0:T(128)S(1)}, u32[]{:S(2)}) copy-start(s32[2]{0:T(128)S(1)} %pad_add_fusion.place) | copy-start | bytes 28
  63.8 5.4 %copy-start.10 = (bf16[4096,256]{1,0:T(8,128)(2,1)S(1)}, bf16[4096,256]{1,0:T(8,128)(2,1)}, u32[]{:S(2)}) copy-start(bf16[4096,256]{1,0:T(8,128)(2,1)} %copy-done.8) | copy-start | bytes 6291460
  68.9 2.0 %copy-start.7 = (bf16[4096,256]{1,0:T(8,128)(2,1)S(1)}, bf16[4096,256]{1,0:T(8,128)(2,1)}, u32[]{:S(2)}) copy-start(bf16[4096,256]{1,0:T(8,128)(2,1)} %copy-done.5) | copy-start | bytes 6291460
  69.2 4.9 %copy-start.11 = (bf16[4,64,2048]{2,1,0:T(8,128)(2,1)}, bf16[4,64,2048]{2,1,0:T(8,128)(2,1)S(1)}, u32[]{:S(2)}) copy-start(bf16[4,64,2048]{2,1,0:T(8,128)(2,1)S(1)} %pad_maximum_fusion.2) | copy-start | bytes 3145732
  69.2 5.0 %copy-start.2 = (bf16[1,4096,256]{2,1,0:T(8,128)(2,1)S(1)}, bf16[1,4096,256]{2,1,0:T(8,128)(2,1)}, u32[]{:S(2)}) copy-start(bf16[1,4096,256]{2,1,0:T(8,128)(2,1)} %param.13) | copy-start | bytes 6291460
  69.2 5.0 %copy-start.4 = (bf16[1,4096,256]{2,1,0:T(8,128)(2,1)S(1)}, bf16[1,4096,256]{2,1,0:T(8,128)(2,1)}, u32[]{:S(2)}) copy-start(bf16[1,4096,256]{2,1,0:T(8,128)(2,1)} %param.14) | copy-start | bytes 6291460
  69.2 4.9 %collective-permute-start.17 = (bf16[256,2048]{1,0:T(8,128)(2,1)S(1)}, bf16[256,2048]{1,0:T(8,128)(2,1)S(1)}, u32[]{:S(2)}, u32[]{:S(2)}) collective-permute-start(bf16[256,2048]{1,0:T(8,128)(2,1)S(1)} %bitcast.45), channel_id=1, source_target_pairs={{0,4},{4,0},{8,12},{12,8},{16,20},{20,16},{24,28},{28,24},{1,5},{5... | collective-permute-start | bytes 3145736 | tf_op jit(solution)/shard_map/ppermute | solution.py:420
  74.0 5.9 %copy-start.13 = (bf16[256,768]{1,0:T(8,128)(2,1)}, bf16[256,768]{1,0:T(8,128)(2,1)S(1)}, u32[]{:S(2)}) copy-start(bf16[256,768]{1,0:T(8,128)(2,1)S(1)} %get-tuple-element.84.mine.acts) | copy-start | bytes 1179652
  74.0 2.9 %collective-permute-start.18 = (bf16[256,768]{1,0:T(8,128)(2,1)S(1)}, bf16[256,768]{1,0:T(8,128)(2,1)S(1)}, u32[]{:S(2)}, u32[]{:S(2)}) collective-permute-start(bf16[256,768]{1,0:T(8,128)(2,1)S(1)} %get-tuple-element.82.other), channel_id=1, source_target_pairs={{0,4},{4,0},{8,12},{12,8},{16,20},{20,16},{24,28},{28,24},{1,5},{5... | collective-permute-start | bytes 1179656 | tf_op jit(solution)/shard_map/ppermute | solution.py:420
  74.1 2.2 %copy-start.15 = (bf16[256,2048]{1,0:T(8,128)(2,1)}, bf16[256,2048]{1,0:T(8,128)(2,1)S(1)}, u32[]{:S(2)}) copy-start(bf16[256,2048]{1,0:T(8,128)(2,1)S(1)} %collective-permute-done.17.refs_5_) | copy-start | bytes 3145732
  76.4 9.5 %collective-permute-start.19 = (bf16[64,2176]{1,0:T(8,128)(2,1)S(1)}, bf16[64,2176]{1,0:T(8,128)(2,1)S(1)}, u32[]{:S(2)}, u32[]{:S(2)}) collective-permute-start(bf16[64,2176]{1,0:T(8,128)(2,1)S(1)} %get-tuple-element.93), channel_id=1, source_target_pairs={{0,8},{4,12},{8,0},{12,4},{16,24},{20,28},{24,16},{28,20},{1,9},{5... | collective-permute-start | bytes 835592 | tf_op jit(solution)/shard_map/ppermute | solution.py:420
  77.0 1.4 %copy-start.16 = (bf16[256,768]{1,0:T(8,128)(2,1)}, bf16[256,768]{1,0:T(8,128)(2,1)S(1)}, u32[]{:S(2)}) copy-start(bf16[256,768]{1,0:T(8,128)(2,1)S(1)} %collective-permute-done.18.got) | copy-start | bytes 1179652
  77.0 17.7 %collective-permute-start.20 = (bf16[64,2176]{1,0:T(8,128)(2,1)S(1)}, bf16[64,2176]{1,0:T(8,128)(2,1)S(1)}, u32[]{:S(2)}, u32[]{:S(2)}) collective-permute-start(bf16[64,2176]{1,0:T(8,128)(2,1)S(1)} %get-tuple-element.94), channel_id=1, source_target_pairs={{0,16},{4,20},{8,24},{12,28},{16,0},{20,4},{24,8},{28,12},{1,17},{... | collective-permute-start | bytes 835592 | tf_op jit(solution)/shard_map/ppermute | solution.py:420
  78.4 8.9 %copy-start.17 = (s32[64,4]{0,1:T(4,128)S(1)}, s32[64,4]{0,1:T(4,128)}, u32[]{:S(2)}) copy-start(s32[64,4]{0,1:T(4,128)} %param.11) | copy-start | bytes 3076
  78.4 16.3 %collective-permute-start.21 = (bf16[64,2176]{1,0:T(8,128)(2,1)S(1)}, bf16[64,2176]{1,0:T(8,128)(2,1)S(1)}, u32[]{:S(2)}, u32[]{:S(2)}) collective-permute-start(bf16[64,2176]{1,0:T(8,128)(2,1)S(1)} %get-tuple-element.95), channel_id=1, source_target_pairs={{0,24},{4,28},{8,16},{12,20},{16,8},{20,12},{24,0},{28,4},{1,25},{... | collective-permute-start | bytes 835592 | tf_op jit(solution)/shard_map/ppermute | solution.py:420
  83.0 15.5 %collective-permute-start.22 = (bf16[64,2048]{1,0:T(8,128)(2,1)}, bf16[64,2048]{1,0:T(8,128)(2,1)S(1)}, u32[]{:S(2)}, u32[]{:S(2)}) collective-permute-start(bf16[64,2048]{1,0:T(8,128)(2,1)} %get-tuple-element.99), channel_id=1, source_target_pairs={{0,8},{4,12},{8,0},{12,4},{16,24},{20,28},{24,16},{28,20},{1,9},{5... | collective-permute-start | bytes 786440 | tf_op jit(solution)/shard_map/ppermute | solution.py:420
  83.7 14.8 %collective-permute-start.23 = (bf16[64,2048]{1,0:T(8,128)(2,1)}, bf16[64,2048]{1,0:T(8,128)(2,1)S(1)}, u32[]{:S(2)}, u32[]{:S(2)}) collective-permute-start(bf16[64,2048]{1,0:T(8,128)(2,1)} %get-tuple-element.100), channel_id=1, source_target_pairs={{0,16},{4,20},{8,24},{12,28},{16,0},{20,4},{24,8},{28,12},{1,17},{... | collective-permute-start | bytes 786440 | tf_op jit(solution)/shard_map/ppermute | solution.py:420
  85.9 17.4 %collective-permute-start.24 = (bf16[64,2048]{1,0:T(8,128)(2,1)}, bf16[64,2048]{1,0:T(8,128)(2,1)S(1)}, u32[]{:S(2)}, u32[]{:S(2)}) collective-permute-start(bf16[64,2048]{1,0:T(8,128)(2,1)} %get-tuple-element.101), channel_id=1, source_target_pairs={{0,24},{4,28},{8,16},{12,20},{16,8},{20,12},{24,0},{28,4},{1,25},{... | collective-permute-start | bytes 786440 | tf_op jit(solution)/shard_map/ppermute | solution.py:420
  94.9 16.7 %collective-permute-start.25 = (bf16[64,1152]{1,0:T(8,128)(2,1)S(1)}, bf16[64,1152]{1,0:T(8,128)(2,1)S(1)}, u32[]{:S(2)}, u32[]{:S(2)}) collective-permute-start(bf16[64,1152]{1,0:T(8,128)(2,1)S(1)} %get-tuple-element.96), channel_id=1, source_target_pairs={{0,3},{1,2},{2,1},{3,0},{4,7},{5,6},{6,5},{7,4},{8,11},{9,10},{10,... | collective-permute-start | bytes 442376 | tf_op jit(solution)/shard_map/ppermute | solution.py:429
  98.5 13.1 %collective-permute-start.26 = (bf16[64,1152]{1,0:T(8,128)(2,1)S(1)}, bf16[64,1152]{1,0:T(8,128)(2,1)S(1)}, u32[]{:S(2)}, u32[]{:S(2)}) collective-permute-start(bf16[64,1152]{1,0:T(8,128)(2,1)S(1)} %get-tuple-element.97), channel_id=1, source_target_pairs={{0,2},{1,3},{2,0},{3,1},{4,6},{5,7},{6,4},{7,5},{8,10},{9,11},{10,... | collective-permute-start | bytes 442376 | tf_op jit(solution)/shard_map/ppermute | solution.py:429
  103.4 8.2 %collective-permute-start.27 = (bf16[64,1152]{1,0:T(8,128)(2,1)S(1)}, bf16[64,1152]{1,0:T(8,128)(2,1)S(1)}, u32[]{:S(2)}, u32[]{:S(2)}) collective-permute-start(bf16[64,1152]{1,0:T(8,128)(2,1)S(1)} %get-tuple-element.104), channel_id=1, source_target_pairs={{0,1},{1,0},{2,3},{3,2},{4,5},{5,4},{6,7},{7,6},{8,9},{9,8},{10,11... | collective-permute-start | bytes 442376 | tf_op jit(solution)/shard_map/ppermute | solution.py:429

commit v5 on v4

--- a/solution.py
+++ b/solution.py
@@ -339,6 +339,12 @@
     )(*args)
 
 
+def join_kernel(left, right, out):
+    width = left.shape[1]
+    out[:, :width] = left[...]
+    out[:, width:] = right[...]
+
+
 def group_sum_kernel(group, n_got, n_expert, first, own, *refs):
     gots, refs = refs[:n_got], refs[n_got:]
     value = own[...]
@@ -437,7 +443,8 @@
     ).astype(BF)
 
     together = lax.optimization_barrier
-    both = jnp.concatenate([tokens, cotangent], axis=1)
+    joined = jax.ShapeDtypeStruct((count, 2 * width), BF)
+    (both,) = call_small(join_kernel, "join", [joined], tokens, cotangent)
     masks = range(2, n_expert, 2)
 
     def to_chips(part, before=()):

time: 114 us -> 114 us (level)
    unnamed x39 -> x42, local copies, waits for them, and re-layouts: 12.3 us -> 13.2 us
where the time goes in v5:
time: 114 us; the launch traced here: 113 us
  starting transfers between devices  30.4 us (27%)
  waiting for transfers between devices  29.9 us (26%)
  Pallas kernels  29.3 us (26%)
  local copies, waits for them, and re-layouts  13.2 us (12%)
  other arithmetic  9.42 us (8%)
    ppermute x22, waiting for transfers between devices, over_expert(): lax.ppermute(value, 'expert', [(i, i ^ mask) for i in range(n_expert)])  22.2 us
    ppermute x22, starting transfers between devices, over_expert(): lax.ppermute(value, 'expert', [(i, i ^ mask) for i in range(n_expert)])  20.5 us
    pallas_call x2, Pallas kernels, outer_products(): pl.pallas_call(functools.partial(outer_kernel, pieces, len(sources), rows...  14.6 us
    unnamed x42, local copies, waits for them, and re-layouts  13.2 us
    ppermute x6, starting transfers between devices, over_slice(): return lax.ppermute(value, 'ffn', [(i, i ^ mask) for i in range(n_slice)])  9.89 us
    ppermute x6, waiting for transfers between devices, over_slice(): return lax.ppermute(value, 'ffn', [(i, i ^ mask) for i in range(n_slice)])  7.7 us
    mul x1, other arithmetic, per_device(): penalty = fisher[0] * (down.astype(F32) - anchor[0])  7.23 us
    pallas_call x2, Pallas kernels, unit_product(): pl.pallas_call(functools.partial(unit_kernel, tokens, slots, route is not...  5.24 us
  transfers between devices with their start and end apart: 28, of which 11 were waited for; matrix products, arithmetic and copies ran while one was open for 8% of the time, Pallas kernels for 25%

profile of v5, /device:TPU:0, one launch (start us, length us, event | category | flops | bytes accessed | tf_op | source)
XLA Modules:
  0.0 113.2 jit_solution(15281934852201394289)
XLA Ops:
  0.6 0.9 copy-done.14
  1.5 0.9 copy-done.15
  2.5 4.1 %collective-permute-start.4 = (bf16[64,2048]{1,0:T(8,128)(2,1)S(1)}, bf16[64,2048]{1,0:T(8,128)(2,1)S(1)}, u32[]{:S(2)}, u32[]{:S(2)}) collective-permute-start(bf16[64,2048]{1,0:T(8,128)(2,1)S(1)} %join.1), channel_id=1, source_target_pairs={{0,2},{1,3},{2,0},{3,1},{4,6},{5,7},{6,4},{7,5},{8,10},{9,11},{10,... | collective-permute-start | bytes 786440 | tf_op jit(solution)/shard_map/ppermute | solution.py:435
  6.6 1.6 %collective-permute-start.3 = (bf16[64,2048]{1,0:T(8,128)(2,1)S(1)}, bf16[64,2048]{1,0:T(8,128)(2,1)S(1)}, u32[]{:S(2)}, u32[]{:S(2)}) collective-permute-start(bf16[64,2048]{1,0:T(8,128)(2,1)S(1)} %join.1), channel_id=1, source_target_pairs={{0,1},{1,0},{2,3},{3,2},{4,5},{5,4},{6,7},{7,6},{8,9},{9,8},{10,11... | collective-permute-start | bytes 786440 | tf_op jit(solution)/shard_map/ppermute | solution.py:435
  8.1 2.4 %collective-permute-start.2 = (bf16[64,2048]{1,0:T(8,128)(2,1)S(1)}, bf16[64,2048]{1,0:T(8,128)(2,1)S(1)}, u32[]{:S(2)}, u32[]{:S(2)}) collective-permute-start(bf16[64,2048]{1,0:T(8,128)(2,1)S(1)} %join.1), channel_id=1, source_target_pairs={{0,24},{4,28},{8,16},{12,20},{16,8},{20,12},{24,0},{28,4},{1,25},{... | collective-permute-start | bytes 786440 | tf_op jit(solution)/shard_map/ppermute | solution.py:426
  11.1 0.5 collective-permute-start
  11.6 7.0 %collective-permute-done.4 = bf16[64,2048]{1,0:T(8,128)(2,1)S(1)} collective-permute-done((bf16[64,2048]{1,0:T(8,128)(2,1)S(1)}, bf16[64,2048]{1,0:T(8,128)(2,1)S(1)}, u32[]{:S(2)}, u32[]{:S(2)}) %collective-permute-start.4) | collective-permute-done | bytes 262176 | tf_op jit(solution)/shard_map/ppermute | solution.py:435
  18.8 3.4 %collective-permute-done.1 = bf16[64,2048]{1,0:T(8,128)(2,1)S(1)} collective-permute-done((bf16[64,2048]{1,0:T(8,128)(2,1)S(1)}, bf16[64,2048]{1,0:T(8,128)(2,1)S(1)}, u32[]{:S(2)}, u32[]{:S(2)}) %collective-permute-start.1) | collective-permute-done | bytes 262176 | tf_op jit(solution)/shard_map/ppermute | solution.py:426
  22.2 0.5 collective-permute-start.8
  22.8 0.7 convert_element_type.9
  23.4 0.8 select_reduce_fusion
  24.6 1.5 %collective-permute-start.6 = (bf16[64,4224]{1,0:T(8,128)(2,1)S(1)}, bf16[64,4224]{1,0:T(8,128)(2,1)S(1)}, u32[]{:S(2)}, u32[]{:S(2)}) collective-permute-start(bf16[64,4224]{1,0:T(8,128)(2,1)S(1)} %pad_maximum_fusion.3), channel_id=1, source_target_pairs={{0,16},{4,20},{8,24},{12,28},{16,0},{20,4},{24,8},{28,12},{1,17},{... | collective-permute-start | bytes 1622024 | tf_op jit(solution)/shard_map/ppermute | solution.py:426
  26.1 1.2 %collective-permute-start.5 = (bf16[64,4224]{1,0:T(8,128)(2,1)S(1)}, bf16[64,4224]{1,0:T(8,128)(2,1)S(1)}, u32[]{:S(2)}, u32[]{:S(2)}) collective-permute-start(bf16[64,4224]{1,0:T(8,128)(2,1)S(1)} %pad_maximum_fusion.3), channel_id=1, source_target_pairs={{0,8},{4,12},{8,0},{12,4},{16,24},{20,28},{24,16},{28,20},{1,9},{5... | collective-permute-start | bytes 1622024 | tf_op jit(solution)/shard_map/ppermute | solution.py:426
  27.3 1.3 %copy-done.5 = bf16[4096,256]{1,0:T(8,128)(2,1)} copy-done((bf16[4096,256]{1,0:T(8,128)(2,1)}, bf16[4096,256]{1,0:T(8,128)(2,1)S(1)}, u32[]{:S(2)}) %copy-start.5) | copy-done | bytes 2097176
  28.6 1.0 collective-permute-done.8.refs_4_.refs_6_.refs_3_
  29.6 1.3 %copy-done.8 = bf16[4096,256]{1,0:T(8,128)(2,1)} copy-done((bf16[4096,256]{1,0:T(8,128)(2,1)}, bf16[4096,256]{1,0:T(8,128)(2,1)S(1)}, u32[]{:S(2)}) %copy-start.8) | copy-done | bytes 2097176
  30.9 1.6 %collective-permute-start.9 = (bf16[64,4224]{1,0:T(8,128)(2,1)S(1)}, bf16[64,4224]{1,0:T(8,128)(2,1)S(1)}, u32[]{:S(2)}, u32[]{:S(2)}) collective-permute-start(bf16[64,4224]{1,0:T(8,128)(2,1)S(1)} %pad_maximum_fusion.3), channel_id=1, source_target_pairs={{0,24},{4,28},{8,16},{12,20},{16,8},{20,12},{24,0},{28,4},{1,25},{... | collective-permute-start | bytes 1622024 | tf_op jit(solution)/shard_map/ppermute | solution.py:426
  32.6 7.2 %fusion.refs_6_ = f32[256,4096]{1,0:T(8,128)} fusion(f32[1,256,4096]{2,1,0:T(8,128)} %param.17, f32[1,256,4096]{2,1,0:T(8,128)} %param.16, bf16[1,256,4096]{2,1,0:T(8,128)(2,1)} %param.15), kind=kLoop, calls=%fused_computation.1 | loop fusion | flops 3145728 | bytes 14680064 | tf_op jit(solution)/shard_map/mul | solution.py:462
  40.0 1.3 %collective-permute-done.5 = bf16[64,4224]{1,0:T(8,128)(2,1)S(1)} collective-permute-done((bf16[64,4224]{1,0:T(8,128)(2,1)S(1)}, bf16[64,4224]{1,0:T(8,128)(2,1)S(1)}, u32[]{:S(2)}, u32[]{:S(2)}) %collective-permute-start.5) | collective-permute-done | bytes 540704 | tf_op jit(solution)/shard_map/ppermute | solution.py:426
  41.3 10.1 %collective-permute-done.9 = bf16[64,4224]{1,0:T(8,128)(2,1)S(1)} collective-permute-done((bf16[64,4224]{1,0:T(8,128)(2,1)S(1)}, bf16[64,4224]{1,0:T(8,128)(2,1)S(1)}, u32[]{:S(2)}, u32[]{:S(2)}) %collective-permute-start.9) | collective-permute-done | bytes 540704 | tf_op jit(solution)/shard_map/ppermute | solution.py:426
  51.7 0.6 collective-permute-start.16
  52.4 2.1 %collective-permute-start.13 = (bf16[64,2048]{1,0:T(8,128)(2,1)S(1)}, bf16[64,2048]{1,0:T(8,128)(2,1)S(1)}, u32[]{:S(2)}, u32[]{:S(2)}) collective-permute-start(bf16[64,2048]{1,0:T(8,128)(2,1)S(1)} %collective-permute-done.10), channel_id=1, source_target_pairs={{0,24},{4,28},{8,16},{12,20},{16,8},{20,12},{24,0},{28,4},{1,25},{... | collective-permute-start | bytes 786440 | tf_op jit(solution)/shard_map/ppermute | solution.py:426
  54.5 0.9 collective-permute-start.12
  55.3 0.6 collective-permute-done.14.refs_5_.refs_7_
  55.9 1.5 %collective-permute-start.11 = (bf16[64,2048]{1,0:T(8,128)(2,1)S(1)}, bf16[64,2048]{1,0:T(8,128)(2,1)S(1)}, u32[]{:S(2)}, u32[]{:S(2)}) collective-permute-start(bf16[64,2048]{1,0:T(8,128)(2,1)S(1)} %collective-permute-done.10), channel_id=1, source_target_pairs={{0,8},{4,12},{8,0},{12,4},{16,24},{20,28},{24,16},{28,20},{1,9},{5... | collective-permute-start | bytes 786440 | tf_op jit(solution)/shard_map/ppermute | solution.py:426
  57.5 1.6 %copy-done.1 = bf16[1,4096,256]{2,1,0:T(8,128)(2,1)S(1)} copy-done((bf16[1,4096,256]{2,1,0:T(8,128)(2,1)S(1)}, bf16[1,4096,256]{2,1,0:T(8,128)(2,1)}, u32[]{:S(2)}) %copy-start.1) | copy-done | bytes 2097176
  59.1 1.6 %copy-done.3 = bf16[1,4096,256]{2,1,0:T(8,128)(2,1)S(1)} copy-done((bf16[1,4096,256]{2,1,0:T(8,128)(2,1)S(1)}, bf16[1,4096,256]{2,1,0:T(8,128)(2,1)}, u32[]{:S(2)}) %copy-start.3) | copy-done | bytes 2097176
  60.7 1.6 %copy-done.6 = bf16[4096,256]{1,0:T(8,128)(2,1)S(1)} copy-done((bf16[4096,256]{1,0:T(8,128)(2,1)S(1)}, bf16[4096,256]{1,0:T(8,128)(2,1)}, u32[]{:S(2)}) %copy-start.6) | copy-done | bytes 2097176
  62.2 1.6 %copy-done.9 = bf16[4096,256]{1,0:T(8,128)(2,1)S(1)} copy-done((bf16[4096,256]{1,0:T(8,128)(2,1)S(1)}, bf16[4096,256]{1,0:T(8,128)(2,1)}, u32[]{:S(2)}) %copy-start.9) | copy-done | bytes 2097176
  63.8 5.1 %forward_near.1.refs_8_ = f32[6,256,256]{2,1,0:T(8,128)S(1)} custom-call(s32[2]{0:T(128)S(1)} %pad_add_fusion.place, bf16[256,2048]{1,0:T(8,128)(2,1)S(1)} %bitcast.51, bf16[256,4224]{1,0:T(8,128)(2,1)S(1)} %bitcast.31, bf16[4096,256]{1,0:T(8,128)(2,1)S(1)} %bitcast.36, bf16[4096,256]{1,0:T(8,128)(2,1)S(1)} %bitcast.41, ...), custom_call_target="tpu_custom_call" | custom-call | flops 2415919104 | bytes 14155776 | tf_op jit(solution)/shard_map/forward_near/pallas_call | solution.py:125
  69.3 1.6 %copy-done.7 = bf16[4096,256]{1,0:T(8,128)(2,1)S(1)} copy-done((bf16[4096,256]{1,0:T(8,128)(2,1)S(1)}, bf16[4096,256]{1,0:T(8,128)(2,1)}, u32[]{:S(2)}) %copy-start.7) | copy-done | bytes 2097176
  70.9 3.1 %forward_rest.1 = (bf16[256,768]{1,0:T(8,128)(2,1)S(1)}, bf16[256,768]{1,0:T(8,128)(2,1)S(1)}, bf16[256,128]{1,0:T(8,128)(2,1)S(1)}) custom-call(s32[2]{0:T(128)S(1)} %pad_add_fusion.place, bf16[256,2048]{1,0:T(8,128)(2,1)S(1)} %bitcast.46, bf16[256,2048]{1,0:T(8,128)(2,1)S(1)} %bitcast.47, bf16[4096,256]{1,0:T(8,128)(2,1)S(1)} %bitcast.37, ...), custom_call_target="tpu_custom_call" | custom-call | flops 805306368 | bytes 5767168 | tf_op jit(solution)/shard_map/forward_rest/pallas_call | solution.py:147
  74.1 2.2 %unit_product.3 = (f32[64,2176]{1,0:T(8,128)S(1)}, bf16[64,2176]{1,0:T(8,128)(2,1)S(1)}, bf16[64,2176]{1,0:T(8,128)(2,1)S(1)}, bf16[64,2176]{1,0:T(8,128)(2,1)S(1)}) custom-call(s32[2]{0:T(128)S(1)} %pad_add_fusion.place, bf16[256,768]{1,0:T(8,128)(2,1)S(1)} %get-tuple-element.84.mine.acts, bf16[256,768]{1,0:T(8,128)(2,1)S(1)} %get-tuple-element.82.other, ...), custom_call_target="tpu_custom_call" | custom-call | flops 1073741824 | bytes 5767168 | tf_op jit(solution)/shard_map/unit_product/pallas_call | solution.py:211
  76.4 0.6 collective-permute-start.19
  77.0 1.4 %collective-permute-start.20 = (bf16[64,2176]{1,0:T(8,128)(2,1)S(1)}, bf16[64,2176]{1,0:T(8,128)(2,1)S(1)}, u32[]{:S(2)}, u32[]{:S(2)}) collective-permute-start(bf16[64,2176]{1,0:T(8,128)(2,1)S(1)} %get-tuple-element.94), channel_id=1, source_target_pairs={{0,16},{4,20},{8,24},{12,28},{16,0},{20,4},{24,8},{28,12},{1,17},{... | collective-permute-start | bytes 835592 | tf_op jit(solution)/shard_map/ppermute | solution.py:426
  78.4 1.5 %collective-permute-start.21 = (bf16[64,2176]{1,0:T(8,128)(2,1)S(1)}, bf16[64,2176]{1,0:T(8,128)(2,1)S(1)}, u32[]{:S(2)}, u32[]{:S(2)}) collective-permute-start(bf16[64,2176]{1,0:T(8,128)(2,1)S(1)} %get-tuple-element.95), channel_id=1, source_target_pairs={{0,24},{4,28},{8,16},{12,20},{16,8},{20,12},{24,0},{28,4},{1,25},{... | collective-permute-start | bytes 835592 | tf_op jit(solution)/shard_map/ppermute | solution.py:426
  79.9 3.1 %unit_product.2 = (f32[64,2048]{1,0:T(8,128)S(1)}, bf16[64,2048]{1,0:T(8,128)(2,1)}, bf16[64,2048]{1,0:T(8,128)(2,1)}, bf16[64,2048]{1,0:T(8,128)(2,1)}) custom-call(s32[2]{0:T(128)S(1)} %pad_add_fusion.place, bf16[256,768]{1,0:T(8,128)(2,1)S(1)} %get-tuple-element.84.mine.acts, bf16[256,768]{1,0:T(8,128)(2,1)S(1)} %get-tuple-element.82.other, ...), custom_call_target="tpu_custom_call" | custom-call | flops 1073741824 | bytes 5767168 | tf_op jit(solution)/shard_map/unit_product/pallas_call | solution.py:211
  83.0 0.7 collective-permute-start.22
  83.7 1.3 %collective-permute-start.23 = (bf16[64,2048]{1,0:T(8,128)(2,1)}, bf16[64,2048]{1,0:T(8,128)(2,1)S(1)}, u32[]{:S(2)}, u32[]{:S(2)}) collective-permute-start(bf16[64,2048]{1,0:T(8,128)(2,1)} %get-tuple-element.100), channel_id=1, source_target_pairs={{0,16},{4,20},{8,24},{12,28},{16,0},{20,4},{24,8},{28,12},{1,17},{... | collective-permute-start | bytes 786440 | tf_op jit(solution)/shard_map/ppermute | solution.py:426
  84.9 0.9 collective-permute-done.19.refs_0_
  85.9 1.4 %collective-permute-start.24 = (bf16[64,2048]{1,0:T(8,128)(2,1)}, bf16[64,2048]{1,0:T(8,128)(2,1)S(1)}, u32[]{:S(2)}, u32[]{:S(2)}) collective-permute-start(bf16[64,2048]{1,0:T(8,128)(2,1)} %get-tuple-element.101), channel_id=1, source_target_pairs={{0,24},{4,28},{8,16},{12,20},{16,8},{20,12},{24,0},{28,4},{1,25},{... | collective-permute-start | bytes 786440 | tf_op jit(solution)/shard_map/ppermute | solution.py:426
  87.4 7.3 %outer_down.1 = bf16[256,4096]{1,0:T(8,128)(2,1)} custom-call(s32[2]{0:T(128)} %copy-done.16, bf16[256,768]{1,0:T(8,128)(2,1)} %copy-done.13, bf16[256,768]{1,0:T(8,128)(2,1)} %copy-done.18, bf16[256,2048]{1,0:T(8,128)(2,1)} %bitcast.52, bf16[256,4224]{1,0:T(8,128)(2,1)} %bitcast.33, bf16[256,2048]{1,0:T(8,128)(2,1)} %bitcast.48, ...), custom_call_target="tpu_custom_call" | custom-call | flops 1073741824 | bytes 10485760 | tf_op jit(solution)/shard_map/outer_down/pallas_call | solution.py:292
  94.9 3.6 %collective-permute-start.25 = (bf16[64,1152]{1,0:T(8,128)(2,1)S(1)}, bf16[64,1152]{1,0:T(8,128)(2,1)S(1)}, u32[]{:S(2)}, u32[]{:S(2)}) collective-permute-start(bf16[64,1152]{1,0:T(8,128)(2,1)S(1)} %get-tuple-element.96), channel_id=1, source_target_pairs={{0,3},{1,2},{2,1},{3,0},{4,7},{5,6},{6,5},{7,4},{8,11},{9,10},{10,... | collective-permute-start | bytes 442376 | tf_op jit(solution)/shard_map/ppermute | solution.py:435
  98.5 4.8 %collective-permute-done.24.refs_2_ = bf16[64,2048]{1,0:T(8,128)(2,1)S(1)} collective-permute-done((bf16[64,2048]{1,0:T(8,128)(2,1)}, bf16[64,2048]{1,0:T(8,128)(2,1)S(1)}, u32[]{:S(2)}, u32[]{:S(2)}) %collective-permute-start.24) | collective-permute-done | bytes 262176 | tf_op jit(solution)/shard_map/ppermute | solution.py:426
  103.7 7.3 %outer_gate_up.1 = (bf16[4096,256]{1,0:T(8,128)(2,1)}, bf16[4096,256]{1,0:T(8,128)(2,1)}) custom-call(s32[2]{0:T(128)} %copy-done.16, bf16[256,768]{1,0:T(8,128)(2,1)} %copy-done.13, bf16[256,768]{1,0:T(8,128)(2,1)} %copy-done.18, bf16[256,2048]{1,0:T(8,128)(2,1)} %bitcast.53, bf16[256,4224]{1,0:T(8,128)(2,1)} %bitcast.34, bf16[256,2048]{1,0:T(8,128)(2,1)} %bitcast.49, ...), custom_call_target="tpu_custom_call" | custom-call | flops 2147483648 | bytes 8388608 | tf_op jit(solution)/shard_map/outer_gate_up/pallas_call | solution.py:292
  111.0 0.5 collective-permute-done.27.refs_2_
  111.6 0.9 final_sum.1
  112.5 0.7 copy.19
  (68 shorter events, 2.9 us)
Async XLA Ops:
  0.6 0.9 copy-start.14
  1.5 0.9 copy-start.15
  2.5 16.1 %collective-permute-start.4 = (bf16[64,2048]{1,0:T(8,128)(2,1)S(1)}, bf16[64,2048]{1,0:T(8,128)(2,1)S(1)}, u32[]{:S(2)}, u32[]{:S(2)}) collective-permute-start(bf16[64,2048]{1,0:T(8,128)(2,1)S(1)} %join.1), channel_id=1, source_target_pairs={{0,2},{1,3},{2,0},{3,1},{4,6},{5,7},{6,4},{7,5},{8,10},{9,11},{10,... | collective-permute-start | bytes 786440 | tf_op jit(solution)/shard_map/ppermute | solution.py:435
  6.6 12.2 %collective-permute-start.3 = (bf16[64,2048]{1,0:T(8,128)(2,1)S(1)}, bf16[64,2048]{1,0:T(8,128)(2,1)S(1)}, u32[]{:S(2)}, u32[]{:S(2)}) collective-permute-start(bf16[64,2048]{1,0:T(8,128)(2,1)S(1)} %join.1), channel_id=1, source_target_pairs={{0,1},{1,0},{2,3},{3,2},{4,5},{5,4},{6,7},{7,6},{8,9},{9,8},{10,11... | collective-permute-start | bytes 786440 | tf_op jit(solution)/shard_map/ppermute | solution.py:435
  8.1 10.6 %collective-permute-start.2 = (bf16[64,2048]{1,0:T(8,128)(2,1)S(1)}, bf16[64,2048]{1,0:T(8,128)(2,1)S(1)}, u32[]{:S(2)}, u32[]{:S(2)}) collective-permute-start(bf16[64,2048]{1,0:T(8,128)(2,1)S(1)} %join.1), channel_id=1, source_target_pairs={{0,24},{4,28},{8,16},{12,20},{16,8},{20,12},{24,0},{28,4},{1,25},{... | collective-permute-start | bytes 786440 | tf_op jit(solution)/shard_map/ppermute | solution.py:426
  10.6 11.6 %collective-permute-start.1 = (bf16[64,2048]{1,0:T(8,128)(2,1)S(1)}, bf16[64,2048]{1,0:T(8,128)(2,1)S(1)}, u32[]{:S(2)}, u32[]{:S(2)}) collective-permute-start(bf16[64,2048]{1,0:T(8,128)(2,1)S(1)} %join.1), channel_id=1, source_target_pairs={{0,16},{4,20},{8,24},{12,28},{16,0},{20,4},{24,8},{28,12},{1,17},{... | collective-permute-start | bytes 786440 | tf_op jit(solution)/shard_map/ppermute | solution.py:426
  11.1 11.1 %collective-permute-start = (bf16[64,2048]{1,0:T(8,128)(2,1)S(1)}, bf16[64,2048]{1,0:T(8,128)(2,1)S(1)}, u32[]{:S(2)}, u32[]{:S(2)}) collective-permute-start(bf16[64,2048]{1,0:T(8,128)(2,1)S(1)} %join.1), channel_id=1, source_target_pairs={{0,8},{4,12},{8,0},{12,4},{16,24},{20,28},{24,16},{28,20},{1,9},{5... | collective-permute-start | bytes 786440 | tf_op jit(solution)/shard_map/ppermute | solution.py:426
  22.2 5.1 %collective-permute-start.7 = (bf16[4096,256]{1,0:T(8,128)(2,1)}, bf16[4096,256]{1,0:T(8,128)(2,1)S(1)}, u32[]{:S(2)}, u32[]{:S(2)}) collective-permute-start(bf16[4096,256]{1,0:T(8,128)(2,1)} %bitcast.35), channel_id=1, source_target_pairs={{0,4},{4,0},{8,12},{12,8},{16,20},{20,16},{24,28},{28,24},{1,5},{5... | collective-permute-start | bytes 6291464 | tf_op jit(solution)/shard_map/ppermute | solution.py:426
  22.2 7.4 %collective-permute-start.8 = (bf16[4096,256]{1,0:T(8,128)(2,1)}, bf16[4096,256]{1,0:T(8,128)(2,1)S(1)}, u32[]{:S(2)}, u32[]{:S(2)}) collective-permute-start(bf16[4096,256]{1,0:T(8,128)(2,1)} %bitcast.40), channel_id=1, source_target_pairs={{0,4},{4,0},{8,12},{12,8},{16,20},{20,16},{24,28},{28,24},{1,5},{5... | collective-permute-start | bytes 6291464 | tf_op jit(solution)/shard_map/ppermute | solution.py:426
  24.3 15.7 %collective-permute-start.10 = (bf16[64,2048]{1,0:T(8,128)(2,1)S(1)}, bf16[64,2048]{1,0:T(8,128)(2,1)S(1)}, u32[]{:S(2)}, u32[]{:S(2)}) collective-permute-start(bf16[64,2048]{1,0:T(8,128)(2,1)S(1)} %join.1), channel_id=1, source_target_pairs={{0,3},{1,2},{2,1},{3,0},{4,7},{5,6},{6,5},{7,4},{8,11},{9,10},{10,... | collective-permute-start | bytes 786440 | tf_op jit(solution)/shard_map/ppermute | solution.py:435
  24.6 15.4 %collective-permute-start.6 = (bf16[64,4224]{1,0:T(8,128)(2,1)S(1)}, bf16[64,4224]{1,0:T(8,128)(2,1)S(1)}, u32[]{:S(2)}, u32[]{:S(2)}) collective-permute-start(bf16[64,4224]{1,0:T(8,128)(2,1)S(1)} %pad_maximum_fusion.3), channel_id=1, source_target_pairs={{0,16},{4,20},{8,24},{12,28},{16,0},{20,4},{24,8},{28,12},{1,17},{... | collective-permute-start | bytes 1622024 | tf_op jit(solution)/shard_map/ppermute | solution.py:426
  26.1 15.2 %collective-permute-start.5 = (bf16[64,4224]{1,0:T(8,128)(2,1)S(1)}, bf16[64,4224]{1,0:T(8,128)(2,1)S(1)}, u32[]{:S(2)}, u32[]{:S(2)}) collective-permute-start(bf16[64,4224]{1,0:T(8,128)(2,1)S(1)} %pad_maximum_fusion.3), channel_id=1, source_target_pairs={{0,8},{4,12},{8,0},{12,4},{16,24},{20,28},{24,16},{28,20},{1,9},{5... | collective-permute-start | bytes 1622024 | tf_op jit(solution)/shard_map/ppermute | solution.py:426
  27.3 1.3 %copy-start.5 = (bf16[4096,256]{1,0:T(8,128)(2,1)}, bf16[4096,256]{1,0:T(8,128)(2,1)S(1)}, u32[]{:S(2)}) copy-start(bf16[4096,256]{1,0:T(8,128)(2,1)S(1)} %collective-permute-done.7.refs_3_.refs_5_.refs_2_) | copy-start | bytes 6291460
  29.6 1.3 %copy-start.8 = (bf16[4096,256]{1,0:T(8,128)(2,1)}, bf16[4096,256]{1,0:T(8,128)(2,1)S(1)}, u32[]{:S(2)}) copy-start(bf16[4096,256]{1,0:T(8,128)(2,1)S(1)} %collective-permute-done.8.refs_4_.refs_6_.refs_3_) | copy-start | bytes 6291460
  30.9 20.5 %collective-permute-start.9 = (bf16[64,4224]{1,0:T(8,128)(2,1)S(1)}, bf16[64,4224]{1,0:T(8,128)(2,1)S(1)}, u32[]{:S(2)}, u32[]{:S(2)}) collective-permute-start(bf16[64,4224]{1,0:T(8,128)(2,1)S(1)} %pad_maximum_fusion.3), channel_id=1, source_target_pairs={{0,24},{4,28},{8,16},{12,20},{16,8},{20,12},{24,0},{28,4},{1,25},{... | collective-permute-start | bytes 1622024 | tf_op jit(solution)/shard_map/ppermute | solution.py:426
  39.9 17.5 %copy-start.12 = (bf16[4,64,2048]{2,1,0:T(8,128)(2,1)}, bf16[4,64,2048]{2,1,0:T(8,128)(2,1)S(1)}, u32[]{:S(2)}) copy-start(bf16[4,64,2048]{2,1,0:T(8,128)(2,1)S(1)} %pad_maximum_fusion.1) | copy-start | bytes 3145732
  51.4 4.5 %collective-permute-start.14 = (bf16[256,4096]{1,0:T(8,128)(2,1)}, bf16[256,4096]{1,0:T(8,128)(2,1)}, u32[]{:S(2)}, u32[]{:S(2)}) collective-permute-start(bf16[256,4096]{1,0:T(8,128)(2,1)} %bitcast.10.refs_2_.refs_4_), channel_id=1, source_target_pairs={{0,4},{4,0},{8,12},{12,8},{16,20},{20,16},{24,28},{28,24},{1,5},{5... | collective-permute-start | bytes 6291464 | tf_op jit(solution)/shard_map/ppermute | solution.py:426
  51.7 17.5 %copy-start = (bf16[4,64,4224]{2,1,0:T(8,128)(2,1)}, bf16[4,64,4224]{2,1,0:T(8,128)(2,1)S(1)}, u32[]{:S(2)}) copy-start(bf16[4,64,4224]{2,1,0:T(8,128)(2,1)S(1)} %pad_maximum_fusion) | copy-start | bytes 6488068
  51.7 17.3 %collective-permute-start.16 = (bf16[256,4224]{1,0:T(8,128)(2,1)S(1)}, bf16[256,4224]{1,0:T(8,128)(2,1)}, u32[]{:S(2)}, u32[]{:S(2)}) collective-permute-start(bf16[256,4224]{1,0:T(8,128)(2,1)S(1)} %bitcast.30), channel_id=1, source_target_pairs={{0,4},{4,0},{8,12},{12,8},{16,20},{20,16},{24,28},{28,24},{1,5},{5... | collective-permute-start | bytes 6488072 | tf_op jit(solution)/shard_map/ppermute | solution.py:426
  52.3 16.7 %collective-permute-start.15 = (bf16[256,2048]{1,0:T(8,128)(2,1)S(1)}, bf16[256,2048]{1,0:T(8,128)(2,1)}, u32[]{:S(2)}, u32[]{:S(2)}) collective-permute-start(bf16[256,2048]{1,0:T(8,128)(2,1)S(1)} %bitcast.50), channel_id=1, source_target_pairs={{0,4},{4,0},{8,12},{12,8},{16,20},{20,16},{24,28},{28,24},{1,5},{5... | collective-permute-start | bytes 3145736 | tf_op jit(solution)/shard_map/ppermute | solution.py:426
  52.4 16.6 %collective-permute-start.13 = (bf16[64,2048]{1,0:T(8,128)(2,1)S(1)}, bf16[64,2048]{1,0:T(8,128)(2,1)S(1)}, u32[]{:S(2)}, u32[]{:S(2)}) collective-permute-start(bf16[64,2048]{1,0:T(8,128)(2,1)S(1)} %collective-permute-done.10), channel_id=1, source_target_pairs={{0,24},{4,28},{8,16},{12,20},{16,8},{20,12},{24,0},{28,4},{1,25},{... | collective-permute-start | bytes 786440 | tf_op jit(solution)/shard_map/ppermute | solution.py:426
  54.5 14.5 %collective-permute-start.12 = (bf16[64,2048]{1,0:T(8,128)(2,1)S(1)}, bf16[64,2048]{1,0:T(8,128)(2,1)S(1)}, u32[]{:S(2)}, u32[]{:S(2)}) collective-permute-start(bf16[64,2048]{1,0:T(8,128)(2,1)S(1)} %collective-permute-done.10), channel_id=1, source_target_pairs={{0,16},{4,20},{8,24},{12,28},{16,0},{20,4},{24,8},{28,12},{1,17},{... | collective-permute-start | bytes 786440 | tf_op jit(solution)/shard_map/ppermute | solution.py:426
  55.9 13.1 %collective-permute-start.11 = (bf16[64,2048]{1,0:T(8,128)(2,1)S(1)}, bf16[64,2048]{1,0:T(8,128)(2,1)S(1)}, u32[]{:S(2)}, u32[]{:S(2)}) collective-permute-start(bf16[64,2048]{1,0:T(8,128)(2,1)S(1)} %collective-permute-done.10), channel_id=1, source_target_pairs={{0,8},{4,12},{8,0},{12,4},{16,24},{20,28},{24,16},{28,20},{1,9},{5... | collective-permute-start | bytes 786440 | tf_op jit(solution)/shard_map/ppermute | solution.py:426
  57.5 1.6 %copy-start.1 = (bf16[1,4096,256]{2,1,0:T(8,128)(2,1)S(1)}, bf16[1,4096,256]{2,1,0:T(8,128)(2,1)}, u32[]{:S(2)}) copy-start(bf16[1,4096,256]{2,1,0:T(8,128)(2,1)} %param.13) | copy-start | bytes 6291460
  59.1 1.6 %copy-start.3 = (bf16[1,4096,256]{2,1,0:T(8,128)(2,1)S(1)}, bf16[1,4096,256]{2,1,0:T(8,128)(2,1)}, u32[]{:S(2)}) copy-start(bf16[1,4096,256]{2,1,0:T(8,128)(2,1)} %param.14) | copy-start | bytes 6291460
  60.7 1.6 %copy-start.6 = (bf16[4096,256]{1,0:T(8,128)(2,1)S(1)}, bf16[4096,256]{1,0:T(8,128)(2,1)}, u32[]{:S(2)}) copy-start(bf16[4096,256]{1,0:T(8,128)(2,1)} %copy-done.5) | copy-start | bytes 6291460
  62.2 1.6 %copy-start.9 = (bf16[4096,256]{1,0:T(8,128)(2,1)S(1)}, bf16[4096,256]{1,0:T(8,128)(2,1)}, u32[]{:S(2)}) copy-start(bf16[4096,256]{1,0:T(8,128)(2,1)} %copy-done.8) | copy-start | bytes 6291460
  63.8 16.1 %copy-start.16 = (s32[2]{0:T(128)}, s32[2]{0:T(128)S(1)}, u32[]{:S(2)}) copy-start(s32[2]{0:T(128)S(1)} %pad_add_fusion.place) | copy-start | bytes 28
  63.8 5.4 %copy-start.10 = (bf16[4096,256]{1,0:T(8,128)(2,1)S(1)}, bf16[4096,256]{1,0:T(8,128)(2,1)}, u32[]{:S(2)}) copy-start(bf16[4096,256]{1,0:T(8,128)(2,1)} %copy-done.8) | copy-start | bytes 6291460
  68.9 2.0 %copy-start.7 = (bf16[4096,256]{1,0:T(8,128)(2,1)S(1)}, bf16[4096,256]{1,0:T(8,128)(2,1)}, u32[]{:S(2)}) copy-start(bf16[4096,256]{1,0:T(8,128)(2,1)} %copy-done.5) | copy-start | bytes 6291460
  69.2 4.9 %copy-start.11 = (bf16[4,64,2048]{2,1,0:T(8,128)(2,1)}, bf16[4,64,2048]{2,1,0:T(8,128)(2,1)S(1)}, u32[]{:S(2)}) copy-start(bf16[4,64,2048]{2,1,0:T(8,128)(2,1)S(1)} %pad_maximum_fusion.2) | copy-start | bytes 3145732
  69.2 5.0 %copy-start.2 = (bf16[1,4096,256]{2,1,0:T(8,128)(2,1)S(1)}, bf16[1,4096,256]{2,1,0:T(8,128)(2,1)}, u32[]{:S(2)}) copy-start(bf16[1,4096,256]{2,1,0:T(8,128)(2,1)} %param.13) | copy-start | bytes 6291460
  69.2 5.0 %copy-start.4 = (bf16[1,4096,256]{2,1,0:T(8,128)(2,1)S(1)}, bf16[1,4096,256]{2,1,0:T(8,128)(2,1)}, u32[]{:S(2)}) copy-start(bf16[1,4096,256]{2,1,0:T(8,128)(2,1)} %param.14) | copy-start | bytes 6291460
  69.2 4.9 %collective-permute-start.17 = (bf16[256,2048]{1,0:T(8,128)(2,1)S(1)}, bf16[256,2048]{1,0:T(8,128)(2,1)S(1)}, u32[]{:S(2)}, u32[]{:S(2)}) collective-permute-start(bf16[256,2048]{1,0:T(8,128)(2,1)S(1)} %bitcast.45), channel_id=1, source_target_pairs={{0,4},{4,0},{8,12},{12,8},{16,20},{20,16},{24,28},{28,24},{1,5},{5... | collective-permute-start | bytes 3145736 | tf_op jit(solution)/shard_map/ppermute | solution.py:426
  74.0 5.9 %copy-start.13 = (bf16[256,768]{1,0:T(8,128)(2,1)}, bf16[256,768]{1,0:T(8,128)(2,1)S(1)}, u32[]{:S(2)}) copy-start(bf16[256,768]{1,0:T(8,128)(2,1)S(1)} %get-tuple-element.84.mine.acts) | copy-start | bytes 1179652
  74.0 2.9 %collective-permute-start.18 = (bf16[256,768]{1,0:T(8,128)(2,1)S(1)}, bf16[256,768]{1,0:T(8,128)(2,1)S(1)}, u32[]{:S(2)}, u32[]{:S(2)}) collective-permute-start(bf16[256,768]{1,0:T(8,128)(2,1)S(1)} %get-tuple-element.82.other), channel_id=1, source_target_pairs={{0,4},{4,0},{8,12},{12,8},{16,20},{20,16},{24,28},{28,24},{1,5},{5... | collective-permute-start | bytes 1179656 | tf_op jit(solution)/shard_map/ppermute | solution.py:426
  74.1 2.2 %copy-start.17 = (bf16[256,2048]{1,0:T(8,128)(2,1)}, bf16[256,2048]{1,0:T(8,128)(2,1)S(1)}, u32[]{:S(2)}) copy-start(bf16[256,2048]{1,0:T(8,128)(2,1)S(1)} %collective-permute-done.17.refs_5_) | copy-start | bytes 3145732
  76.4 9.5 %collective-permute-start.19 = (bf16[64,2176]{1,0:T(8,128)(2,1)S(1)}, bf16[64,2176]{1,0:T(8,128)(2,1)S(1)}, u32[]{:S(2)}, u32[]{:S(2)}) collective-permute-start(bf16[64,2176]{1,0:T(8,128)(2,1)S(1)} %get-tuple-element.93), channel_id=1, source_target_pairs={{0,8},{4,12},{8,0},{12,4},{16,24},{20,28},{24,16},{28,20},{1,9},{5... | collective-permute-start | bytes 835592 | tf_op jit(solution)/shard_map/ppermute | solution.py:426
  77.0 1.4 %copy-start.18 = (bf16[256,768]{1,0:T(8,128)(2,1)}, bf16[256,768]{1,0:T(8,128)(2,1)S(1)}, u32[]{:S(2)}) copy-start(bf16[256,768]{1,0:T(8,128)(2,1)S(1)} %collective-permute-done.18.got) | copy-start | bytes 1179652
  77.0 17.7 %collective-permute-start.20 = (bf16[64,2176]{1,0:T(8,128)(2,1)S(1)}, bf16[64,2176]{1,0:T(8,128)(2,1)S(1)}, u32[]{:S(2)}, u32[]{:S(2)}) collective-permute-start(bf16[64,2176]{1,0:T(8,128)(2,1)S(1)} %get-tuple-element.94), channel_id=1, source_target_pairs={{0,16},{4,20},{8,24},{12,28},{16,0},{20,4},{24,8},{28,12},{1,17},{... | collective-permute-start | bytes 835592 | tf_op jit(solution)/shard_map/ppermute | solution.py:426
  78.4 8.9 %copy-start.19 = (s32[64,4]{0,1:T(4,128)S(1)}, s32[64,4]{0,1:T(4,128)}, u32[]{:S(2)}) copy-start(s32[64,4]{0,1:T(4,128)} %param.11) | copy-start | bytes 3076
  78.4 16.3 %collective-permute-start.21 = (bf16[64,2176]{1,0:T(8,128)(2,1)S(1)}, bf16[64,2176]{1,0:T(8,128)(2,1)S(1)}, u32[]{:S(2)}, u32[]{:S(2)}) collective-permute-start(bf16[64,2176]{1,0:T(8,128)(2,1)S(1)} %get-tuple-element.95), channel_id=1, source_target_pairs={{0,24},{4,28},{8,16},{12,20},{16,8},{20,12},{24,0},{28,4},{1,25},{... | collective-permute-start | bytes 835592 | tf_op jit(solution)/shard_map/ppermute | solution.py:426
  83.0 15.5 %collective-permute-start.22 = (bf16[64,2048]{1,0:T(8,128)(2,1)}, bf16[64,2048]{1,0:T(8,128)(2,1)S(1)}, u32[]{:S(2)}, u32[]{:S(2)}) collective-permute-start(bf16[64,2048]{1,0:T(8,128)(2,1)} %get-tuple-element.99), channel_id=1, source_target_pairs={{0,8},{4,12},{8,0},{12,4},{16,24},{20,28},{24,16},{28,20},{1,9},{5... | collective-permute-start | bytes 786440 | tf_op jit(solution)/shard_map/ppermute | solution.py:426
  83.7 14.8 %collective-permute-start.23 = (bf16[64,2048]{1,0:T(8,128)(2,1)}, bf16[64,2048]{1,0:T(8,128)(2,1)S(1)}, u32[]{:S(2)}, u32[]{:S(2)}) collective-permute-start(bf16[64,2048]{1,0:T(8,128)(2,1)} %get-tuple-element.100), channel_id=1, source_target_pairs={{0,16},{4,20},{8,24},{12,28},{16,0},{20,4},{24,8},{28,12},{1,17},{... | collective-permute-start | bytes 786440 | tf_op jit(solution)/shard_map/ppermute | solution.py:426
  85.9 17.4 %collective-permute-start.24 = (bf16[64,2048]{1,0:T(8,128)(2,1)}, bf16[64,2048]{1,0:T(8,128)(2,1)S(1)}, u32[]{:S(2)}, u32[]{:S(2)}) collective-permute-start(bf16[64,2048]{1,0:T(8,128)(2,1)} %get-tuple-element.101), channel_id=1, source_target_pairs={{0,24},{4,28},{8,16},{12,20},{16,8},{20,12},{24,0},{28,4},{1,25},{... | collective-permute-start | bytes 786440 | tf_op jit(solution)/shard_map/ppermute | solution.py:426
  94.9 16.7 %collective-permute-start.25 = (bf16[64,1152]{1,0:T(8,128)(2,1)S(1)}, bf16[64,1152]{1,0:T(8,128)(2,1)S(1)}, u32[]{:S(2)}, u32[]{:S(2)}) collective-permute-start(bf16[64,1152]{1,0:T(8,128)(2,1)S(1)} %get-tuple-element.96), channel_id=1, source_target_pairs={{0,3},{1,2},{2,1},{3,0},{4,7},{5,6},{6,5},{7,4},{8,11},{9,10},{10,... | collective-permute-start | bytes 442376 | tf_op jit(solution)/shard_map/ppermute | solution.py:435
  98.5 13.1 %collective-permute-start.26 = (bf16[64,1152]{1,0:T(8,128)(2,1)S(1)}, bf16[64,1152]{1,0:T(8,128)(2,1)S(1)}, u32[]{:S(2)}, u32[]{:S(2)}) collective-permute-start(bf16[64,1152]{1,0:T(8,128)(2,1)S(1)} %get-tuple-element.97), channel_id=1, source_target_pairs={{0,2},{1,3},{2,0},{3,1},{4,6},{5,7},{6,4},{7,5},{8,10},{9,11},{10,... | collective-permute-start | bytes 442376 | tf_op jit(solution)/shard_map/ppermute | solution.py:435
  103.4 8.2 %collective-permute-start.27 = (bf16[64,1152]{1,0:T(8,128)(2,1)S(1)}, bf16[64,1152]{1,0:T(8,128)(2,1)S(1)}, u32[]{:S(2)}, u32[]{:S(2)}) collective-permute-start(bf16[64,1152]{1,0:T(8,128)(2,1)S(1)} %get-tuple-element.104), channel_id=1, source_target_pairs={{0,1},{1,0},{2,3},{3,2},{4,5},{5,4},{6,7},{7,6},{8,9},{9,8},{10,11... | collective-permute-start | bytes 442376 | tf_op jit(solution)/shard_map/ppermute | solution.py:435
